TPU v7x, 32 devices: a whole 2x2x4 slice. The times are simulated.
32 devices in a mesh: row: 8 (over y, x, core), col: 4 (over z).
Axes of the slice: x: 2, y: 2, z: 4, core: 2. Of those that a mesh axis runs over, the one named last changes fastest.
Arguments:
- factor_rows: bfloat16 [2, 1024, 16384], P(None, None, ('row', 'col')), may hold values from -0.09375 to 0.09375
- solved: bfloat16 [64, 16384], P(None, ('row', 'col')), may hold values from -6 to 6
- inverses: bfloat16 [2, 1024, 1024], P(None, 'row', 'col'), as said below
- link_tile: bfloat16 [1024, 1024], P('col', 'row'), may hold values from -0.1875 to 0.1875
- right_side: float32 [2, 1024, 64], P(None, 'col'), may hold values from -6 to 6
Outputs:
- back_solved: float32 [2, 1024, 64], P(None, 'col')
- remaining: float32 [64, 16384], P(None, ('row', 'col'))
Inputs may be any that keep to these rules, and one draw needn't show every extreme that they name: `inverses`: each of the two blocks is lower triangular with a positive diagonal.
All inputs are finite; a program needn't handle non-finite values.
Results may differ from a plain program's by a relative error of at most 0.015.
Values may be sent and summed in bfloat16 or wider, within the bound.
No kernel may reach another device: no remote copies, remote signals or barrier semaphores. Data moves between devices by JAX's collectives and lax.ppermute only.
A program may use at most 64 MiB of HBM per device.

v0:
```python
import jax
import jax.numpy as jnp
from jax import lax
from jax.sharding import PartitionSpec as P


def shards(factor_rows, solved, inverses, link_tile, right_side):
    partial_value = jnp.einsum(
        "kic,nc->kin", factor_rows, solved, preferred_element_type=jnp.float32
    )
    column_part = lax.psum_scatter(partial_value, "col", scatter_dimension=1, tiled=True)
    panel_sum = lax.psum(column_part.astype(jnp.bfloat16), "row").astype(jnp.float32)

    def forward_solve(which, residue):
        rows_part = jnp.dot(inverses[which], residue, preferred_element_type=jnp.float32)
        solved_rows = lax.psum(rows_part, "col").astype(jnp.bfloat16)
        return (solved_rows, solved_rows)

    residue_first = (right_side[0] - panel_sum[0]).astype(jnp.bfloat16)
    first_all, first_rows = forward_solve(0, residue_first)
    link_part = jnp.dot(link_tile, first_rows, preferred_element_type=jnp.float32)
    link_sum = lax.psum(link_part, "row")
    residue_last = (right_side[1] - panel_sum[1] - link_sum).astype(jnp.bfloat16)
    last_all, last_rows = forward_solve(1, residue_last)

    def transpose_solve(which, vector_rows):
        product = jnp.einsum(
            "ij,in->jn", inverses[which], vector_rows, preferred_element_type=jnp.float32
        )
        return lax.psum(product, "row")

    last_out = transpose_solve(1, last_rows)
    last_short = last_out.astype(jnp.bfloat16)
    back_part = jnp.einsum("ji,jn->in", link_tile, last_short, preferred_element_type=jnp.float32)
    back_sum = lax.psum(back_part, "col")
    carry_rows = (first_rows.astype(jnp.float32) - back_sum).astype(jnp.bfloat16)
    first_out = transpose_solve(0, carry_rows)
    first_short = first_out.astype(jnp.bfloat16)
    both_whole = lax.all_gather(jnp.stack([first_short, last_short]), "col", axis=1, tiled=True)
    update = jnp.einsum("kiw,kin->nw", factor_rows, both_whole, preferred_element_type=jnp.float32)
    remaining = solved.astype(jnp.float32) - update
    back_solved = jnp.stack([first_out, last_out])
    return (back_solved, remaining)


def solution(mesh):
    placed = (
        P(None, None, ("row", "col")),
        P(None, ("row", "col")),
        P(None, "row", "col"),
        P("col", "row"),
        P(None, "col", None),
    )
    return jax.shard_map(
        shards,
        mesh=mesh,
        in_specs=placed,
        out_specs=(P(None, "col", None), P(None, ("row", "col"))),
        check_vma=False,
    )
```

profile of v0, /device:TPU:0, one launch (start us, length us, event | category | flops | bytes accessed | tf_op | source)
XLA Modules:
  0.0 323.3 jit_solution(2729693944165837772)
XLA Ops:
  7.2 0.0 reduce-scatter.2.cloned.1.call-start
  7.3 1.5 copy-done
  8.8 2.4 fusion.9
  11.1 0.0 reduce-scatter.2.cloned.1.call-update
  11.2 0.0 all-reduce.5.cloned.1.call-start
  11.2 24.5 %reduce-scatter.2.cloned.1.call-done = f32[2,256,64]{1,2,0:T(8,128)} async-done(((f32[2,1024,64]{1,2,0:T(8,128)}), f32[2,256,64]{1,2,0:T(8,128)}) %reduce-scatter.2.cloned.1.call-update) | async-done | bytes 131088 | tf_op jit(solution)/shard_map/reduce_scatter | solution.py:11
  35.7 1.5 convert_element_type.36
  37.2 0.0 all-reduce.5.cloned.1.call-update
  37.3 0.0 all-reduce.7.cloned.1.call-start
  37.3 52.6 %all-reduce.5.cloned.1.call-done = bf16[2,256,64]{1,2,0:T(8,128)(2,1)} async-done(((bf16[2,256,64]{1,2,0:T(8,128)(2,1)}), bf16[2,256,64]{1,2,0:T(8,128)(2,1)}) %all-reduce.5.cloned.1.call-update) | async-done | bytes 65552 | tf_op jit(solution)/shard_map/psum | solution.py:12
  89.9 0.8 convert_element_type.37
  90.8 0.1 convolution_bitcast_fusion.6
  90.9 19.0 %psum.50 = bf16[128,64]{0,1:T(8,128)(2,1)S(1)} all-reduce(f32[128,64]{0,1:T(8,128)S(1)} %convolution_bitcast_fusion.6), channel_id=1, replica_groups=mesh['row'=8,'col'=4] {'col'}, use_global_device_ids=true, to_apply=%region_2.0 | all-reduce | flops 8192 | bytes 49152 | tf_op jit(solution)/shard_map/psum | solution.py:16
  109.9 0.8 convolution_bitcast_fusion.3
  110.7 0.0 all-reduce.7.cloned.1.call-update
  110.7 0.0 all-reduce.9.cloned.1.call-start
  110.8 49.2 %all-reduce.7.cloned.1.call-done = f32[256,64]{0,1:T(8,128)} async-done(((f32[256,64]{0,1:T(8,128)}), f32[256,64]{0,1:T(8,128)}) %all-reduce.7.cloned.1.call-update) | async-done | bytes 65552 | tf_op jit(solution)/shard_map/psum | solution.py:22
  160.0 1.0 convolution_bitcast_fusion.5
  161.0 19.0 %psum.52 = bf16[128,64]{0,1:T(8,128)(2,1)S(1)} all-reduce(f32[128,64]{0,1:T(8,128)S(1)} %convolution_bitcast_fusion.5), channel_id=1, replica_groups=mesh['row'=8,'col'=4] {'col'}, use_global_device_ids=true, to_apply=%region_4.0 | all-reduce | flops 8192 | bytes 49152 | tf_op jit(solution)/shard_map/psum | solution.py:16
  180.0 0.8 convolution_bitcast_fusion.2
  180.8 0.0 all-reduce.9.cloned.1.call-update
  180.8 0.0 all-reduce.11.cloned.1.call-start
  180.8 49.2 %all-reduce.9.cloned.1.call-done = f32[256,64]{0,1:T(8,128)} async-done(((f32[256,64]{0,1:T(8,128)}), f32[256,64]{0,1:T(8,128)}) %all-reduce.9.cloned.1.call-update) | async-done | bytes 65552 | tf_op jit(solution)/shard_map/psum | solution.py:30
  230.1 1.0 convolution_bitcast_fusion.4
  231.1 19.0 %psum.54 = f32[128,64]{0,1:T(8,128)S(1)} all-reduce(f32[128,64]{0,1:T(8,128)S(1)} %convolution_bitcast_fusion.4), channel_id=1, replica_groups=mesh['row'=8,'col'=4] {'col'}, use_global_device_ids=true, to_apply=%region_6.0 | all-reduce | flops 8192 | bytes 65536 | tf_op jit(solution)/shard_map/psum | solution.py:35
  250.1 0.8 convolution_bitcast_fusion.1
  250.9 0.8 convert_bitcast_fusion.1
  251.7 48.4 %all-reduce.11.cloned.1.call-done = f32[256,64]{0,1:T(8,128)} async-done(((f32[256,64]{0,1:T(8,128)}), f32[256,64]{0,1:T(8,128)}) %all-reduce.11.cloned.1.call-update) | async-done | bytes 65552 | tf_op jit(solution)/shard_map/psum | solution.py:30
  300.1 0.9 convert_bitcast_fusion
  301.1 13.9 %all_gather.3 = bf16[2,1024,64]{1,2,0:T(8,128)(2,1)S(1)} all-gather(bf16[2,256,64]{1,2,0:T(8,128)(2,1)S(1)} %pad_maximum_fusion.1), channel_id=1, replica_groups=mesh['row'=8,'col'=4] {'col'}, dimensions={1}, use_global_device_ids=true | all-gather | bytes 327680 | tf_op jit(solution)/shard_map/all_gather | solution.py:39
  315.0 1.1 fusion
  316.1 0.7 pad_maximum_fusion
  (15 shorter events, 0.1 us)
Async XLA Ops:
  7.2 1.6 copy-start
  7.2 83.6 %copy-start.2 = (bf16[2,128,256]{2,1,0:T(8,128)(2,1)S(1)}, bf16[2,128,256]{2,1,0:T(8,128)(2,1)}, u32[]{:S(2)}) copy-start(bf16[2,128,256]{2,1,0:T(8,128)(2,1)} %param.7) | copy-start | bytes 393220
  7.2 83.6 %copy-start.6 = (f32[2,256,64]{1,2,0:T(8,128)S(1)}, f32[2,256,64]{1,2,0:T(8,128)}, u32[]{:S(2)}) copy-start(f32[2,256,64]{1,2,0:T(8,128)} %param.9) | copy-start | bytes 393220
  7.2 102.7 %copy-start.3 = (bf16[256,128]{1,0:T(8,128)(2,1)S(1)}, bf16[256,128]{1,0:T(8,128)(2,1)}, u32[]{:S(2)}) copy-start(bf16[256,128]{1,0:T(8,128)(2,1)} %param.8) | copy-start | bytes 196612
  7.2 28.5 %reduce-scatter.2.cloned.1.call-start = ((), (), s32[]{:S(2)}) async-start(), calls=%async_computation.1 | async-start | bytes 655360 | tf_op jit(solution)/shard_map/reduce_scatter | solution.py:11
  11.1 303.9 %copy-start.5 = (bf16[64,512]{1,0:T(8,128)(2,1)S(1)}, bf16[64,512]{1,0:T(8,128)(2,1)}, u32[]{:S(2)}) copy-start(bf16[64,512]{1,0:T(8,128)(2,1)} %param.6) | copy-start | bytes 196612
  11.2 78.7 %all-reduce.5.cloned.1.call-start = ((), (), s32[]{:S(2)}) async-start(), calls=%async_computation.2 | async-start | bytes 131072 | tf_op jit(solution)/shard_map/psum | solution.py:12
  37.3 122.8 %all-reduce.7.cloned.1.call-start = ((), (), s32[]{:S(2)}) async-start(), calls=%async_computation.3 | async-start | bytes 131072 | tf_op jit(solution)/shard_map/psum | solution.py:22
  110.7 119.3 %all-reduce.9.cloned.1.call-start = ((), (), s32[]{:S(2)}) async-start(), calls=%async_computation.4 | async-start | bytes 131072 | tf_op jit(solution)/shard_map/psum | solution.py:30
  180.8 119.3 %all-reduce.11.cloned.1.call-start = ((), (), s32[]{:S(2)}) async-start(), calls=%async_computation.5 | async-start | bytes 131072 | tf_op jit(solution)/shard_map/psum | solution.py:30
  230.1 86.1 %copy-start.1 = (f32[256,64]{0,1:T(8,128)S(1)}, f32[256,64]{0,1:T(8,128)}, u32[]{:S(2)}) copy-start(f32[256,64]{0,1:T(8,128)} %all-reduce.9.cloned.1.call-done) | copy-start | bytes 196612
  300.1 16.0 %copy-start.4 = (f32[256,64]{0,1:T(8,128)S(1)}, f32[256,64]{0,1:T(8,128)}, u32[]{:S(2)}) copy-start(f32[256,64]{0,1:T(8,128)} %all-reduce.11.cloned.1.call-done) | copy-start | bytes 196612
Sparse Core Ops, SparseCore 0:
  11.3 24.3 reduce-scatter.1
  39.3 50.5 all-reduce.4
  110.9 49.1 all-reduce.6
  180.9 49.1 all-reduce.8
  251.0 49.0 all-reduce.10
where the time goes:
time: 324 us; the launch traced here: 323 us
  waiting for transfers between devices  224 us (69%)
  blocking collectives  70.9 us (22%)
  between operations  13.8 us (4%)
  matrix products  7.98 us (2%)
  other arithmetic  4.83 us (1%)
    psum x2, waiting for transfers between devices, transpose_solve(): return lax.psum(product, 'row')  97.6 us
    psum x1, waiting for transfers between devices, shards(): lax.psum(column_part.astype(jnp.bfloat16), 'row').astype(jnp.float32)  52.6 us
    psum x1, waiting for transfers between devices, shards(): link_sum = lax.psum(link_part, 'row')  49.2 us
    psum x2, blocking collectives, forward_solve(): solved_rows = lax.psum(rows_part, 'col').astype(jnp.bfloat16)  38 us
    reduce_scatter x1, waiting for transfers between devices, shards(): lax.psum_scatter(partial_value, 'col', scatter_dimension=1, tiled=True)  24.5 us
    psum x1, blocking collectives, shards(): back_sum = lax.psum(back_part, 'col')  19 us
    all_gather x1, blocking collectives, shards(): lax.all_gather(jnp.stack([first_short, last_short]), 'col', axis=1, tiled...  13.9 us
  transfers between devices with their start and end apart: 5, of which 5 were waited for; matrix products, arithmetic and copies ran while one was open for 0% of the time, Pallas kernels for 0%

commit v1 on v0

v1 whole, which is shorter than its diff:
```python
import jax
import jax.numpy as jnp
from jax import lax
from jax.sharding import PartitionSpec as P

BF = jnp.bfloat16
F32 = jnp.float32


def dot(left, right, contract):
    return lax.dot_general(left, right, ((contract[0], contract[1]), ((), ())), preferred_element_type=F32)


def build(R, C):
    def exchange(value, axes):
        return lax.all_to_all(value, axes, 0, 0, tiled=False)

    def xor_row(value, step):
        return lax.ppermute(value, "row", [(i, i ^ step) for i in range(R)])

    def sum_over_col(part):
        sent = jnp.broadcast_to(part.astype(BF)[None], (C,) + part.shape)
        return jnp.sum(exchange(sent, "col").astype(F32), axis=0)

    def shards(factor_rows, solved, inverses, link_tile, right_side):
        nrhs = solved.shape[0]
        group = nrhs // R
        rows = right_side.shape[1]
        order = rows * C
        own = jnp.concatenate([inverses, link_tile.T[None]], axis=0)
        near = [own] + [xor_row(own, step) for step in range(2, R, 2)]
        near = jnp.stack(near, axis=1)
        mate = xor_row(near, 1)
        weights = jnp.concatenate([near, mate], axis=1).reshape(3, order, rows)
        first_tile, last_tile, link_back = weights[0], weights[1], weights[2]

        part = jnp.einsum("nc,kic->nki", solved, factor_rows, preferred_element_type=F32).astype(BF)
        part = part.reshape(R, group, 2, C, rows).transpose(0, 3, 2, 1, 4).reshape(R * C, 2 * group, rows)
        panel = jnp.sum(exchange(part, ("row", "col")).astype(F32), axis=0).reshape(2, group, rows)
        mine = lax.dynamic_slice_in_dim(right_side, lax.axis_index("row") * group, group, 2)
        residue = mine.transpose(0, 2, 1) - panel

        first_solved = sum_over_col(dot(residue[0].astype(BF), first_tile, ((1,), (1,)))).astype(BF)
        link_term = dot(first_solved, link_back, ((1,), (0,)))
        residue_last = (residue[1] - link_term).astype(BF)
        last_solved = sum_over_col(dot(residue_last, last_tile, ((1,), (1,)))).astype(BF)
        last_short = dot(last_solved, last_tile, ((1,), (0,))).astype(BF)
        back_term = sum_over_col(dot(last_short, link_back, ((1,), (1,))))
        carry = (first_solved.astype(F32) - back_term).astype(BF)
        first_short = dot(carry, first_tile, ((1,), (0,))).astype(BF)

        both = jnp.concatenate([first_short, last_short], axis=0)
        sent = jnp.broadcast_to(both[None], (R * C,) + both.shape)
        whole = exchange(sent, ("row", "col")).reshape(R, C, 2, group, rows)
        whole = whole.transpose(2, 0, 3, 1, 4).reshape(2, nrhs, order)
        update = jnp.einsum("kni,kic->nc", whole, factor_rows, preferred_element_type=F32)
        remaining = solved.astype(F32) - update
        here = lax.dynamic_slice_in_dim(whole, lax.axis_index("col") * rows, rows, 2)
        return (here.astype(F32).transpose(0, 2, 1), remaining)

    return shards


def solution(mesh):
    placed = (
        P(None, None, ("row", "col")),
        P(None, ("row", "col")),
        P(None, "row", "col"),
        P("col", "row"),
        P(None, "col", None),
    )
    return jax.shard_map(
        build(mesh.shape["row"], mesh.shape["col"]),
        mesh=mesh,
        in_specs=placed,
        out_specs=(P(None, "col", None), P(None, ("row", "col"))),
        check_vma=False,
    )
```

time: 324 us -> 75.5 us (0.23)
  waiting for transfers between devices: 224 us -> 16.4 us
  blocking collectives: 70.9 us -> 24.8 us
  starting transfers between devices: 0.21 us -> 13.7 us
  between operations: 13.8 us -> 0.74 us
  local copies, waits for them, and re-layouts: 1.54 us -> 9.01 us
    psum x4 -> x0, waiting for transfers between devices: 199 us -> none  [the longest x2 97.6 us: transpose_solve(): return lax.psum(product, 'row')]
    psum x3 -> x0, blocking collectives: 57 us -> none  [the longest x2 38 us: forward_solve(): solved_rows = lax.psum(rows_part, 'col').astype(jnp.bfloat16)]
    all_to_all x0 -> x3, blocking collectives: none -> 24.8 us  [exchange(): return lax.all_to_all(value, axes, 0, 0, tiled=False)]
    reduce_scatter x1 -> x0, waiting for transfers between devices: 24.5 us -> none  [shards(): lax.psum_scatter(partial_value, 'col', scatter_dimension=1, tiled=True)]
    all_to_all x0 -> x2, waiting for transfers between devices: none -> 16.4 us  [exchange(): return lax.all_to_all(value, axes, 0, 0, tiled=False)]
    all_gather x1 -> x0, blocking collectives: 13.9 us -> none  [shards(): lax.all_gather(jnp.stack([first_short, last_short]), 'col', axis=1, tiled...]
    all_to_all x0 -> x2, starting transfers between devices: none -> 8.89 us  [exchange(): return lax.all_to_all(value, axes, 0, 0, tiled=False)]
    ppermute x0 -> x4, starting transfers between devices: none -> 4.8 us  [xor_row(): return lax.ppermute(value, 'row', [(i, i ^ step) for i in range(R)])]
  transfers between devices with their start and end apart: 5 -> 6, of which waited for: 5 -> 2; matrix products, arithmetic and copies ran while one was open for 0% -> 9% of each run, Pallas kernels for 0% -> 0%
where the time goes in v1:
time: 75.5 us; the launch traced here: 74.9 us
  blocking collectives  24.8 us (33%)
  waiting for transfers between devices  16.4 us (22%)
  starting transfers between devices  13.7 us (18%)
  local copies, waits for them, and re-layouts  9.01 us (12%)
  matrix products  6.13 us (8%)
  other arithmetic  4.09 us (5%)
    all_to_all x3, blocking collectives, exchange(): return lax.all_to_all(value, axes, 0, 0, tiled=False)  24.8 us
    all_to_all x2, waiting for transfers between devices, exchange(): return lax.all_to_all(value, axes, 0, 0, tiled=False)  16.4 us
    all_to_all x2, starting transfers between devices, exchange(): return lax.all_to_all(value, axes, 0, 0, tiled=False)  8.89 us
    ppermute x4, starting transfers between devices, xor_row(): return lax.ppermute(value, 'row', [(i, i ^ step) for i in range(R)])  4.8 us
    dot_general x5, matrix products, dot(): lax.dot_general(left, right, ((contract[0], contract[1]), ((), ())), pref...  3.4 us
    slice x1, local copies, waits for them, and re-layouts, shards(): first_tile, last_tile, link_back = (weights[0], weights[1], weights[2])  2.28 us
    unnamed x9, local copies, waits for them, and re-layouts  2.08 us
    concatenate x1, local copies, waits for them, and re-layouts, shards(): weights = jnp.concatenate([near, mate], axis=1).reshape(3, order, rows)  2.08 us
  transfers between devices with their start and end apart: 6, of which 2 were waited for; matrix products, arithmetic and copies ran while one was open for 9% of the time, Pallas kernels for 0%

profile of v1, /device:TPU:0, one launch (start us, length us, event | category | flops | bytes accessed | tf_op | source)
XLA Modules:
  0.0 74.9 jit_solution(7794603830105430248)
XLA Ops:
  0.6 0.0 copy-start
  0.6 1.1 %copy.12 = bf16[1,128,256]{2,1,0:T(8,128)(2,1)S(1)} copy(bf16[1,128,256]{1,2,0:T(8,128)(2,1)} %bitcast.69) | data formatting | bytes 131072 | tf_op jit(solution)/shard_map/broadcast_in_dim | solution.py:30
  1.7 0.9 %fusion.5 = (bf16[3,1,128,256]{3,2,0,1:T(8,128)(2,1)S(1)}, bf16[3,128,256]{2,1,0:T(8,128)(2,1)S(1)}) fusion(bf16[1,128,256]{2,1,0:T(8,128)(2,1)S(1)} %copy.12, bf16[2,128,256]{2,1,0:T(8,128)(2,1)} %param.7), kind=kLoop, calls=%fused_computation.27 | loop fusion | flops 98304 | bytes 589824 | tf_op jit(solution)/shard_map/stack | solution.py:32
  2.7 3.0 %collective-permute-start = (bf16[3,128,256]{2,1,0:T(8,128)(2,1)S(1)}, bf16[3,128,256]{2,1,0:T(8,128)(2,1)S(1)}, u32[]{:S(2)}, u32[]{:S(2)}) collective-permute-start(bf16[3,128,256]{2,1,0:T(8,128)(2,1)S(1)} %get-tuple-element.6), channel_id=1, source_target_pairs={{0,8},{4,12},{8,0},{12,4},{16,24},{20,28},{24,16},{28,20},{1,9},{5... | collective-permute-start | bytes 589832 | tf_op jit(solution)/shard_map/ppermute | solution.py:19
  5.7 1.5 %collective-permute-start.1 = (bf16[3,128,256]{2,1,0:T(8,128)(2,1)S(1)}, bf16[3,128,256]{2,1,0:T(8,128)(2,1)S(1)}, u32[]{:S(2)}, u32[]{:S(2)}) collective-permute-start(bf16[3,128,256]{2,1,0:T(8,128)(2,1)S(1)} %get-tuple-element.6), channel_id=1, source_target_pairs={{0,16},{4,20},{8,24},{12,28},{16,0},{20,4},{24,8},{28,12},{1,17},{... | collective-permute-start | bytes 589832 | tf_op jit(solution)/shard_map/ppermute | solution.py:19
  7.2 0.0 collective-permute-start.2
  7.2 1.6 %convolution_convert_fusion = bf16[64,2,1024]{2,0,1:T(8,128)(2,1)S(1)} fusion(bf16[2,1024,512]{2,1,0:T(8,128)(2,1)S(1)} %copy-done, bf16[64,512]{1,0:T(8,128)(2,1)} %param.6), kind=kOutput, calls=%fused_computation | convolution fusion | flops 134348800 | bytes 2424832 | tf_op jit(solution)/shard_map/nc,kic->nki/dot_general | solution.py:37
  8.8 0.7 copy.11
  9.5 6.3 %all-to-all-start = ((bf16[32,16,256]{2,1,0:T(8,128)(2,1)}), bf16[32,16,256]{2,1,0:T(8,128)(2,1)S(1)}, u32[]{:S(2)}, u32[]{:S(2)}) async-start(bf16[32,16,256]{2,1,0:T(8,128)(2,1)} %bitcast.4), calls=%async_computation | async-start | bytes 524288 | tf_op jit(solution)/shard_map/all_to_all | solution.py:16
  15.9 0.7 constant_dynamic-update-slice_fusion.4
  16.6 1.0 %pad_maximum_fusion = bf16[3,4,128,256]{3,2,0,1:T(8,128)(2,1)} fusion(bf16[3,1,128,256]{3,2,0,1:T(8,128)(2,1)S(1)} %bitcast.68, bf16[3,1,128,256]{3,2,0,1:T(8,128)(2,1)S(1)} %bitcast.67, bf16[3,1,128,256]{3,2,0,1:T(8,128)(2,1)S(1)} %bitcast.66, bf16[3,1,128,256]{3,2,0,1:T(8,128)(2,1)S(1)} %get-tuple-element.5), kind=kLoop, calls=%fused_computation.10 | loop fusion | flops 1179648 | bytes 1572864 | tf_op jit(solution)/shard_map/stack | solution.py:32
  17.6 0.3 collective-permute-start.3
  17.8 0.7 constant_dynamic-update-slice_fusion.3
  18.5 0.7 constant_dynamic-update-slice_fusion.2
  19.2 0.7 constant_dynamic-update-slice_fusion.1
  19.9 6.2 %all-to-all-done = bf16[32,16,256]{2,1,0:T(8,128)(2,1)S(1)} async-done(((bf16[32,16,256]{2,1,0:T(8,128)(2,1)}), bf16[32,16,256]{2,1,0:T(8,128)(2,1)S(1)}, u32[]{:S(2)}, u32[]{:S(2)}) %all-to-all-start) | async-done | bytes 262176 | tf_op jit(solution)/shard_map/all_to_all | solution.py:16
  26.1 0.7 bitcast_subtract_fusion
  26.8 2.1 %constant_dynamic-update-slice_fusion = bf16[3,8,128,256]{3,2,0,1:T(8,128)(2,1)} fusion(bf16[3,8,128,256]{3,2,0,1:T(8,128)(2,1)} %constant_dynamic-update-slice_fusion.1, bf16[3,4,128,256]{3,2,0,1:T(8,128)(2,1)} %collective-permute-done.3), kind=kLoop, calls=%fused_computation.18 | loop fusion | bytes 1572864 | tf_op jit(solution)/shard_map/concatenate | solution.py:34
  28.9 2.3 %fusion.6 = (bf16[1,8,128,256]{3,2,0,1:T(8,128)(2,1)S(1)}, bf16[1,8,128,256]{3,2,0,1:T(8,128)(2,1)}, bf16[1,8,128,256]{3,2,0,1:T(8,128)(2,1)S(1)}) fusion(bf16[3,8,128,256]{3,2,0,1:T(8,128)(2,1)} %constant_dynamic-update-slice_fusion), kind=kLoop, calls=%fused_computation.28 | loop fusion | bytes 3145728 | tf_op jit(solution)/shard_map/slice | solution.py:35
  31.2 0.2 convolution_convert_fusion.3
  31.4 8.6 %all_to_all.25 = bf16[4,8,1024]{2,1,0:T(8,128)(2,1)S(1)} all-to-all(bf16[4,8,1024]{2,1,0:T(8,128)(2,1)S(1)} %broadcast_in_dim.11), channel_id=1, replica_groups=mesh['row'=8,'col'=4] {'col'}, dimensions={0} | all-to-all | bytes 131072 | tf_op jit(solution)/shard_map/all_to_all | solution.py:16
  40.0 1.5 %convolution_convert_fusion.2 = bf16[8,1024]{1,0:T(8,128)(2,1)S(1)} fusion(bf16[1024,256]{1,0:T(8,128)(2,1)} %bitcast.60, bf16[8,1024]{1,0:T(8,128)(2,1)S(1)} %reduce_sum.43, bf16[1024,256]{1,0:T(8,128)(2,1)S(1)} %bitcast.58, f32[2,8,256]{2,1,0:T(8,128)S(1)} %bitcast_subtract_fusion), kind=kOutput, calls=%fused_computation.4 | convolution fusion | flops 8400896 | bytes 1089536 | tf_op jit(solution)/shard_map/dot_general | solution.py:11
  41.6 8.1 %all_to_all.26 = bf16[4,8,1024]{2,1,0:T(8,128)(2,1)S(1)} all-to-all(bf16[4,8,1024]{2,1,0:T(8,128)(2,1)S(1)} %broadcast_in_dim.12), channel_id=1, replica_groups=mesh['row'=8,'col'=4] {'col'}, dimensions={0} | all-to-all | bytes 131072 | tf_op jit(solution)/shard_map/all_to_all | solution.py:16
  49.7 1.2 %convolution_convert_fusion.5 = bf16[8,256]{1,0:T(8,128)(2,1)S(1)} fusion(bf16[8,1024]{1,0:T(8,128)(2,1)S(1)} %reduce_sum.44, bf16[1024,256]{1,0:T(8,128)(2,1)} %bitcast.61), kind=kOutput, calls=%fused_computation.9 | convolution fusion | flops 4196352 | bytes 544768 | tf_op jit(solution)/shard_map/dot_general | solution.py:11
  51.0 0.2 convolution_convert_fusion.1
  51.2 8.1 %all_to_all.27 = bf16[4,8,1024]{2,1,0:T(8,128)(2,1)S(1)} all-to-all(bf16[4,8,1024]{2,1,0:T(8,128)(2,1)S(1)} %broadcast_in_dim.13), channel_id=1, replica_groups=mesh['row'=8,'col'=4] {'col'}, dimensions={0} | all-to-all | bytes 131072 | tf_op jit(solution)/shard_map/all_to_all | solution.py:16
  59.4 0.2 convolution_convert_fusion.4
  59.5 0.7 broadcast_in_dim.14
  60.3 2.6 %all-to-all-start.4 = ((bf16[32,16,256]{2,1,0:T(8,128)(2,1)}), bf16[32,16,256]{2,1,0:T(8,128)(2,1)S(1)}, u32[]{:S(2)}, u32[]{:S(2)}) async-start(bf16[32,16,256]{2,1,0:T(8,128)(2,1)} %broadcast_in_dim.14), calls=%async_computation.4 | async-start | bytes 524288 | tf_op jit(solution)/shard_map/all_to_all | solution.py:16
  62.9 10.2 %all-to-all-done.4 = bf16[32,16,256]{2,1,0:T(8,128)(2,1)S(1)} async-done(((bf16[32,16,256]{2,1,0:T(8,128)(2,1)}), bf16[32,16,256]{2,1,0:T(8,128)(2,1)S(1)}, u32[]{:S(2)}, u32[]{:S(2)}) %all-to-all-start.4) | async-done | bytes 262176 | tf_op jit(solution)/shard_map/all_to_all | solution.py:16
  73.1 1.1 %fusion = f32[64,512]{1,0:T(8,128)} fusion(bf16[2,64,1024]{2,1,0:T(8,128)(2,1)S(1)} %bitcast.62, bf16[2,1024,512]{2,1,0:T(8,128)(2,1)S(1)} %copy-done, bf16[64,512]{1,0:T(8,128)(2,1)S(1)} %copy-done.2), kind=kOutput, calls=%fused_computation.2 | convolution fusion | flops 134283264 | bytes 2555904 | tf_op jit(solution)/shard_map/kni,kic->nc/dot_general | solution.py:56
  74.2 0.7 convert_bitcast_fusion
  (18 shorter events, 0.2 us)
Async XLA Ops:
  0.6 6.6 %copy-start = (bf16[2,1024,512]{2,1,0:T(8,128)(2,1)S(1)}, bf16[2,1024,512]{2,1,0:T(8,128)(2,1)}, u32[]{:S(2)}) copy-start(bf16[2,1024,512]{2,1,0:T(8,128)(2,1)} %param.5) | copy-start | bytes 6291460
  2.7 13.2 %copy-start.1 = (bf16[2,128,256]{2,1,0:T(8,128)(2,1)S(1)}, bf16[2,128,256]{2,1,0:T(8,128)(2,1)}, u32[]{:S(2)}) copy-start(bf16[2,128,256]{2,1,0:T(8,128)(2,1)} %param.7) | copy-start | bytes 393220
  2.7 13.9 %collective-permute-start = (bf16[3,128,256]{2,1,0:T(8,128)(2,1)S(1)}, bf16[3,128,256]{2,1,0:T(8,128)(2,1)S(1)}, u32[]{:S(2)}, u32[]{:S(2)}) collective-permute-start(bf16[3,128,256]{2,1,0:T(8,128)(2,1)S(1)} %get-tuple-element.6), channel_id=1, source_target_pairs={{0,8},{4,12},{8,0},{12,4},{16,24},{20,28},{24,16},{28,20},{1,9},{5... | collective-permute-start | bytes 589832 | tf_op jit(solution)/shard_map/ppermute | solution.py:19
  5.7 10.9 %collective-permute-start.1 = (bf16[3,128,256]{2,1,0:T(8,128)(2,1)S(1)}, bf16[3,128,256]{2,1,0:T(8,128)(2,1)S(1)}, u32[]{:S(2)}, u32[]{:S(2)}) collective-permute-start(bf16[3,128,256]{2,1,0:T(8,128)(2,1)S(1)} %get-tuple-element.6), channel_id=1, source_target_pairs={{0,16},{4,20},{8,24},{12,28},{16,0},{20,4},{24,8},{28,12},{1,17},{... | collective-permute-start | bytes 589832 | tf_op jit(solution)/shard_map/ppermute | solution.py:19
  7.2 9.4 %collective-permute-start.2 = (bf16[3,128,256]{2,1,0:T(8,128)(2,1)S(1)}, bf16[3,128,256]{2,1,0:T(8,128)(2,1)S(1)}, u32[]{:S(2)}, u32[]{:S(2)}) collective-permute-start(bf16[3,128,256]{2,1,0:T(8,128)(2,1)S(1)} %get-tuple-element.6), channel_id=1, source_target_pairs={{0,24},{4,28},{8,16},{12,20},{16,8},{20,12},{24,0},{28,4},{1,25},{... | collective-permute-start | bytes 589832 | tf_op jit(solution)/shard_map/ppermute | solution.py:19
  9.5 16.5 %all-to-all-start = ((bf16[32,16,256]{2,1,0:T(8,128)(2,1)}), bf16[32,16,256]{2,1,0:T(8,128)(2,1)S(1)}, u32[]{:S(2)}, u32[]{:S(2)}) async-start(bf16[32,16,256]{2,1,0:T(8,128)(2,1)} %bitcast.4), calls=%async_computation | async-start | bytes 524288 | tf_op jit(solution)/shard_map/all_to_all | solution.py:16
  17.6 9.3 %collective-permute-start.3 = (bf16[3,4,128,256]{3,2,0,1:T(8,128)(2,1)}, bf16[3,4,128,256]{3,2,0,1:T(8,128)(2,1)}, u32[]{:S(2)}, u32[]{:S(2)}) collective-permute-start(bf16[3,4,128,256]{3,2,0,1:T(8,128)(2,1)} %pad_maximum_fusion), channel_id=1, source_target_pairs={{0,4},{4,0},{8,12},{12,8},{16,20},{20,16},{24,28},{28,24},{1,5},{5... | collective-permute-start | bytes 2359304 | tf_op jit(solution)/shard_map/ppermute | solution.py:19
  49.7 23.4 %copy-start.2 = (bf16[64,512]{1,0:T(8,128)(2,1)S(1)}, bf16[64,512]{1,0:T(8,128)(2,1)}, u32[]{:S(2)}) copy-start(bf16[64,512]{1,0:T(8,128)(2,1)} %param.6) | copy-start | bytes 196612
  60.3 12.8 %all-to-all-start.4 = ((bf16[32,16,256]{2,1,0:T(8,128)(2,1)}), bf16[32,16,256]{2,1,0:T(8,128)(2,1)S(1)}, u32[]{:S(2)}, u32[]{:S(2)}) async-start(bf16[32,16,256]{2,1,0:T(8,128)(2,1)} %broadcast_in_dim.14), calls=%async_computation.4 | async-start | bytes 524288 | tf_op jit(solution)/shard_map/all_to_all | solution.py:16

commit v2 on v1

v2 whole, which is shorter than its diff:
```python
import functools

import jax
import jax.numpy as jnp
from jax import lax
from jax.experimental import pallas as pl
from jax.experimental.pallas import tpu as pltpu
from jax.sharding import PartitionSpec as P

BF = jnp.bfloat16
F32 = jnp.float32
PARAMS = pltpu.CompilerParams(vmem_limit_bytes=40 * 2**20)


def dot(left, right, contract):
    return lax.dot_general(left, right, ((contract[0], contract[1]), ((), ())), preferred_element_type=F32)


def plain(left, right):
    return dot(left, right, ((1,), (0,)))


def flipped(left, right):
    return dot(left, right, ((1,), (1,)))


def exchange(value, axes):
    return lax.all_to_all(value, axes, 0, 0, tiled=False)


def generic(R, C):
    def xor_row(value, step):
        return lax.ppermute(value, "row", [(i, i ^ step) for i in range(R)])

    def sum_over_col(part):
        sent = jnp.broadcast_to(part.astype(BF)[None], (C,) + part.shape)
        return jnp.sum(exchange(sent, "col").astype(F32), axis=0)

    def shards(factor_rows, solved, inverses, link_tile, right_side):
        nrhs = solved.shape[0]
        group = nrhs // R
        rows = right_side.shape[1]
        order = rows * C
        own = jnp.concatenate([inverses, link_tile.T[None]], axis=0)
        near = [own] + [xor_row(own, step) for step in range(2, R, 2)]
        near = jnp.stack(near, axis=1)
        mate = xor_row(near, 1)
        weights = jnp.concatenate([near, mate], axis=1).reshape(3, order, rows)
        first_tile, last_tile, link_back = weights[0], weights[1], weights[2]

        part = jnp.einsum("nc,kic->nki", solved, factor_rows, preferred_element_type=F32).astype(BF)
        part = part.reshape(R, group, 2, C, rows).transpose(0, 3, 2, 1, 4).reshape(R * C, 2 * group, rows)
        panel = jnp.sum(exchange(part, ("row", "col")).astype(F32), axis=0).reshape(2, group, rows)
        mine = lax.dynamic_slice_in_dim(right_side, lax.axis_index("row") * group, group, 2)
        residue = mine.transpose(0, 2, 1) - panel

        first_solved = sum_over_col(flipped(residue[0].astype(BF), first_tile)).astype(BF)
        residue_last = (residue[1] - plain(first_solved, link_back)).astype(BF)
        last_solved = sum_over_col(flipped(residue_last, last_tile)).astype(BF)
        last_short = plain(last_solved, last_tile).astype(BF)
        back_term = sum_over_col(flipped(last_short, link_back))
        carry = (first_solved.astype(F32) - back_term).astype(BF)
        first_short = plain(carry, first_tile).astype(BF)

        both = jnp.concatenate([first_short, last_short], axis=0)
        sent = jnp.broadcast_to(both[None], (R * C,) + both.shape)
        return finish(factor_rows, solved, exchange(sent, ("row", "col")), R, C)

    return shards


def finish(factor_rows, solved, arrived, R, C):
    nrhs = solved.shape[0]
    group, rows = nrhs // R, arrived.shape[2]
    whole = arrived.reshape(R, C, 2, group, rows)
    whole = whole.transpose(2, 0, 3, 1, 4).reshape(2, nrhs, rows * C)
    update = jnp.einsum("kni,kic->nc", whole, factor_rows, preferred_element_type=F32)
    remaining = solved.astype(F32) - update
    here = lax.dynamic_slice_in_dim(whole, lax.axis_index("col") * rows, rows, 2)
    return (here.astype(F32).transpose(0, 2, 1), remaining)


def pack_kernel(inv_ref, link_ref, own_ref, far_ref):
    own_ref[0] = inv_ref[0]
    own_ref[1] = inv_ref[1]
    far_ref[0] = inv_ref[1]
    turned = link_ref[...].T
    own_ref[2] = turned
    far_ref[1] = turned


def panel_kernel(solved_ref, factor_ref, part_ref):
    R, _, double, rows = part_ref.shape
    group = double // 2
    value = solved_ref[...]
    upper = flipped(value, factor_ref[0]).reshape(R, group, rows)
    lower = flipped(value, factor_ref[1]).reshape(R, group, rows)
    part_ref[:, 0] = jnp.concatenate([upper, lower], axis=1).astype(BF)


def stack_kernel(*refs):
    for i, ref in enumerate(refs[:-1]):
        refs[-1][i] = ref[...]


def first_kernel(count, near, panel_ref, side_ref, *refs):
    tiles, sent_ref = refs[:near], refs[near]
    group = side_ref.shape[0] // 2
    total = panel_ref[0].astype(F32)
    for i in range(1, panel_ref.shape[0]):
        total += panel_ref[i].astype(F32)
    residue = side_ref[...] - total
    first = residue[:group].astype(BF)
    last = residue[group:]
    outs = [flipped(first, tile[0]) for tile in tiles]
    half = near // 2
    top = jnp.concatenate(outs[:half] + [last[:, : last.shape[1] // 2]], axis=1)
    low = jnp.concatenate(outs[half:] + [last[:, last.shape[1] // 2 :]], axis=1)
    both = jnp.concatenate([top, low], axis=0).astype(BF)
    for i in range(count):
        sent_ref[i] = both


def chain_kernel(near, C, arrived_ref, *refs):
    tiles, others, sent_ref = refs[:near], refs[near : 2 * near], refs[2 * near]
    here = lax.axis_index("col")
    group = arrived_ref.shape[1] // 2
    size = tiles[0].shape[1]
    half = near // 2
    wide = half * size
    total = arrived_ref[0, :, :wide].astype(F32)
    for i in range(1, C):
        total += arrived_ref[i, :, :wide].astype(F32)
    total = total.astype(BF)
    first = [total[(s // half) * group : (s // half + 1) * group, (s % half) * size : (s % half + 1) * size] for s in range(near)]

    def last_tile(s, z):
        return tiles[s][1] if z == 0 else others[s][z - 1, 0]

    def link_back(s, z):
        return tiles[s][2] if z == 0 else others[s][z - 1, 1]

    turn = []
    for z in range(C):
        raw = arrived_ref[here ^ z, :, wide:].astype(F32)
        value = jnp.concatenate([raw[:group], raw[group:]], axis=1)
        for s in range(near):
            value -= plain(first[s], link_back(s, z))
        turn.append(value.astype(BF))
    last = []
    for s in range(near):
        value = flipped(turn[0], last_tile(s, 0))
        for z in range(1, C):
            value += flipped(turn[z], last_tile(s, z))
        last.append(value.astype(BF))
    short = []
    for z in range(C):
        value = plain(last[0], last_tile(0, z))
        for s in range(1, near):
            value += plain(last[s], last_tile(s, z))
        short.append(value.astype(BF))
    first_out = None
    for s in range(near):
        carry = first[s].astype(F32)
        for z in range(C):
            carry -= flipped(short[z], link_back(s, z))
        value = plain(carry.astype(BF), tiles[s][0])
        first_out = value if first_out is None else first_out + value
    both = jnp.concatenate([first_out.astype(BF), short[0]], axis=0)
    for i in range(sent_ref.shape[0]):
        sent_ref[i] = both


def tiled(R, C):
    def xor_row(value, step):
        return lax.ppermute(value, "row", [(i, i ^ step) for i in range(R)])

    def xor_col(value, step):
        return lax.ppermute(value, "col", [(i, i ^ step) for i in range(C)])

    def shards(factor_rows, solved, inverses, link_tile, right_side):
        nrhs, width = solved.shape
        group = nrhs // R
        rows = right_side.shape[1]
        size = inverses.shape[1]
        order = rows * C
        own, far = pl.pallas_call(
            pack_kernel,
            out_shape=(
                jax.ShapeDtypeStruct((3, size, rows), BF),
                jax.ShapeDtypeStruct((2, size, rows), BF),
            ),
            compiler_params=PARAMS,
        )(inverses, link_tile)
        fars = [xor_col(far, step) for step in range(1, C)]
        evens = [own] + [xor_row(own, step) for step in range(2, R, 2)]
        tiles = [block for even in evens for block in (even, xor_row(even, 1))]

        part = pl.pallas_call(
            panel_kernel,
            grid=(C,),
            in_specs=[
                pl.BlockSpec((nrhs, width), lambda c: (0, 0)),
                pl.BlockSpec((2, rows, width), lambda c: (0, c, 0)),
            ],
            out_specs=pl.BlockSpec((R, 1, 2 * group, rows), lambda c: (0, c, 0, 0)),
            out_shape=jax.ShapeDtypeStruct((R, C, 2 * group, rows), BF),
            compiler_params=PARAMS,
        )(solved, factor_rows)
        mine = lax.dynamic_slice_in_dim(right_side, lax.axis_index("row") * group, group, 2)
        mine = mine.transpose(0, 2, 1).reshape(2 * group, rows)
        panel = exchange(part.reshape(R * C, 2 * group, rows), ("row", "col"))

        stack = pl.pallas_call(
            stack_kernel,
            out_shape=jax.ShapeDtypeStruct((C - 1, 2, size, rows), BF),
            compiler_params=PARAMS,
        )(*fars)
        evens = [stack] + [xor_row(stack, step) for step in range(2, R, 2)]
        others = [block for even in evens for block in (even, xor_row(even, 1))]

        wide = (order + rows) // 2
        only_first = pl.BlockSpec((1, size, rows), lambda i: (0, 0, 0))
        sent = pl.pallas_call(
            functools.partial(first_kernel, C, R),
            grid=(1,),
            in_specs=[
                pl.BlockSpec(panel.shape, lambda i: (0, 0, 0)),
                pl.BlockSpec(mine.shape, lambda i: (0, 0)),
            ]
            + [only_first] * R,
            out_specs=pl.BlockSpec((C, 2 * group, wide), lambda i: (0, 0, 0)),
            out_shape=jax.ShapeDtypeStruct((C, 2 * group, wide), BF),
            compiler_params=PARAMS,
        )(panel, mine, *tiles)
        arrived = exchange(sent, "col")
        sent = pl.pallas_call(
            functools.partial(chain_kernel, R, C),
            out_shape=jax.ShapeDtypeStruct((R * C, 2 * group, rows), BF),
            compiler_params=PARAMS,
        )(arrived, *tiles, *others)
        return finish(factor_rows, solved, exchange(sent, ("row", "col")), R, C)

    return shards


def solution(mesh):
    R, C = mesh.shape["row"], mesh.shape["col"]

    def shards(factor_rows, solved, inverses, link_tile, right_side):
        group = solved.shape[0] // R
        aligned = group % 8 == 0 and inverses.shape[1] % 128 == 0 and inverses.shape[2] % 256 == 0
        build = tiled if aligned else generic
        return build(R, C)(factor_rows, solved, inverses, link_tile, right_side)

    placed = (
        P(None, None, ("row", "col")),
        P(None, ("row", "col")),
        P(None, "row", "col"),
        P("col", "row"),
        P(None, "col", None),
    )
    return jax.shard_map(
        shards,
        mesh=mesh,
        in_specs=placed,
        out_specs=(P(None, "col", None), P(None, ("row", "col"))),
        check_vma=False,
    )
```

time: 75.5 us -> 78.3 us (1.037)
  blocking collectives: 24.8 us -> 0 us
  waiting for transfers between devices: 16.4 us -> 35.5 us
  starting transfers between devices: 13.7 us -> 23.4 us
  Pallas kernels: 0 us -> 8.25 us
  matrix products: 6.13 us -> 1.14 us
  other arithmetic: 4.09 us -> 0.66 us
  local copies, waits for them, and re-layouts: 9.01 us -> 7.95 us
    all_to_all x3 -> x0, blocking collectives: 24.8 us -> none  [exchange(): return lax.all_to_all(value, axes, 0, 0, tiled=False)]
    ppermute x4 -> x14, waiting for transfers between devices: 0.01 us -> 10.6 us  [xor_row(): return lax.ppermute(value, 'row', [(i, i ^ step) for i in range(R)])]
    ppermute x0 -> x3, waiting for transfers between devices: none -> 8.97 us  [xor_col(): return lax.ppermute(value, 'col', [(i, i ^ step) for i in range(C)])]
    pallas_call x0 -> x5, Pallas kernels: none -> 8.25 us  [the longest x1 4.98 us: shards(): pl.pallas_call(functools.partial(chain_kernel, R, C), out_shape=jax.Shape...]
    unnamed x9 -> x30, local copies, waits for them, and re-layouts: 2.08 us -> 7.93 us
    ppermute x4 -> x14, starting transfers between devices: 4.8 us -> 10.1 us  [xor_row(): return lax.ppermute(value, 'row', [(i, i ^ step) for i in range(R)])]
    dot_general x7 -> x1, matrix products: 6.13 us -> 1.14 us  [finish(): jnp.einsum('kni,kic->nc', whole, factor_rows, preferred_element_type=F32)]
    ppermute x0 -> x3, starting transfers between devices: none -> 4.39 us  [xor_col(): return lax.ppermute(value, 'col', [(i, i ^ step) for i in range(C)])]
  transfers between devices with their start and end apart: 6 -> 20, of which waited for: 2 -> 8; matrix products, arithmetic and copies ran while one was open for 9% -> 0% of each run, Pallas kernels for 0% -> 4%
where the time goes in v2:
time: 78.3 us; the launch traced here: 77.6 us
  waiting for transfers between devices  35.5 us (45%)
  starting transfers between devices  23.4 us (30%)
  Pallas kernels  8.25 us (11%)
  local copies, waits for them, and re-layouts  7.95 us (10%)
  matrix products  1.14 us (1%)
    all_to_all x3, waiting for transfers between devices, exchange(): return lax.all_to_all(value, axes, 0, 0, tiled=False)  15.9 us
    ppermute x14, waiting for transfers between devices, xor_row(): return lax.ppermute(value, 'row', [(i, i ^ step) for i in range(R)])  10.6 us
    ppermute x14, starting transfers between devices, xor_row(): return lax.ppermute(value, 'row', [(i, i ^ step) for i in range(R)])  10.1 us
    ppermute x3, waiting for transfers between devices, xor_col(): return lax.ppermute(value, 'col', [(i, i ^ step) for i in range(C)])  8.97 us
    all_to_all x3, starting transfers between devices, exchange(): return lax.all_to_all(value, axes, 0, 0, tiled=False)  8.85 us
    unnamed x30, local copies, waits for them, and re-layouts  7.93 us
    pallas_call x1, Pallas kernels, shards(): pl.pallas_call(functools.partial(chain_kernel, R, C), out_shape=jax.Shape...  4.98 us
    ppermute x3, starting transfers between devices, xor_col(): return lax.ppermute(value, 'col', [(i, i ^ step) for i in range(C)])  4.39 us
  transfers between devices with their start and end apart: 20, of which 8 were waited for; matrix products, arithmetic and copies ran while one was open for 0% of the time, Pallas kernels for 4%

profile of v2, /device:TPU:0, one launch (start us, length us, event | category | flops | bytes accessed | tf_op | source)
XLA Modules:
  0.0 77.6 jit_solution(5004604020998180613)
XLA Ops:
  0.7 0.9 %copy-done.13 = bf16[2,128,256]{2,1,0:T(8,128)(2,1)S(1)} copy-done((bf16[2,128,256]{2,1,0:T(8,128)(2,1)S(1)}, bf16[2,128,256]{2,1,0:T(8,128)(2,1)}, u32[]{:S(2)}) %copy-start.13) | copy-done | bytes 131096
  1.6 0.8 %copy-done.14 = bf16[256,128]{1,0:T(8,128)(2,1)S(1)} copy-done((bf16[256,128]{1,0:T(8,128)(2,1)S(1)}, bf16[256,128]{1,0:T(8,128)(2,1)}, u32[]{:S(2)}) %copy-start.14) | copy-done | bytes 65560
  2.5 4.0 %collective-permute-start.5 = (bf16[3,128,256]{2,1,0:T(8,128)(2,1)S(1)}, bf16[3,128,256]{2,1,0:T(8,128)(2,1)S(1)}, u32[]{:S(2)}, u32[]{:S(2)}) collective-permute-start(bf16[3,128,256]{2,1,0:T(8,128)(2,1)S(1)} %get-tuple-element.4.refs_0_), channel_id=1, source_target_pairs={{0,24},{4,28},{8,16},{12,20},{16,8},{20,12},{24,0},{28,4},{1,25},{... | collective-permute-start | bytes 589832 | tf_op jit(solution)/shard_map/ppermute | solution.py:176
  6.5 3.6 %collective-permute-start.9 = (bf16[2,128,256]{2,1,0:T(8,128)(2,1)S(1)}, bf16[2,128,256]{2,1,0:T(8,128)(2,1)S(1)}, u32[]{:S(2)}, u32[]{:S(2)}) collective-permute-start(bf16[2,128,256]{2,1,0:T(8,128)(2,1)S(1)} %get-tuple-element.5), channel_id=1, source_target_pairs={{0,3},{1,2},{2,1},{3,0},{4,7},{5,6},{6,5},{7,4},{8,11},{9,10},{10,... | collective-permute-start | bytes 393224 | tf_op jit(solution)/shard_map/ppermute | solution.py:179
  10.1 0.8 %collective-permute-start.7 = (bf16[2,128,256]{2,1,0:T(8,128)(2,1)S(1)}, bf16[2,128,256]{2,1,0:T(8,128)(2,1)S(1)}, u32[]{:S(2)}, u32[]{:S(2)}) collective-permute-start(bf16[2,128,256]{2,1,0:T(8,128)(2,1)S(1)} %get-tuple-element.5), channel_id=1, source_target_pairs={{0,1},{1,0},{2,3},{3,2},{4,5},{5,4},{6,7},{7,6},{8,9},{9,8},{10,11... | collective-permute-start | bytes 393224 | tf_op jit(solution)/shard_map/ppermute | solution.py:179
  10.8 0.5 collective-permute-start.3
  11.4 3.4 %collective-permute-done.9.refs_2_ = bf16[2,128,256]{2,1,0:T(8,128)(2,1)S(1)} collective-permute-done((bf16[2,128,256]{2,1,0:T(8,128)(2,1)S(1)}, bf16[2,128,256]{2,1,0:T(8,128)(2,1)S(1)}, u32[]{:S(2)}, u32[]{:S(2)}) %collective-permute-start.9) | collective-permute-done | bytes 131104 | tf_op jit(solution)/shard_map/ppermute | solution.py:179
  14.7 0.5 collective-permute-start.1
  15.3 5.6 %collective-permute-done.8.refs_1_ = bf16[2,128,256]{2,1,0:T(8,128)(2,1)S(1)} collective-permute-done((bf16[2,128,256]{2,1,0:T(8,128)(2,1)S(1)}, bf16[2,128,256]{2,1,0:T(8,128)(2,1)S(1)}, u32[]{:S(2)}, u32[]{:S(2)}) %collective-permute-start.8) | collective-permute-done | bytes 131104 | tf_op jit(solution)/shard_map/ppermute | solution.py:179
  20.9 0.5 collective-permute-start.15
  21.4 1.5 %collective-permute-start.13 = (bf16[3,2,128,256]{3,2,1,0:T(8,128)(2,1)S(1)}, bf16[3,2,128,256]{3,2,1,0:T(8,128)(2,1)}, u32[]{:S(2)}, u32[]{:S(2)}) collective-permute-start(bf16[3,2,128,256]{3,2,1,0:T(8,128)(2,1)S(1)} %shard_map.71.refs_8_), channel_id=1, source_target_pairs={{0,16},{4,20},{8,24},{12,28},{16,0},{20,4},{24,8},{28,12},{1,17},{... | collective-permute-start | bytes 1179656 | tf_op jit(solution)/shard_map/ppermute | solution.py:176
  23.0 1.5 %collective-permute-start.11 = (bf16[3,2,128,256]{3,2,1,0:T(8,128)(2,1)S(1)}, bf16[3,2,128,256]{3,2,1,0:T(8,128)(2,1)}, u32[]{:S(2)}, u32[]{:S(2)}) collective-permute-start(bf16[3,2,128,256]{3,2,1,0:T(8,128)(2,1)S(1)} %shard_map.71.refs_8_), channel_id=1, source_target_pairs={{0,8},{4,12},{8,0},{12,4},{16,24},{20,28},{24,16},{28,20},{1,9},{5... | collective-permute-start | bytes 1179656 | tf_op jit(solution)/shard_map/ppermute | solution.py:176
  24.5 1.6 %copy-done.1 = bf16[2,1024,512]{2,1,0:T(8,128)(2,1)S(1)} copy-done((bf16[2,1024,512]{2,1,0:T(8,128)(2,1)S(1)}, bf16[2,1024,512]{2,1,0:T(8,128)(2,1)}, u32[]{:S(2)}) %copy-start.1) | copy-done | bytes 2097176
  26.1 0.8 %copy-done.11 = bf16[64,512]{1,0:T(8,128)(2,1)S(1)} copy-done((bf16[64,512]{1,0:T(8,128)(2,1)S(1)}, bf16[64,512]{1,0:T(8,128)(2,1)}, u32[]{:S(2)}) %copy-start.11) | copy-done | bytes 65560
  26.9 2.3 %shard_map.68 = bf16[8,4,16,256]{3,2,1,0:T(8,128)(2,1)} custom-call(bf16[64,512]{1,0:T(8,128)(2,1)S(1)} %copy-done.11, bf16[2,1024,512]{2,1,0:T(8,128)(2,1)S(1)} %copy-done.1), custom_call_target="tpu_custom_call" | custom-call | tf_op jit(solution)/shard_map/pallas_call | solution.py:199
  29.2 3.0 %all-to-all-start = ((bf16[32,16,256]{2,1,0:T(8,128)(2,1)}), bf16[32,16,256]{2,1,0:T(8,128)(2,1)S(1)}, u32[]{:S(2)}, u32[]{:S(2)}) async-start(bf16[32,16,256]{2,1,0:T(8,128)(2,1)} %bitcast), calls=%async_computation | async-start | bytes 524288 | tf_op jit(solution)/shard_map/all_to_all | solution.py:28
  32.7 0.9 %collective-permute-done.6.refs_7_ = bf16[3,128,256]{2,1,0:T(8,128)(2,1)S(1)} collective-permute-done((bf16[3,128,256]{2,1,0:T(8,128)(2,1)S(1)}, bf16[3,128,256]{2,1,0:T(8,128)(2,1)S(1)}, u32[]{:S(2)}, u32[]{:S(2)}) %collective-permute-start.6) | collective-permute-done | bytes 196640 | tf_op jit(solution)/shard_map/ppermute | solution.py:176
  34.2 7.8 %collective-permute-done.13.refs_12_ = bf16[3,2,128,256]{3,2,1,0:T(8,128)(2,1)} collective-permute-done((bf16[3,2,128,256]{3,2,1,0:T(8,128)(2,1)S(1)}, bf16[3,2,128,256]{3,2,1,0:T(8,128)(2,1)}, u32[]{:S(2)}, u32[]{:S(2)}) %collective-permute-start.13) | collective-permute-done | bytes 393248 | tf_op jit(solution)/shard_map/ppermute | solution.py:176
  42.0 0.5 collective-permute-start.12
  42.6 1.7 %collective-permute-done.2.refs_3_ = bf16[3,128,256]{2,1,0:T(8,128)(2,1)S(1)} collective-permute-done((bf16[3,128,256]{2,1,0:T(8,128)(2,1)S(1)}, bf16[3,128,256]{2,1,0:T(8,128)(2,1)S(1)}, u32[]{:S(2)}, u32[]{:S(2)}) %collective-permute-start.2) | collective-permute-done | bytes 196640 | tf_op jit(solution)/shard_map/ppermute | solution.py:176
  44.3 0.9 %shard_map.70 = bf16[4,16,640]{2,1,0:T(8,128)(2,1)} custom-call(bf16[32,16,256]{2,1,0:T(8,128)(2,1)S(1)} %all-to-all-done.panel_ref, f32[16,256]{1,0:T(8,128)S(1)} %dynamic-slice_bitcast_fusion.side_ref, bf16[3,128,256]{2,1,0:T(8,128)(2,1)S(1)} %get-tuple-element.4.refs_0_, bf16[3,128,256]{2,1,0:T(8,128)(2,1)S(1)} %collective-permute-done.refs_1_, ...), custom_call_target="tpu_custom_call" | custom-call | tf_op jit(solution)/shard_map/pallas_call | solution.py:224
  45.2 3.3 %all-to-all-start.1 = ((bf16[4,16,640]{2,1,0:T(8,128)(2,1)}), bf16[4,16,640]{2,1,0:T(8,128)(2,1)S(1)}, u32[]{:S(2)}, u32[]{:S(2)}) async-start(bf16[4,16,640]{2,1,0:T(8,128)(2,1)} %shard_map.70), calls=%async_computation.1 | async-start | bytes 163840 | tf_op jit(solution)/shard_map/all_to_all | solution.py:28
  48.6 5.7 %all-to-all-done.1.arrived_ref = bf16[4,16,640]{2,1,0:T(8,128)(2,1)S(1)} async-done(((bf16[4,16,640]{2,1,0:T(8,128)(2,1)}), bf16[4,16,640]{2,1,0:T(8,128)(2,1)S(1)}, u32[]{:S(2)}, u32[]{:S(2)}) %all-to-all-start.1) | async-done | bytes 81952 | tf_op jit(solution)/shard_map/all_to_all | solution.py:28
  54.3 0.9 %copy-done.4 = bf16[3,128,256]{2,1,0:T(8,128)(2,1)S(1)} copy-done((bf16[3,128,256]{2,1,0:T(8,128)(2,1)S(1)}, bf16[3,128,256]{2,1,0:T(8,128)(2,1)}, u32[]{:S(2)}) %copy-start.4) | copy-done | bytes 196632
  55.2 0.9 %copy-done.6 = bf16[3,128,256]{2,1,0:T(8,128)(2,1)S(1)} copy-done((bf16[3,128,256]{2,1,0:T(8,128)(2,1)S(1)}, bf16[3,128,256]{2,1,0:T(8,128)(2,1)}, u32[]{:S(2)}) %copy-start.6) | copy-done | bytes 196632
  56.2 0.9 %copy-done.8 = bf16[3,128,256]{2,1,0:T(8,128)(2,1)S(1)} copy-done((bf16[3,128,256]{2,1,0:T(8,128)(2,1)S(1)}, bf16[3,128,256]{2,1,0:T(8,128)(2,1)}, u32[]{:S(2)}) %copy-start.8) | copy-done | bytes 196632
  57.1 0.9 %copy-done.10 = bf16[3,128,256]{2,1,0:T(8,128)(2,1)S(1)} copy-done((bf16[3,128,256]{2,1,0:T(8,128)(2,1)S(1)}, bf16[3,128,256]{2,1,0:T(8,128)(2,1)}, u32[]{:S(2)}) %copy-start.10) | copy-done | bytes 196632
  58.0 5.0 %shard_map.72 = bf16[32,16,256]{2,1,0:T(8,128)(2,1)} custom-call(bf16[4,16,640]{2,1,0:T(8,128)(2,1)S(1)} %all-to-all-done.1.arrived_ref, bf16[3,128,256]{2,1,0:T(8,128)(2,1)S(1)} %get-tuple-element.4.refs_0_, bf16[3,128,256]{2,1,0:T(8,128)(2,1)S(1)} %copy-done.4, bf16[3,128,256]{2,1,0:T(8,128)(2,1)S(1)} %collective-permute-done.1.refs_2_, ...), custom_call_target="tpu_custom_call" | custom-call | tf_op jit(solution)/shard_map/pallas_call | solution.py:237
  63.0 2.6 %all-to-all-start.2 = ((bf16[32,16,256]{2,1,0:T(8,128)(2,1)}), bf16[32,16,256]{2,1,0:T(8,128)(2,1)S(1)}, u32[]{:S(2)}, u32[]{:S(2)}) async-start(bf16[32,16,256]{2,1,0:T(8,128)(2,1)} %shard_map.72), calls=%async_computation.2 | async-start | bytes 524288 | tf_op jit(solution)/shard_map/all_to_all | solution.py:28
  65.6 10.2 %all-to-all-done.2 = bf16[32,16,256]{2,1,0:T(8,128)(2,1)S(1)} async-done(((bf16[32,16,256]{2,1,0:T(8,128)(2,1)}), bf16[32,16,256]{2,1,0:T(8,128)(2,1)S(1)}, u32[]{:S(2)}, u32[]{:S(2)}) %all-to-all-start.2) | async-done | bytes 262176 | tf_op jit(solution)/shard_map/all_to_all | solution.py:28
  75.8 1.1 %fusion = f32[64,512]{1,0:T(8,128)} fusion(bf16[2,64,1024]{2,1,0:T(8,128)(2,1)S(1)} %bitcast.17, bf16[2,1024,512]{2,1,0:T(8,128)(2,1)S(1)} %copy-done.2, bf16[64,512]{1,0:T(8,128)(2,1)S(1)} %copy-done.12), kind=kOutput, calls=%fused_computation.1 | convolution fusion | flops 134283264 | bytes 2555904 | tf_op jit(solution)/shard_map/kni,kic->nc/dot_general | solution.py:77
  77.0 0.7 convert_bitcast_fusion
  (47 shorter events, 1.4 us)
Async XLA Ops:
  0.6 42.0 %copy-start = (f32[2,256,64]{1,2,0:T(8,128)S(1)}, f32[2,256,64]{1,2,0:T(8,128)}, u32[]{:S(2)}) copy-start(f32[2,256,64]{1,2,0:T(8,128)} %param.9) | copy-start | bytes 393220
  0.6 0.9 %copy-start.13 = (bf16[2,128,256]{2,1,0:T(8,128)(2,1)S(1)}, bf16[2,128,256]{2,1,0:T(8,128)(2,1)}, u32[]{:S(2)}) copy-start(bf16[2,128,256]{2,1,0:T(8,128)(2,1)} %inv_ref.1) | copy-start | bytes 393220
  2.5 20.5 %collective-permute-start.5 = (bf16[3,128,256]{2,1,0:T(8,128)(2,1)S(1)}, bf16[3,128,256]{2,1,0:T(8,128)(2,1)S(1)}, u32[]{:S(2)}, u32[]{:S(2)}) collective-permute-start(bf16[3,128,256]{2,1,0:T(8,128)(2,1)S(1)} %get-tuple-element.4.refs_0_), channel_id=1, source_target_pairs={{0,24},{4,28},{8,16},{12,20},{16,8},{20,12},{24,0},{28,4},{1,25},{... | collective-permute-start | bytes 589832 | tf_op jit(solution)/shard_map/ppermute | solution.py:176
  6.5 8.3 %collective-permute-start.9 = (bf16[2,128,256]{2,1,0:T(8,128)(2,1)S(1)}, bf16[2,128,256]{2,1,0:T(8,128)(2,1)S(1)}, u32[]{:S(2)}, u32[]{:S(2)}) collective-permute-start(bf16[2,128,256]{2,1,0:T(8,128)(2,1)S(1)} %get-tuple-element.5), channel_id=1, source_target_pairs={{0,3},{1,2},{2,1},{3,0},{4,7},{5,6},{6,5},{7,4},{8,11},{9,10},{10,... | collective-permute-start | bytes 393224 | tf_op jit(solution)/shard_map/ppermute | solution.py:179
  10.1 10.8 %collective-permute-start.8 = (bf16[2,128,256]{2,1,0:T(8,128)(2,1)S(1)}, bf16[2,128,256]{2,1,0:T(8,128)(2,1)S(1)}, u32[]{:S(2)}, u32[]{:S(2)}) collective-permute-start(bf16[2,128,256]{2,1,0:T(8,128)(2,1)S(1)} %get-tuple-element.5), channel_id=1, source_target_pairs={{0,2},{1,3},{2,0},{3,1},{4,6},{5,7},{6,4},{7,5},{8,10},{9,11},{10,... | collective-permute-start | bytes 393224 | tf_op jit(solution)/shard_map/ppermute | solution.py:179
  10.1 10.8 %collective-permute-start.7 = (bf16[2,128,256]{2,1,0:T(8,128)(2,1)S(1)}, bf16[2,128,256]{2,1,0:T(8,128)(2,1)S(1)}, u32[]{:S(2)}, u32[]{:S(2)}) collective-permute-start(bf16[2,128,256]{2,1,0:T(8,128)(2,1)S(1)} %get-tuple-element.5), channel_id=1, source_target_pairs={{0,1},{1,0},{2,3},{3,2},{4,5},{5,4},{6,7},{7,6},{8,9},{9,8},{10,11... | collective-permute-start | bytes 393224 | tf_op jit(solution)/shard_map/ppermute | solution.py:179
  10.8 13.6 %collective-permute-start.3 = (bf16[3,128,256]{2,1,0:T(8,128)(2,1)S(1)}, bf16[3,128,256]{2,1,0:T(8,128)(2,1)S(1)}, u32[]{:S(2)}, u32[]{:S(2)}) collective-permute-start(bf16[3,128,256]{2,1,0:T(8,128)(2,1)S(1)} %get-tuple-element.4.refs_0_), channel_id=1, source_target_pairs={{0,16},{4,20},{8,24},{12,28},{16,0},{20,4},{24,8},{28,12},{1,17},{... | collective-permute-start | bytes 589832 | tf_op jit(solution)/shard_map/ppermute | solution.py:176
  14.7 17.4 %collective-permute-start.1 = (bf16[3,128,256]{2,1,0:T(8,128)(2,1)S(1)}, bf16[3,128,256]{2,1,0:T(8,128)(2,1)S(1)}, u32[]{:S(2)}, u32[]{:S(2)}) collective-permute-start(bf16[3,128,256]{2,1,0:T(8,128)(2,1)S(1)} %get-tuple-element.4.refs_0_), channel_id=1, source_target_pairs={{0,8},{4,12},{8,0},{12,4},{16,24},{20,28},{24,16},{28,20},{1,9},{5... | collective-permute-start | bytes 589832 | tf_op jit(solution)/shard_map/ppermute | solution.py:176
  20.9 13.1 %collective-permute-start.15 = (bf16[3,2,128,256]{3,2,1,0:T(8,128)(2,1)S(1)}, bf16[3,2,128,256]{3,2,1,0:T(8,128)(2,1)}, u32[]{:S(2)}, u32[]{:S(2)}) collective-permute-start(bf16[3,2,128,256]{3,2,1,0:T(8,128)(2,1)S(1)} %shard_map.71.refs_8_), channel_id=1, source_target_pairs={{0,24},{4,28},{8,16},{12,20},{16,8},{20,12},{24,0},{28,4},{1,25},{... | collective-permute-start | bytes 1179656 | tf_op jit(solution)/shard_map/ppermute | solution.py:176
  21.4 20.6 %collective-permute-start.13 = (bf16[3,2,128,256]{3,2,1,0:T(8,128)(2,1)S(1)}, bf16[3,2,128,256]{3,2,1,0:T(8,128)(2,1)}, u32[]{:S(2)}, u32[]{:S(2)}) collective-permute-start(bf16[3,2,128,256]{3,2,1,0:T(8,128)(2,1)S(1)} %shard_map.71.refs_8_), channel_id=1, source_target_pairs={{0,16},{4,20},{8,24},{12,28},{16,0},{20,4},{24,8},{28,12},{1,17},{... | collective-permute-start | bytes 1179656 | tf_op jit(solution)/shard_map/ppermute | solution.py:176
  23.0 19.1 %collective-permute-start.11 = (bf16[3,2,128,256]{3,2,1,0:T(8,128)(2,1)S(1)}, bf16[3,2,128,256]{3,2,1,0:T(8,128)(2,1)}, u32[]{:S(2)}, u32[]{:S(2)}) collective-permute-start(bf16[3,2,128,256]{3,2,1,0:T(8,128)(2,1)S(1)} %shard_map.71.refs_8_), channel_id=1, source_target_pairs={{0,8},{4,12},{8,0},{12,4},{16,24},{20,28},{24,16},{28,20},{1,9},{5... | collective-permute-start | bytes 1179656 | tf_op jit(solution)/shard_map/ppermute | solution.py:176
  24.5 8.0 %collective-permute-start = (bf16[3,128,256]{2,1,0:T(8,128)(2,1)S(1)}, bf16[3,128,256]{2,1,0:T(8,128)(2,1)S(1)}, u32[]{:S(2)}, u32[]{:S(2)}) collective-permute-start(bf16[3,128,256]{2,1,0:T(8,128)(2,1)S(1)} %get-tuple-element.4.refs_0_), channel_id=1, source_target_pairs={{0,4},{4,0},{8,12},{12,8},{16,20},{20,16},{24,28},{28,24},{1,5},{5... | collective-permute-start | bytes 589832 | tf_op jit(solution)/shard_map/ppermute | solution.py:176
  24.5 1.6 %copy-start.1 = (bf16[2,1024,512]{2,1,0:T(8,128)(2,1)S(1)}, bf16[2,1024,512]{2,1,0:T(8,128)(2,1)}, u32[]{:S(2)}) copy-start(bf16[2,1024,512]{2,1,0:T(8,128)(2,1)} %factor_ref.1) | copy-start | bytes 6291460
  29.2 15.1 %all-to-all-start = ((bf16[32,16,256]{2,1,0:T(8,128)(2,1)}), bf16[32,16,256]{2,1,0:T(8,128)(2,1)S(1)}, u32[]{:S(2)}, u32[]{:S(2)}) async-start(bf16[32,16,256]{2,1,0:T(8,128)(2,1)} %bitcast), calls=%async_computation | async-start | bytes 524288 | tf_op jit(solution)/shard_map/all_to_all | solution.py:28
  32.1 1.5 %collective-permute-start.6 = (bf16[3,128,256]{2,1,0:T(8,128)(2,1)S(1)}, bf16[3,128,256]{2,1,0:T(8,128)(2,1)S(1)}, u32[]{:S(2)}, u32[]{:S(2)}) collective-permute-start(bf16[3,128,256]{2,1,0:T(8,128)(2,1)S(1)} %collective-permute-done.5.refs_6_), channel_id=1, source_target_pairs={{0,4},{4,0},{8,12},{12,8},{16,20},{20,16},{24,28},{28,24},{1,5},{5... | collective-permute-start | bytes 589832 | tf_op jit(solution)/shard_map/ppermute | solution.py:176
  32.5 12.7 %copy-start.3 = (bf16[3,128,256]{2,1,0:T(8,128)(2,1)}, bf16[3,128,256]{2,1,0:T(8,128)(2,1)S(1)}, u32[]{:S(2)}) copy-start(bf16[3,128,256]{2,1,0:T(8,128)(2,1)S(1)} %collective-permute-done.refs_1_) | copy-start | bytes 589828
  32.5 10.1 %collective-permute-start.4 = (bf16[3,128,256]{2,1,0:T(8,128)(2,1)S(1)}, bf16[3,128,256]{2,1,0:T(8,128)(2,1)S(1)}, u32[]{:S(2)}, u32[]{:S(2)}) collective-permute-start(bf16[3,128,256]{2,1,0:T(8,128)(2,1)S(1)} %collective-permute-done.3.refs_4_), channel_id=1, source_target_pairs={{0,4},{4,0},{8,12},{12,8},{16,20},{20,16},{24,28},{28,24},{1,5},{5... | collective-permute-start | bytes 589832 | tf_op jit(solution)/shard_map/ppermute | solution.py:176
  33.6 11.6 %copy-start.5 = (bf16[3,128,256]{2,1,0:T(8,128)(2,1)}, bf16[3,128,256]{2,1,0:T(8,128)(2,1)S(1)}, u32[]{:S(2)}) copy-start(bf16[3,128,256]{2,1,0:T(8,128)(2,1)S(1)} %collective-permute-done.6.refs_7_) | copy-start | bytes 589828
  33.6 14.9 %collective-permute-start.10 = (bf16[3,2,128,256]{3,2,1,0:T(8,128)(2,1)S(1)}, bf16[3,2,128,256]{3,2,1,0:T(8,128)(2,1)}, u32[]{:S(2)}, u32[]{:S(2)}) collective-permute-start(bf16[3,2,128,256]{3,2,1,0:T(8,128)(2,1)S(1)} %shard_map.71.refs_8_), channel_id=1, source_target_pairs={{0,4},{4,0},{8,12},{12,8},{16,20},{20,16},{24,28},{28,24},{1,5},{5... | collective-permute-start | bytes 1179656 | tf_op jit(solution)/shard_map/ppermute | solution.py:176
  34.0 20.3 %collective-permute-start.16 = (bf16[3,2,128,256]{3,2,1,0:T(8,128)(2,1)}, bf16[3,2,128,256]{3,2,1,0:T(8,128)(2,1)}, u32[]{:S(2)}, u32[]{:S(2)}) collective-permute-start(bf16[3,2,128,256]{3,2,1,0:T(8,128)(2,1)} %collective-permute-done.15.refs_14_), channel_id=1, source_target_pairs={{0,4},{4,0},{8,12},{12,8},{16,20},{20,16},{24,28},{28,24},{1,5},{5... | collective-permute-start | bytes 1179656 | tf_op jit(solution)/shard_map/ppermute | solution.py:176
  42.0 12.3 %collective-permute-start.14 = (bf16[3,2,128,256]{3,2,1,0:T(8,128)(2,1)}, bf16[3,2,128,256]{3,2,1,0:T(8,128)(2,1)}, u32[]{:S(2)}, u32[]{:S(2)}) collective-permute-start(bf16[3,2,128,256]{3,2,1,0:T(8,128)(2,1)} %collective-permute-done.13.refs_12_), channel_id=1, source_target_pairs={{0,4},{4,0},{8,12},{12,8},{16,20},{20,16},{24,28},{28,24},{1,5},{5... | collective-permute-start | bytes 1179656 | tf_op jit(solution)/shard_map/ppermute | solution.py:176
  42.0 12.3 %collective-permute-start.12 = (bf16[3,2,128,256]{3,2,1,0:T(8,128)(2,1)}, bf16[3,2,128,256]{3,2,1,0:T(8,128)(2,1)}, u32[]{:S(2)}, u32[]{:S(2)}) collective-permute-start(bf16[3,2,128,256]{3,2,1,0:T(8,128)(2,1)} %collective-permute-done.11.refs_10_), channel_id=1, source_target_pairs={{0,4},{4,0},{8,12},{12,8},{16,20},{20,16},{24,28},{28,24},{1,5},{5... | collective-permute-start | bytes 1179656 | tf_op jit(solution)/shard_map/ppermute | solution.py:176
  42.5 2.7 %copy-start.7 = (bf16[3,128,256]{2,1,0:T(8,128)(2,1)}, bf16[3,128,256]{2,1,0:T(8,128)(2,1)S(1)}, u32[]{:S(2)}) copy-start(bf16[3,128,256]{2,1,0:T(8,128)(2,1)S(1)} %collective-permute-done.4.refs_5_) | copy-start | bytes 589828
  42.5 1.8 %collective-permute-start.2 = (bf16[3,128,256]{2,1,0:T(8,128)(2,1)S(1)}, bf16[3,128,256]{2,1,0:T(8,128)(2,1)S(1)}, u32[]{:S(2)}, u32[]{:S(2)}) collective-permute-start(bf16[3,128,256]{2,1,0:T(8,128)(2,1)S(1)} %collective-permute-done.1.refs_2_), channel_id=1, source_target_pairs={{0,4},{4,0},{8,12},{12,8},{16,20},{20,16},{24,28},{28,24},{1,5},{5... | collective-permute-start | bytes 589832 | tf_op jit(solution)/shard_map/ppermute | solution.py:176
  45.2 30.6 %copy-start.12 = (bf16[64,512]{1,0:T(8,128)(2,1)S(1)}, bf16[64,512]{1,0:T(8,128)(2,1)}, u32[]{:S(2)}) copy-start(bf16[64,512]{1,0:T(8,128)(2,1)} %solved_ref.1) | copy-start | bytes 196612
  45.2 9.1 %all-to-all-start.1 = ((bf16[4,16,640]{2,1,0:T(8,128)(2,1)}), bf16[4,16,640]{2,1,0:T(8,128)(2,1)S(1)}, u32[]{:S(2)}, u32[]{:S(2)}) async-start(bf16[4,16,640]{2,1,0:T(8,128)(2,1)} %shard_map.70), calls=%async_computation.1 | async-start | bytes 163840 | tf_op jit(solution)/shard_map/all_to_all | solution.py:28
  48.5 27.3 %copy-start.2 = (bf16[2,1024,512]{2,1,0:T(8,128)(2,1)S(1)}, bf16[2,1024,512]{2,1,0:T(8,128)(2,1)}, u32[]{:S(2)}) copy-start(bf16[2,1024,512]{2,1,0:T(8,128)(2,1)} %factor_ref.1) | copy-start | bytes 6291460
  54.3 0.9 %copy-start.4 = (bf16[3,128,256]{2,1,0:T(8,128)(2,1)S(1)}, bf16[3,128,256]{2,1,0:T(8,128)(2,1)}, u32[]{:S(2)}) copy-start(bf16[3,128,256]{2,1,0:T(8,128)(2,1)} %copy-done.3) | copy-start | bytes 589828
  55.2 0.9 %copy-start.6 = (bf16[3,128,256]{2,1,0:T(8,128)(2,1)S(1)}, bf16[3,128,256]{2,1,0:T(8,128)(2,1)}, u32[]{:S(2)}) copy-start(bf16[3,128,256]{2,1,0:T(8,128)(2,1)} %copy-done.5) | copy-start | bytes 589828
  56.2 0.9 %copy-start.8 = (bf16[3,128,256]{2,1,0:T(8,128)(2,1)S(1)}, bf16[3,128,256]{2,1,0:T(8,128)(2,1)}, u32[]{:S(2)}) copy-start(bf16[3,128,256]{2,1,0:T(8,128)(2,1)} %copy-done.7) | copy-start | bytes 589828
  57.1 0.9 %copy-start.10 = (bf16[3,128,256]{2,1,0:T(8,128)(2,1)S(1)}, bf16[3,128,256]{2,1,0:T(8,128)(2,1)}, u32[]{:S(2)}) copy-start(bf16[3,128,256]{2,1,0:T(8,128)(2,1)} %copy-done.9) | copy-start | bytes 589828
  63.0 12.8 %all-to-all-start.2 = ((bf16[32,16,256]{2,1,0:T(8,128)(2,1)}), bf16[32,16,256]{2,1,0:T(8,128)(2,1)S(1)}, u32[]{:S(2)}, u32[]{:S(2)}) async-start(bf16[32,16,256]{2,1,0:T(8,128)(2,1)} %shard_map.72), calls=%async_computation.2 | async-start | bytes 524288 | tf_op jit(solution)/shard_map/all_to_all | solution.py:28
  (3 other events, 2.6 us)

commit v3 on v1

v3 whole, which is shorter than its diff:
```python
import functools

import jax
import jax.numpy as jnp
from jax import lax
from jax.experimental import pallas as pl
from jax.experimental.pallas import tpu as pltpu
from jax.sharding import PartitionSpec as P

BF = jnp.bfloat16
F32 = jnp.float32
PARAMS = pltpu.CompilerParams(vmem_limit_bytes=12 * 2**20)
WIDE = pltpu.CompilerParams(vmem_limit_bytes=62 * 2**20)


def dot(left, right, contract):
    return lax.dot_general(left, right, ((contract[0], contract[1]), ((), ())), preferred_element_type=F32)


def plain(left, right):
    return dot(left, right, ((1,), (0,)))


def flipped(left, right):
    return dot(left, right, ((1,), (1,)))


def exchange(value, axes):
    return lax.all_to_all(value, axes, 0, 0, tiled=False)


def generic(R, C):
    def xor_row(value, step):
        return lax.ppermute(value, "row", [(i, i ^ step) for i in range(R)])

    def sum_over_col(part):
        sent = jnp.broadcast_to(part.astype(BF)[None], (C,) + part.shape)
        return jnp.sum(exchange(sent, "col").astype(F32), axis=0)

    def shards(factor_rows, solved, inverses, link_tile, right_side):
        nrhs = solved.shape[0]
        group = nrhs // R
        rows = right_side.shape[1]
        order = rows * C
        own = jnp.concatenate([inverses, link_tile.T[None]], axis=0)
        near = [own] + [xor_row(own, step) for step in range(2, R, 2)]
        near = jnp.stack(near, axis=1)
        mate = xor_row(near, 1)
        weights = jnp.concatenate([near, mate], axis=1).reshape(3, order, rows)
        first_tile, last_tile, link_back = weights[0], weights[1], weights[2]

        part = jnp.einsum("nc,kic->nki", solved, factor_rows, preferred_element_type=F32).astype(BF)
        part = part.reshape(R, group, 2, C, rows).transpose(0, 3, 2, 1, 4).reshape(R * C, 2 * group, rows)
        panel = jnp.sum(exchange(part, ("row", "col")).astype(F32), axis=0).reshape(2, group, rows)
        mine = lax.dynamic_slice_in_dim(right_side, lax.axis_index("row") * group, group, 2)
        residue = mine.transpose(0, 2, 1) - panel

        first_solved = sum_over_col(flipped(residue[0].astype(BF), first_tile)).astype(BF)
        residue_last = (residue[1] - plain(first_solved, link_back)).astype(BF)
        last_solved = sum_over_col(flipped(residue_last, last_tile)).astype(BF)
        last_short = plain(last_solved, last_tile).astype(BF)
        back_term = sum_over_col(flipped(last_short, link_back))
        carry = (first_solved.astype(F32) - back_term).astype(BF)
        first_short = plain(carry, first_tile).astype(BF)

        both = jnp.concatenate([first_short, last_short], axis=0)
        sent = jnp.broadcast_to(both[None], (R * C,) + both.shape)
        whole = exchange(sent, ("row", "col")).reshape(R, C, 2, group, rows)
        whole = whole.transpose(2, 0, 3, 1, 4).reshape(2, nrhs, order)
        return finish(factor_rows, solved, (whole[0], whole[1]), rows)

    return shards


def finish(factor_rows, solved, both, rows):
    update = plain(both[0], factor_rows[0]) + plain(both[1], factor_rows[1])
    remaining = solved.astype(F32) - update
    here = [lax.dynamic_slice_in_dim(one, lax.axis_index("col") * rows, rows, 1) for one in both]
    return (jnp.stack([one.astype(F32).T for one in here]), remaining)


def fold(value):
    half = value.shape[-1] // 2
    return jnp.concatenate([value[..., :half], value[..., half:]], axis=-2)


def unfold(value):
    half = value.shape[-2] // 2
    return jnp.concatenate([value[..., :half, :], value[..., half:, :]], axis=-1)


def pack_kernel(inv_ref, link_ref, first_ref, pair_ref):
    first_ref[0] = inv_ref[0]
    pair_ref[0] = inv_ref[1]
    pair_ref[1] = link_ref[...].T


def stack_kernel(own_ref, far_ref, both_ref):
    both_ref[:2] = own_ref[...]
    both_ref[2:] = far_ref[...]


def order_kernel(value_ref, part_ref):
    R, C, double, rows = part_ref.shape
    for c in range(C):
        halves = [value_ref[k, :, c * rows : (c + 1) * rows].astype(F32).reshape(R, double // 2, rows) for k in range(2)]
        part_ref[:, c] = jnp.concatenate(halves, axis=1).astype(BF)


def closing_kernel(C, solved_ref, factor_ref, whole_ref, remaining_ref, back_ref):
    group, rows = whole_ref.shape[1] // 2, whole_ref.shape[2]
    nrhs = solved_ref.shape[0]
    R = nrhs // group
    here = lax.axis_index("col")

    def columns(k, c):
        return jnp.concatenate([whole_ref[r * C + c, k * group : (k + 1) * group].astype(F32) for r in range(R)], axis=0)

    update = None
    for k in range(2):
        back_ref[k] = columns(k, here)
        for c in range(C):
            term = plain(columns(k, c).astype(BF), factor_ref[k, c * rows : (c + 1) * rows])
            update = term if update is None else update + term
    remaining_ref[...] = solved_ref[...].astype(F32) - update


def across(value, tiles):
    return jnp.concatenate([flipped(value, tile[0]) for tile in tiles], axis=1)


def along(value, tiles):
    size = tiles[0].shape[1]
    total = None
    for s, tile in enumerate(tiles):
        term = plain(value[:, s * size : (s + 1) * size], tile[0])
        total = term if total is None else total + term
    return total


def first_kernel(side_ref, panel_ref, *refs):
    tiles, sent_ref = refs[:-1], refs[-1]
    group = side_ref.shape[0] // 2
    total = panel_ref[0].astype(F32)
    for i in range(1, panel_ref.shape[0]):
        total += panel_ref[i].astype(F32)
    residue = side_ref[...] - total
    solved = across(residue[:group].astype(BF), tiles)
    sent_ref[...] = jnp.concatenate([fold(solved), fold(residue[group:])], axis=1).astype(BF)


def pair_sum(own_ref, other_ref):
    return unfold(own_ref[...].astype(F32) + other_ref[...].astype(F32))


def link_kernel(near, own_ref, other_ref, side_ref, *refs):
    links, last_tiles = refs[: 2 * near], refs[2 * near : 4 * near]
    sent_ref, first_ref = refs[4 * near :]
    first = pair_sum(own_ref, other_ref).astype(BF)
    first_ref[...] = first
    total = None
    for j in range(2):
        residue = unfold(side_ref[j].astype(F32)) - along(first, links[j * near : (j + 1) * near])
        term = across(residue.astype(BF), last_tiles[j * near : (j + 1) * near])
        total = term if total is None else total + term
    sent_ref[...] = fold(total).astype(BF)


def turn_kernel(near, own_ref, other_ref, *refs):
    last_tiles, links = refs[: 2 * near], refs[2 * near : 4 * near]
    sent_ref, short_ref = refs[4 * near :]
    last = pair_sum(own_ref, other_ref).astype(BF)
    total = None
    for j in range(2):
        short = along(last, last_tiles[j * near : (j + 1) * near]).astype(BF)
        if j == 0:
            short_ref[...] = short
        term = across(short, links[j * near : (j + 1) * near])
        total = term if total is None else total + term
    sent_ref[...] = fold(total).astype(BF)


def last_kernel(first_ref, short_ref, own_ref, other_ref, *refs):
    tiles, sent_ref = refs[:-1], refs[-1]
    carry = (first_ref[...].astype(F32) - pair_sum(own_ref, other_ref)).astype(BF)
    both = jnp.concatenate([along(carry, tiles), short_ref[...].astype(F32)], axis=0).astype(BF)
    for i in range(sent_ref.shape[0]):
        sent_ref[i] = both


def whole_spec(shape):
    return pl.BlockSpec(shape, lambda i: (0,) * len(shape))


def call(kernel, operands, tiles, shapes, params=PARAMS):
    def tile_spec(array, which):
        return pl.BlockSpec((1,) + array.shape[1:], lambda i: (which, 0, 0))

    return pl.pallas_call(
        kernel,
        grid=(1,),
        in_specs=[whole_spec(one.shape) for one in operands] + [tile_spec(*tile) for tile in tiles],
        out_specs=[whole_spec(shape) for shape in shapes],
        out_shape=[jax.ShapeDtypeStruct(shape, BF) for shape in shapes],
        compiler_params=params,
    )(*operands, *[tile[0] for tile in tiles])


def tiled(R, C):
    def xor_row(value, step):
        return lax.ppermute(value, "row", [(i, i ^ step) for i in range(R)])

    def xor_col(value, step):
        return lax.ppermute(value, "col", [(i, i ^ step) for i in range(C)])

    def in_plane(value):
        return [value] + [xor_row(value, step) for step in range(2, R, 2)]

    def with_mates(evens):
        return [block for even in evens for block in (even, xor_row(even, 1))]

    def shards(factor_rows, solved, inverses, link_tile, right_side):
        nrhs = solved.shape[0]
        group = nrhs // R
        rows = right_side.shape[1]
        size = inverses.shape[1]
        order = rows * C
        cut = (2 * group, rows)

        first_own, pair = call(pack_kernel, [inverses, link_tile], [], [(1, size, rows), (2, size, rows)], WIDE)
        held = solved
        part = jnp.einsum("nc,kic->nki", held, factor_rows, preferred_element_type=F32).astype(BF)
        part = part.reshape(R, group, 2, C, rows).transpose(0, 3, 2, 1, 4)
        far = xor_col(pair, 1)
        first_in = first_own
        evens = in_plane(first_in)
        part, *_ = lax.optimization_barrier((part, far, *evens))
        panel = exchange(part.reshape((R * C,) + cut), ("row", "col"))
        mine = lax.dynamic_slice_in_dim(right_side, lax.axis_index("row") * group, group, 2)
        mine = mine.transpose(0, 2, 1).reshape(cut)

        first_tiles = [(tile, 0) for tile in with_mates(evens)]
        own_pair = pair
        (both,) = call(stack_kernel, [own_pair, far], [], [(4, size, rows)])
        wide = order // 2
        summed = (2 * group, wide)
        (sent,) = call(first_kernel, [mine, panel], first_tiles, [(2 * group, wide + rows // 2)])
        evens = in_plane(both)
        arrived = xor_col(sent, 1)
        mates = []
        spare = evens[0]
        spare, *_ = lax.optimization_barrier((spare, arrived))
        mates.append(xor_row(spare, 1))
        spare = evens[1]
        spare, *_ = lax.optimization_barrier((spare, arrived))
        mates.append(xor_row(spare, 1))
        spare = evens[2]
        spare, *_ = lax.optimization_barrier((spare, arrived))
        mates.append(xor_row(spare, 1))
        spare = evens[3]
        spare, *_ = lax.optimization_barrier((spare, arrived))
        mates.append(xor_row(spare, 1))
        pairs = [block for one in zip(evens, mates) for block in one]
        last_tiles = [(tile, i) for i in (0, 2) for tile in pairs]
        links = [(tile, i) for i in (1, 3) for tile in pairs]
        side = jnp.stack([sent[:, wide:], arrived[:, wide:]])
        sent = (sent[:, :wide].astype(F32) + arrived[:, :wide].astype(F32)).astype(BF)
        link = functools.partial(link_kernel, R)
        sent, first = call(link, [sent, xor_col(sent, 2), side], links + last_tiles, [summed, (group, order)])
        turn = functools.partial(turn_kernel, R)
        sent, short = call(turn, [sent, xor_col(sent, 2)], last_tiles + links, [summed, (group, rows)])
        (sent,) = call(last_kernel, [first, short, sent, xor_col(sent, 2)], first_tiles, [(R * C,) + cut])
        remaining, back = pl.pallas_call(
            functools.partial(closing_kernel, C),
            out_shape=(
                jax.ShapeDtypeStruct(solved.shape, F32),
                jax.ShapeDtypeStruct((2, nrhs, rows), F32),
            ),
            compiler_params=PARAMS,
        )(solved, factor_rows, exchange(sent, ("row", "col")))
        return (back.transpose(0, 2, 1), remaining)

    return shards


def solution(mesh):
    R, C = mesh.shape["row"], mesh.shape["col"]

    def shards(factor_rows, solved, inverses, link_tile, right_side):
        group = solved.shape[0] // R
        aligned = group == 8 and inverses.shape[1] % 128 == 0 and inverses.shape[2] % 256 == 0
        build = tiled if aligned and C == 4 else generic
        return build(R, C)(factor_rows, solved, inverses, link_tile, right_side)

    placed = (
        P(None, None, ("row", "col")),
        P(None, ("row", "col")),
        P(None, "row", "col"),
        P("col", "row"),
        P(None, "col", None),
    )
    return jax.shard_map(
        shards,
        mesh=mesh,
        in_specs=placed,
        out_specs=(P(None, "col", None), P(None, ("row", "col"))),
        check_vma=False,
    )
```

time: 75.5 us -> 64.7 us (0.86)
  blocking collectives: 24.8 us -> 13.7 us
  starting transfers between devices: 13.7 us -> 24.5 us
  local copies, waits for them, and re-layouts: 9.01 us -> 0.76 us
  Pallas kernels: 0 us -> 4.81 us
  other arithmetic: 4.09 us -> 0.01 us
  matrix products: 6.13 us -> 2.38 us
  waiting for transfers between devices: 16.4 us -> 17.6 us
    all_to_all x3 -> x1, blocking collectives: 24.8 us -> 13.7 us  [exchange(): return lax.all_to_all(value, axes, 0, 0, tiled=False)]
    all_to_all x2 -> x1, waiting for transfers between devices: 16.4 us -> 5.7 us  [exchange(): return lax.all_to_all(value, axes, 0, 0, tiled=False)]
    ppermute x0 -> x5, waiting for transfers between devices: none -> 8.49 us  [xor_col(): return lax.ppermute(value, 'col', [(i, i ^ step) for i in range(C)])]
    ppermute x0 -> x5, starting transfers between devices: none -> 8.05 us  [xor_col(): return lax.ppermute(value, 'col', [(i, i ^ step) for i in range(C)])]
    ppermute x4 -> x14, starting transfers between devices: 4.8 us -> 10.2 us  [xor_row(): return lax.ppermute(value, 'row', [(i, i ^ step) for i in range(R)])]
    pallas_call x0 -> x7, Pallas kernels: none -> 4.81 us  [the longest x6 3.67 us: call(): pl.pallas_call(kernel, grid=(1,), in_specs=[whole_spec(one.shape) for one...]
    dot_general x7 -> x1, matrix products: 6.13 us -> 2.38 us  [shards(): jnp.einsum('nc,kic->nki', held, factor_rows, preferred_element_type=F32)]
    ppermute x4 -> x14, waiting for transfers between devices: 0.01 us -> 3.4 us  [xor_row(): return lax.ppermute(value, 'row', [(i, i ^ step) for i in range(R)])]
  transfers between devices with their start and end apart: 6 -> 20, of which waited for: 2 -> 9; matrix products, arithmetic and copies ran while one was open for 9% -> 5% of each run, Pallas kernels for 0% -> 0%
where the time goes in v3:
time: 64.7 us; the launch traced here: 64.5 us
  starting transfers between devices  24.5 us (38%)
  waiting for transfers between devices  17.6 us (27%)
  blocking collectives  13.7 us (21%)
  Pallas kernels  4.81 us (7%)
  matrix products  2.38 us (4%)
  local copies, waits for them, and re-layouts  0.76 us (1%)
  between operations  0.7 us (1%)
    all_to_all x1, blocking collectives, exchange(): return lax.all_to_all(value, axes, 0, 0, tiled=False)  13.7 us
    ppermute x14, starting transfers between devices, xor_row(): return lax.ppermute(value, 'row', [(i, i ^ step) for i in range(R)])  10.2 us
    ppermute x5, waiting for transfers between devices, xor_col(): return lax.ppermute(value, 'col', [(i, i ^ step) for i in range(C)])  8.49 us
    ppermute x5, starting transfers between devices, xor_col(): return lax.ppermute(value, 'col', [(i, i ^ step) for i in range(C)])  8.05 us
    all_to_all x1, starting transfers between devices, exchange(): return lax.all_to_all(value, axes, 0, 0, tiled=False)  6.26 us
    all_to_all x1, waiting for transfers between devices, exchange(): return lax.all_to_all(value, axes, 0, 0, tiled=False)  5.7 us
    pallas_call x6, Pallas kernels, call(): pl.pallas_call(kernel, grid=(1,), in_specs=[whole_spec(one.shape) for one...  3.67 us
    ppermute x14, waiting for transfers between devices, xor_row(): return lax.ppermute(value, 'row', [(i, i ^ step) for i in range(R)])  3.4 us
  transfers between devices with their start and end apart: 20, of which 9 were waited for; matrix products, arithmetic and copies ran while one was open for 5% of the time, Pallas kernels for 0%

profile of v3, /device:TPU:0, one launch (start us, length us, event | category | flops | bytes accessed | tf_op | source)
XLA Modules:
  0.0 64.5 jit_solution(15915424697295276901)
XLA Ops:
  0.6 1.7 %shard_map.68 = (bf16[1,128,256]{2,1,0:T(8,128)(2,1)}, bf16[2,128,256]{2,1,0:T(8,128)(2,1)}) custom-call(bf16[2,128,256]{2,1,0:T(8,128)(2,1)} %inv_ref.1, bf16[256,128]{1,0:T(8,128)(2,1)} %link_ref.1), custom_call_target="tpu_custom_call" | custom-call | tf_op jit(solution)/shard_map/pallas_call | solution.py:199
  2.3 3.9 %collective-permute-start.3 = (bf16[1,128,256]{2,1,0:T(8,128)(2,1)}, bf16[1,128,256]{2,1,0:T(8,128)(2,1)S(1)}, u32[]{:S(2)}, u32[]{:S(2)}) collective-permute-start(bf16[1,128,256]{2,1,0:T(8,128)(2,1)} %get-tuple-element.16.refs_0_), channel_id=1, source_target_pairs={{0,24},{4,28},{8,16},{12,20},{16,8},{20,12},{24,0},{28,4},{1,25},{... | collective-permute-start | bytes 196616 | tf_op jit(solution)/shard_map/ppermute | solution.py:211
  6.2 0.5 collective-permute-start.2
  6.8 2.0 %collective-permute-start = (bf16[2,128,256]{2,1,0:T(8,128)(2,1)}, bf16[2,128,256]{2,1,0:T(8,128)(2,1)S(1)}, u32[]{:S(2)}, u32[]{:S(2)}) collective-permute-start(bf16[2,128,256]{2,1,0:T(8,128)(2,1)} %get-tuple-element.15.own_ref), channel_id=1, source_target_pairs={{0,1},{1,0},{2,3},{3,2},{4,5},{5,4},{6,7},{7,6},{8,9},{9,8},{10,11... | collective-permute-start | bytes 393224 | tf_op jit(solution)/shard_map/ppermute | solution.py:214
  8.8 2.4 %convolution_convert_fusion = bf16[64,2,1024]{2,0,1:T(8,128)(2,1)S(1)} fusion(bf16[2,1024,512]{2,1,0:T(8,128)(2,1)} %factor_ref.1, bf16[64,512]{1,0:T(8,128)(2,1)} %solved_ref.1), kind=kOutput, calls=%fused_computation | convolution fusion | flops 134348800 | bytes 2424832 | tf_op jit(solution)/shard_map/nc,kic->nki/dot_general | solution.py:232
  11.2 0.7 %copy.9 = bf16[8,8,2,4,256]{4,1,2,3,0:T(8,128)(2,1)} copy(bf16[8,8,2,4,256]{4,1,3,0,2:T(8,128)(2,1)S(1)} %bitcast.18) | data formatting | bytes 524288 | tf_op jit(solution)/shard_map/reshape | solution.py:233
  12.0 6.3 %all-to-all-start = ((bf16[32,16,256]{2,1,0:T(8,128)(2,1)}), bf16[32,16,256]{2,1,0:T(8,128)(2,1)S(1)}, u32[]{:S(2)}, u32[]{:S(2)}) async-start(bf16[32,16,256]{2,1,0:T(8,128)(2,1)} %bitcast.5), calls=%async_computation | async-start | bytes 524288 | tf_op jit(solution)/shard_map/all_to_all | solution.py:29
  18.3 0.3 collective-permute-start.4
  18.6 0.3 collective-permute-start.7
  18.9 0.3 collective-permute-start.6
  19.1 0.3 collective-permute-start.5
  19.4 2.7 %collective-permute-start.15 = (bf16[4,128,256]{2,1,0:T(8,128)(2,1)S(1)}, bf16[4,128,256]{2,1,0:T(8,128)(2,1)S(1)}, u32[]{:S(2)}, u32[]{:S(2)}) collective-permute-start(bf16[4,128,256]{2,1,0:T(8,128)(2,1)S(1)} %shard_map.70.refs_0_.refs_8_.refs_16_.refs_24_), channel_id=1, source_target_pairs={{0,24},{4,28},{8,16},{12,20},{16,8},{20,12},{24,0},{28,4},{1,25},{... | collective-permute-start | bytes 786440 | tf_op jit(solution)/shard_map/ppermute | solution.py:211
  22.2 0.6 collective-permute-start.13
  22.7 0.3 collective-permute-start.11
  23.0 5.7 %all-to-all-done.panel_ref = bf16[32,16,256]{2,1,0:T(8,128)(2,1)S(1)} async-done(((bf16[32,16,256]{2,1,0:T(8,128)(2,1)}), bf16[32,16,256]{2,1,0:T(8,128)(2,1)S(1)}, u32[]{:S(2)}, u32[]{:S(2)}) %all-to-all-start) | async-done | bytes 262176 | tf_op jit(solution)/shard_map/all_to_all | solution.py:29
  28.9 1.0 %collective-permute-start.8 = (bf16[16,640]{1,0:T(8,128)(2,1)S(1)}, bf16[16,640]{1,0:T(8,128)(2,1)S(1)}, u32[]{:S(2)}, u32[]{:S(2)}) collective-permute-start(bf16[16,640]{1,0:T(8,128)(2,1)S(1)} %shard_map.69), channel_id=1, source_target_pairs={{0,1},{1,0},{2,3},{3,2},{4,5},{5,4},{6,7},{7,6},{8,9},{9,8},{10,11... | collective-permute-start | bytes 61448 | tf_op jit(solution)/shard_map/ppermute | solution.py:214
  29.9 2.9 %collective-permute-done.8 = bf16[16,640]{1,0:T(8,128)(2,1)S(1)} collective-permute-done((bf16[16,640]{1,0:T(8,128)(2,1)S(1)}, bf16[16,640]{1,0:T(8,128)(2,1)S(1)}, u32[]{:S(2)}, u32[]{:S(2)}) %collective-permute-start.8) | collective-permute-done | bytes 20512 | tf_op jit(solution)/shard_map/ppermute | solution.py:214
  32.7 0.6 %collective-permute-start.9 = (bf16[16,512]{1,0:T(8,128)(2,1)S(1)}, bf16[16,512]{1,0:T(8,128)(2,1)S(1)}, u32[]{:S(2)}, u32[]{:S(2)}) collective-permute-start(bf16[16,512]{1,0:T(8,128)(2,1)S(1)} %add_convert_fusion.own_ref), channel_id=1, source_target_pairs={{0,2},{1,3},{2,0},{3,1},{4,6},{5,7},{6,4},{7,5},{8,10},{9,11},{10,... | collective-permute-start | bytes 49160 | tf_op jit(solution)/shard_map/ppermute | solution.py:214
  33.4 0.5 collective-permute-start.16
  33.9 2.5 %collective-permute-done.13.refs_4_.refs_12_.refs_20_.refs_28_ = bf16[4,128,256]{2,1,0:T(8,128)(2,1)S(1)} collective-permute-done((bf16[4,128,256]{2,1,0:T(8,128)(2,1)S(1)}, bf16[4,128,256]{2,1,0:T(8,128)(2,1)S(1)}, u32[]{:S(2)}, u32[]{:S(2)}) %collective-permute-start.13) | collective-permute-done | bytes 262176 | tf_op jit(solution)/shard_map/ppermute | solution.py:211
  36.4 0.5 collective-permute-start.12
  36.9 0.5 collective-permute-done.9.other_ref
  37.4 0.5 collective-permute-done.14.refs_5_.refs_13_.refs_21_.refs_29_
  37.9 0.4 collective-permute-done.12.refs_3_.refs_11_.refs_19_.refs_27_
  38.3 0.8 %shard_map.71 = (bf16[16,512]{1,0:T(8,128)(2,1)S(1)}, bf16[8,1024]{1,0:T(8,128)(2,1)S(1)}) custom-call(bf16[16,512]{1,0:T(8,128)(2,1)S(1)} %add_convert_fusion.own_ref, bf16[16,512]{1,0:T(8,128)(2,1)S(1)} %collective-permute-done.9.other_ref, bf16[2,16,128]{2,1,0:T(8,128)(2,1)S(1)} %pad_maximum_fusion.side_ref, ...), custom_call_target="tpu_custom_call" | custom-call | tf_op jit(solution)/shard_map/pallas_call | solution.py:199
  39.1 2.3 %collective-permute-start.17 = (bf16[16,512]{1,0:T(8,128)(2,1)S(1)}, bf16[16,512]{1,0:T(8,128)(2,1)S(1)}, u32[]{:S(2)}, u32[]{:S(2)}) collective-permute-start(bf16[16,512]{1,0:T(8,128)(2,1)S(1)} %get-tuple-element.23.own_ref), channel_id=1, source_target_pairs={{0,2},{1,3},{2,0},{3,1},{4,6},{5,7},{6,4},{7,5},{8,10},{9,11},{10,... | collective-permute-start | bytes 49160 | tf_op jit(solution)/shard_map/ppermute | solution.py:214
  41.4 2.5 %collective-permute-done.17.other_ref = bf16[16,512]{1,0:T(8,128)(2,1)S(1)} collective-permute-done((bf16[16,512]{1,0:T(8,128)(2,1)S(1)}, bf16[16,512]{1,0:T(8,128)(2,1)S(1)}, u32[]{:S(2)}, u32[]{:S(2)}) %collective-permute-start.17) | collective-permute-done | bytes 16416 | tf_op jit(solution)/shard_map/ppermute | solution.py:214
  43.9 0.8 %shard_map.72 = (bf16[16,512]{1,0:T(8,128)(2,1)S(1)}, bf16[8,256]{1,0:T(8,128)(2,1)S(1)}) custom-call(bf16[16,512]{1,0:T(8,128)(2,1)S(1)} %get-tuple-element.23.own_ref, bf16[16,512]{1,0:T(8,128)(2,1)S(1)} %collective-permute-done.17.other_ref, bf16[4,128,256]{2,1,0:T(8,128)(2,1)S(1)} %shard_map.70.refs_0_.refs_8_.refs_16_.refs_24_, ...), custom_call_target="tpu_custom_call" | custom-call | tf_op jit(solution)/shard_map/pallas_call | solution.py:199
  44.7 2.2 %collective-permute-start.18 = (bf16[16,512]{1,0:T(8,128)(2,1)S(1)}, bf16[16,512]{1,0:T(8,128)(2,1)S(1)}, u32[]{:S(2)}, u32[]{:S(2)}) collective-permute-start(bf16[16,512]{1,0:T(8,128)(2,1)S(1)} %get-tuple-element.25.own_ref), channel_id=1, source_target_pairs={{0,2},{1,3},{2,0},{3,1},{4,6},{5,7},{6,4},{7,5},{8,10},{9,11},{10,... | collective-permute-start | bytes 49160 | tf_op jit(solution)/shard_map/ppermute | solution.py:214
  46.9 2.5 %collective-permute-done.18.other_ref = bf16[16,512]{1,0:T(8,128)(2,1)S(1)} collective-permute-done((bf16[16,512]{1,0:T(8,128)(2,1)S(1)}, bf16[16,512]{1,0:T(8,128)(2,1)S(1)}, u32[]{:S(2)}, u32[]{:S(2)}) %collective-permute-start.18) | collective-permute-done | bytes 16416 | tf_op jit(solution)/shard_map/ppermute | solution.py:214
  49.6 13.7 %all_to_all.10.whole_ref = bf16[32,16,256]{2,1,0:T(8,128)(2,1)S(1)} all-to-all(bf16[32,16,256]{2,1,0:T(8,128)(2,1)S(1)} %shard_map.73), channel_id=1, replica_groups=mesh['row'=8,'col'=4] {'row','col'}, dimensions={0} | all-to-all | bytes 524288 | tf_op jit(solution)/shard_map/all_to_all | solution.py:29
  63.3 1.1 %shard_map.74 = (f32[64,512]{1,0:T(8,128)}, f32[2,64,256]{2,1,0:T(8,128)}) custom-call(bf16[64,512]{1,0:T(8,128)(2,1)S(1)} %copy-done.2, bf16[2,1024,512]{2,1,0:T(8,128)(2,1)S(1)} %copy-done.1, bf16[32,16,256]{2,1,0:T(8,128)(2,1)S(1)} %all_to_all.10.whole_ref), custom_call_target="tpu_custom_call" | custom-call | tf_op jit(solution)/shard_map/pallas_call | solution.py:273
  (33 shorter events, 0.7 us)
Async XLA Ops:
  0.6 18.8 %copy-start = (f32[2,256,64]{1,2,0:T(8,128)S(1)}, f32[2,256,64]{1,2,0:T(8,128)}, u32[]{:S(2)}) copy-start(f32[2,256,64]{1,2,0:T(8,128)} %param.9) | copy-start | bytes 393220
  2.3 16.0 %copy-start.3 = (bf16[1,128,256]{2,1,0:T(8,128)(2,1)S(1)}, bf16[1,128,256]{2,1,0:T(8,128)(2,1)}, u32[]{:S(2)}) copy-start(bf16[1,128,256]{2,1,0:T(8,128)(2,1)} %get-tuple-element.16.refs_0_) | copy-start | bytes 196612
  2.3 17.1 %copy-start.4 = (bf16[2,128,256]{2,1,0:T(8,128)(2,1)S(1)}, bf16[2,128,256]{2,1,0:T(8,128)(2,1)}, u32[]{:S(2)}) copy-start(bf16[2,128,256]{2,1,0:T(8,128)(2,1)} %get-tuple-element.15.own_ref) | copy-start | bytes 393220
  2.3 9.6 %collective-permute-start.3 = (bf16[1,128,256]{2,1,0:T(8,128)(2,1)}, bf16[1,128,256]{2,1,0:T(8,128)(2,1)S(1)}, u32[]{:S(2)}, u32[]{:S(2)}) collective-permute-start(bf16[1,128,256]{2,1,0:T(8,128)(2,1)} %get-tuple-element.16.refs_0_), channel_id=1, source_target_pairs={{0,24},{4,28},{8,16},{12,20},{16,8},{20,12},{24,0},{28,4},{1,25},{... | collective-permute-start | bytes 196616 | tf_op jit(solution)/shard_map/ppermute | solution.py:211
  6.2 5.7 %collective-permute-start.2 = (bf16[1,128,256]{2,1,0:T(8,128)(2,1)}, bf16[1,128,256]{2,1,0:T(8,128)(2,1)S(1)}, u32[]{:S(2)}, u32[]{:S(2)}) collective-permute-start(bf16[1,128,256]{2,1,0:T(8,128)(2,1)} %get-tuple-element.16.refs_0_), channel_id=1, source_target_pairs={{0,16},{4,20},{8,24},{12,28},{16,0},{20,4},{24,8},{28,12},{1,17},{... | collective-permute-start | bytes 196616 | tf_op jit(solution)/shard_map/ppermute | solution.py:211
  6.7 5.2 %collective-permute-start.1 = (bf16[1,128,256]{2,1,0:T(8,128)(2,1)}, bf16[1,128,256]{2,1,0:T(8,128)(2,1)S(1)}, u32[]{:S(2)}, u32[]{:S(2)}) collective-permute-start(bf16[1,128,256]{2,1,0:T(8,128)(2,1)} %get-tuple-element.16.refs_0_), channel_id=1, source_target_pairs={{0,8},{4,12},{8,0},{12,4},{16,24},{20,28},{24,16},{28,20},{1,9},{5... | collective-permute-start | bytes 196616 | tf_op jit(solution)/shard_map/ppermute | solution.py:211
  6.8 5.2 %collective-permute-start = (bf16[2,128,256]{2,1,0:T(8,128)(2,1)}, bf16[2,128,256]{2,1,0:T(8,128)(2,1)S(1)}, u32[]{:S(2)}, u32[]{:S(2)}) collective-permute-start(bf16[2,128,256]{2,1,0:T(8,128)(2,1)} %get-tuple-element.15.own_ref), channel_id=1, source_target_pairs={{0,1},{1,0},{2,3},{3,2},{4,5},{5,4},{6,7},{7,6},{8,9},{9,8},{10,11... | collective-permute-start | bytes 393224 | tf_op jit(solution)/shard_map/ppermute | solution.py:214
  12.0 16.7 %all-to-all-start = ((bf16[32,16,256]{2,1,0:T(8,128)(2,1)}), bf16[32,16,256]{2,1,0:T(8,128)(2,1)S(1)}, u32[]{:S(2)}, u32[]{:S(2)}) async-start(bf16[32,16,256]{2,1,0:T(8,128)(2,1)} %bitcast.5), calls=%async_computation | async-start | bytes 524288 | tf_op jit(solution)/shard_map/all_to_all | solution.py:29
  18.3 3.9 %collective-permute-start.4 = (bf16[1,128,256]{2,1,0:T(8,128)(2,1)S(1)}, bf16[1,128,256]{2,1,0:T(8,128)(2,1)S(1)}, u32[]{:S(2)}, u32[]{:S(2)}) collective-permute-start(bf16[1,128,256]{2,1,0:T(8,128)(2,1)S(1)} %copy-done.3), channel_id=1, source_target_pairs={{0,4},{4,0},{8,12},{12,8},{16,20},{20,16},{24,28},{28,24},{1,5},{5... | collective-permute-start | bytes 196616 | tf_op jit(solution)/shard_map/ppermute | solution.py:211
  18.6 4.1 %collective-permute-start.7 = (bf16[1,128,256]{2,1,0:T(8,128)(2,1)S(1)}, bf16[1,128,256]{2,1,0:T(8,128)(2,1)S(1)}, u32[]{:S(2)}, u32[]{:S(2)}) collective-permute-start(bf16[1,128,256]{2,1,0:T(8,128)(2,1)S(1)} %collective-permute-done.3.refs_6_), channel_id=1, source_target_pairs={{0,4},{4,0},{8,12},{12,8},{16,20},{20,16},{24,28},{28,24},{1,5},{5... | collective-permute-start | bytes 196616 | tf_op jit(solution)/shard_map/ppermute | solution.py:211
  18.9 4.1 %collective-permute-start.6 = (bf16[1,128,256]{2,1,0:T(8,128)(2,1)S(1)}, bf16[1,128,256]{2,1,0:T(8,128)(2,1)S(1)}, u32[]{:S(2)}, u32[]{:S(2)}) collective-permute-start(bf16[1,128,256]{2,1,0:T(8,128)(2,1)S(1)} %collective-permute-done.2.refs_4_), channel_id=1, source_target_pairs={{0,4},{4,0},{8,12},{12,8},{16,20},{20,16},{24,28},{28,24},{1,5},{5... | collective-permute-start | bytes 196616 | tf_op jit(solution)/shard_map/ppermute | solution.py:211
  19.1 3.9 %collective-permute-start.5 = (bf16[1,128,256]{2,1,0:T(8,128)(2,1)S(1)}, bf16[1,128,256]{2,1,0:T(8,128)(2,1)S(1)}, u32[]{:S(2)}, u32[]{:S(2)}) collective-permute-start(bf16[1,128,256]{2,1,0:T(8,128)(2,1)S(1)} %collective-permute-done.1.refs_2_), channel_id=1, source_target_pairs={{0,4},{4,0},{8,12},{12,8},{16,20},{20,16},{24,28},{28,24},{1,5},{5... | collective-permute-start | bytes 196616 | tf_op jit(solution)/shard_map/ppermute | solution.py:211
  19.4 14.0 %collective-permute-start.15 = (bf16[4,128,256]{2,1,0:T(8,128)(2,1)S(1)}, bf16[4,128,256]{2,1,0:T(8,128)(2,1)S(1)}, u32[]{:S(2)}, u32[]{:S(2)}) collective-permute-start(bf16[4,128,256]{2,1,0:T(8,128)(2,1)S(1)} %shard_map.70.refs_0_.refs_8_.refs_16_.refs_24_), channel_id=1, source_target_pairs={{0,24},{4,28},{8,16},{12,20},{16,8},{20,12},{24,0},{28,4},{1,25},{... | collective-permute-start | bytes 786440 | tf_op jit(solution)/shard_map/ppermute | solution.py:211
  22.2 14.2 %collective-permute-start.13 = (bf16[4,128,256]{2,1,0:T(8,128)(2,1)S(1)}, bf16[4,128,256]{2,1,0:T(8,128)(2,1)S(1)}, u32[]{:S(2)}, u32[]{:S(2)}) collective-permute-start(bf16[4,128,256]{2,1,0:T(8,128)(2,1)S(1)} %shard_map.70.refs_0_.refs_8_.refs_16_.refs_24_), channel_id=1, source_target_pairs={{0,16},{4,20},{8,24},{12,28},{16,0},{20,4},{24,8},{28,12},{1,17},{... | collective-permute-start | bytes 786440 | tf_op jit(solution)/shard_map/ppermute | solution.py:211
  22.7 13.7 %collective-permute-start.11 = (bf16[4,128,256]{2,1,0:T(8,128)(2,1)S(1)}, bf16[4,128,256]{2,1,0:T(8,128)(2,1)S(1)}, u32[]{:S(2)}, u32[]{:S(2)}) collective-permute-start(bf16[4,128,256]{2,1,0:T(8,128)(2,1)S(1)} %shard_map.70.refs_0_.refs_8_.refs_16_.refs_24_), channel_id=1, source_target_pairs={{0,8},{4,12},{8,0},{12,4},{16,24},{20,28},{24,16},{28,20},{1,9},{5... | collective-permute-start | bytes 786440 | tf_op jit(solution)/shard_map/ppermute | solution.py:211
  28.9 3.8 %collective-permute-start.8 = (bf16[16,640]{1,0:T(8,128)(2,1)S(1)}, bf16[16,640]{1,0:T(8,128)(2,1)S(1)}, u32[]{:S(2)}, u32[]{:S(2)}) collective-permute-start(bf16[16,640]{1,0:T(8,128)(2,1)S(1)} %shard_map.69), channel_id=1, source_target_pairs={{0,1},{1,0},{2,3},{3,2},{4,5},{5,4},{6,7},{7,6},{8,9},{9,8},{10,11... | collective-permute-start | bytes 61448 | tf_op jit(solution)/shard_map/ppermute | solution.py:214
  32.7 4.7 %collective-permute-start.9 = (bf16[16,512]{1,0:T(8,128)(2,1)S(1)}, bf16[16,512]{1,0:T(8,128)(2,1)S(1)}, u32[]{:S(2)}, u32[]{:S(2)}) collective-permute-start(bf16[16,512]{1,0:T(8,128)(2,1)S(1)} %add_convert_fusion.own_ref), channel_id=1, source_target_pairs={{0,2},{1,3},{2,0},{3,1},{4,6},{5,7},{6,4},{7,5},{8,10},{9,11},{10,... | collective-permute-start | bytes 49160 | tf_op jit(solution)/shard_map/ppermute | solution.py:214
  33.4 4.1 %collective-permute-start.10 = (bf16[4,128,256]{2,1,0:T(8,128)(2,1)S(1)}, bf16[4,128,256]{2,1,0:T(8,128)(2,1)S(1)}, u32[]{:S(2)}, u32[]{:S(2)}) collective-permute-start(bf16[4,128,256]{2,1,0:T(8,128)(2,1)S(1)} %shard_map.70.refs_0_.refs_8_.refs_16_.refs_24_), channel_id=1, source_target_pairs={{0,4},{4,0},{8,12},{12,8},{16,20},{20,16},{24,28},{28,24},{1,5},{5... | collective-permute-start | bytes 786440 | tf_op jit(solution)/shard_map/ppermute | solution.py:211
  33.4 4.1 %collective-permute-start.16 = (bf16[4,128,256]{2,1,0:T(8,128)(2,1)S(1)}, bf16[4,128,256]{2,1,0:T(8,128)(2,1)S(1)}, u32[]{:S(2)}, u32[]{:S(2)}) collective-permute-start(bf16[4,128,256]{2,1,0:T(8,128)(2,1)S(1)} %collective-permute-done.15.refs_6_.refs_14_.refs_22_.refs_30_), channel_id=1, source_target_pairs={{0,4},{4,0},{8,12},{12,8},{16,20},{20,16},{24,28},{28,24},{1,5},{5... | collective-permute-start | bytes 786440 | tf_op jit(solution)/shard_map/ppermute | solution.py:211
  36.4 1.5 %collective-permute-start.14 = (bf16[4,128,256]{2,1,0:T(8,128)(2,1)S(1)}, bf16[4,128,256]{2,1,0:T(8,128)(2,1)S(1)}, u32[]{:S(2)}, u32[]{:S(2)}) collective-permute-start(bf16[4,128,256]{2,1,0:T(8,128)(2,1)S(1)} %collective-permute-done.13.refs_4_.refs_12_.refs_20_.refs_28_), channel_id=1, source_target_pairs={{0,4},{4,0},{8,12},{12,8},{16,20},{20,16},{24,28},{28,24},{1,5},{5... | collective-permute-start | bytes 786440 | tf_op jit(solution)/shard_map/ppermute | solution.py:211
  36.4 1.9 %collective-permute-start.12 = (bf16[4,128,256]{2,1,0:T(8,128)(2,1)S(1)}, bf16[4,128,256]{2,1,0:T(8,128)(2,1)S(1)}, u32[]{:S(2)}, u32[]{:S(2)}) collective-permute-start(bf16[4,128,256]{2,1,0:T(8,128)(2,1)S(1)} %collective-permute-done.11.refs_2_.refs_10_.refs_18_.refs_26_), channel_id=1, source_target_pairs={{0,4},{4,0},{8,12},{12,8},{16,20},{20,16},{24,28},{28,24},{1,5},{5... | collective-permute-start | bytes 786440 | tf_op jit(solution)/shard_map/ppermute | solution.py:211
  39.1 24.2 %copy-start.2 = (bf16[64,512]{1,0:T(8,128)(2,1)S(1)}, bf16[64,512]{1,0:T(8,128)(2,1)}, u32[]{:S(2)}) copy-start(bf16[64,512]{1,0:T(8,128)(2,1)} %solved_ref.1) | copy-start | bytes 196612
  39.1 4.8 %collective-permute-start.17 = (bf16[16,512]{1,0:T(8,128)(2,1)S(1)}, bf16[16,512]{1,0:T(8,128)(2,1)S(1)}, u32[]{:S(2)}, u32[]{:S(2)}) collective-permute-start(bf16[16,512]{1,0:T(8,128)(2,1)S(1)} %get-tuple-element.23.own_ref), channel_id=1, source_target_pairs={{0,2},{1,3},{2,0},{3,1},{4,6},{5,7},{6,4},{7,5},{8,10},{9,11},{10,... | collective-permute-start | bytes 49160 | tf_op jit(solution)/shard_map/ppermute | solution.py:214
  43.9 19.4 %copy-start.1 = (bf16[2,1024,512]{2,1,0:T(8,128)(2,1)S(1)}, bf16[2,1024,512]{2,1,0:T(8,128)(2,1)}, u32[]{:S(2)}) copy-start(bf16[2,1024,512]{2,1,0:T(8,128)(2,1)} %factor_ref.1) | copy-start | bytes 6291460
  44.7 4.7 %collective-permute-start.18 = (bf16[16,512]{1,0:T(8,128)(2,1)S(1)}, bf16[16,512]{1,0:T(8,128)(2,1)S(1)}, u32[]{:S(2)}, u32[]{:S(2)}) collective-permute-start(bf16[16,512]{1,0:T(8,128)(2,1)S(1)} %get-tuple-element.25.own_ref), channel_id=1, source_target_pairs={{0,2},{1,3},{2,0},{3,1},{4,6},{5,7},{6,4},{7,5},{8,10},{9,11},{10,... | collective-permute-start | bytes 49160 | tf_op jit(solution)/shard_map/ppermute | solution.py:214

commit v4 on v3

--- a/solution.py
+++ b/solution.py
@@ -5,10 +5,12 @@
 from jax import lax
 from jax.experimental import pallas as pl
 from jax.experimental.pallas import tpu as pltpu
+from jax.sharding import Mesh
 from jax.sharding import PartitionSpec as P
 
 BF = jnp.bfloat16
 F32 = jnp.float32
+ROW = ("chip", "core")
 PARAMS = pltpu.CompilerParams(vmem_limit_bytes=12 * 2**20)
 WIDE = pltpu.CompilerParams(vmem_limit_bytes=62 * 2**20)
 
@@ -100,21 +102,38 @@
     both_ref[2:] = far_ref[...]
 
 
-def order_kernel(value_ref, part_ref):
+def panel_kernel(solved_ref, factor_ref, part_ref, solved, factor, sems):
     R, C, double, rows = part_ref.shape
+    step = C // 4
+    copies = [pltpu.make_async_copy(solved_ref, solved, sems.at[0])]
+    for i in range(4):
+        chunk = pl.ds(i * step * rows, step * rows)
+        copies.append(pltpu.make_async_copy(factor_ref.at[:, chunk], factor.at[:, chunk], sems.at[1 + i]))
+    for copy in copies:
+        copy.start()
+    copies[0].wait()
+    value = solved[...]
     for c in range(C):
-        halves = [value_ref[k, :, c * rows : (c + 1) * rows].astype(F32).reshape(R, double // 2, rows) for k in range(2)]
+        if c % step == 0:
+            copies[1 + c // step].wait()
+        halves = [flipped(value, factor[k, c * rows : (c + 1) * rows]) for k in range(2)]
+        halves = [half.reshape(R, double // 2, rows) for half in halves]
         part_ref[:, c] = jnp.concatenate(halves, axis=1).astype(BF)
 
 
-def closing_kernel(C, solved_ref, factor_ref, whole_ref, remaining_ref, back_ref):
-    group, rows = whole_ref.shape[1] // 2, whole_ref.shape[2]
-    nrhs = solved_ref.shape[0]
-    R = nrhs // group
+def closing_kernel(C, solved_ref, factor_ref, own_ref, other_ref, remaining_ref, back_ref):
+    chips = own_ref.shape[0] // C
+    group, rows = own_ref.shape[1] // 2, own_ref.shape[2]
+    even = lax.axis_index("core") == 0
     here = lax.axis_index("col")
 
     def columns(k, c):
-        return jnp.concatenate([whole_ref[r * C + c, k * group : (k + 1) * group].astype(F32) for r in range(R)], axis=0)
+        parts = []
+        for chip in range(chips):
+            own = own_ref[chip * C + c, k * group : (k + 1) * group].astype(F32)
+            other = other_ref[chip * C + c, k * group : (k + 1) * group].astype(F32)
+            parts += [jnp.where(even, own, other), jnp.where(even, other, own)]
+        return jnp.concatenate(parts, axis=0)
 
     update = None
     for k in range(2):
@@ -206,9 +225,29 @@
     )(*operands, *[tile[0] for tile in tiles])
 
 
+def call_flat(kernel, operands, tiles, shapes):
+    arrays = []
+    for array, _ in tiles:
+        if all(array is not one for one in arrays):
+            arrays.append(array)
+    places = [([array is one for one in arrays].index(True), which) for array, which in tiles]
+    count = len(operands)
+
+    def body(*refs):
+        held = refs[count : count + len(arrays)]
+        views = [held[i].at[pl.ds(which, 1)] for i, which in places]
+        kernel(*refs[:count], *views, *refs[count + len(arrays) :])
+
+    return pl.pallas_call(
+        body,
+        out_shape=[jax.ShapeDtypeStruct(shape, BF) for shape in shapes],
+        compiler_params=PARAMS,
+    )(*operands, *arrays)
+
+
 def tiled(R, C):
     def xor_row(value, step):
-        return lax.ppermute(value, "row", [(i, i ^ step) for i in range(R)])
+        return lax.ppermute(value, ROW, [(i, i ^ step) for i in range(R)])
 
     def xor_col(value, step):
         return lax.ppermute(value, "col", [(i, i ^ step) for i in range(C)])
@@ -229,14 +268,23 @@
 
         first_own, pair = call(pack_kernel, [inverses, link_tile], [], [(1, size, rows), (2, size, rows)], WIDE)
         held = solved
-        part = jnp.einsum("nc,kic->nki", held, factor_rows, preferred_element_type=F32).astype(BF)
-        part = part.reshape(R, group, 2, C, rows).transpose(0, 3, 2, 1, 4)
+        part = pl.pallas_call(
+            panel_kernel,
+            in_specs=[pl.BlockSpec(memory_space=pl.ANY)] * 2,
+            out_shape=jax.ShapeDtypeStruct((R, C) + cut, BF),
+            scratch_shapes=[
+                pltpu.VMEM(solved.shape, BF),
+                pltpu.VMEM(factor_rows.shape, BF),
+                pltpu.SemaphoreType.DMA((5,)),
+            ],
+            compiler_params=WIDE,
+        )(held, factor_rows)
         far = xor_col(pair, 1)
         first_in = first_own
         evens = in_plane(first_in)
         part, *_ = lax.optimization_barrier((part, far, *evens))
-        panel = exchange(part.reshape((R * C,) + cut), ("row", "col"))
-        mine = lax.dynamic_slice_in_dim(right_side, lax.axis_index("row") * group, group, 2)
+        panel = exchange(part.reshape((R * C,) + cut), ROW + ("col",))
+        mine = lax.dynamic_slice_in_dim(right_side, lax.axis_index(ROW) * group, group, 2)
         mine = mine.transpose(0, 2, 1).reshape(cut)
 
         first_tiles = [(tile, 0) for tile in with_mates(evens)]
@@ -266,10 +314,11 @@
         side = jnp.stack([sent[:, wide:], arrived[:, wide:]])
         sent = (sent[:, :wide].astype(F32) + arrived[:, :wide].astype(F32)).astype(BF)
         link = functools.partial(link_kernel, R)
-        sent, first = call(link, [sent, xor_col(sent, 2), side], links + last_tiles, [summed, (group, order)])
+        sent, first = call_flat(link, [sent, xor_col(sent, 2), side], links + last_tiles, [summed, (group, order)])
         turn = functools.partial(turn_kernel, R)
-        sent, short = call(turn, [sent, xor_col(sent, 2)], last_tiles + links, [summed, (group, rows)])
-        (sent,) = call(last_kernel, [first, short, sent, xor_col(sent, 2)], first_tiles, [(R * C,) + cut])
+        sent, short = call_flat(turn, [sent, xor_col(sent, 2)], last_tiles + links, [summed, (group, rows)])
+        (sent,) = call_flat(last_kernel, [first, short, sent, xor_col(sent, 2)], first_tiles, [(R // 2 * C,) + cut])
+        whole = exchange(sent, ("chip", "col"))
         remaining, back = pl.pallas_call(
             functools.partial(closing_kernel, C),
             out_shape=(
@@ -277,7 +326,7 @@
                 jax.ShapeDtypeStruct((2, nrhs, rows), F32),
             ),
             compiler_params=PARAMS,
-        )(solved, factor_rows, exchange(sent, ("row", "col")))
+        )(solved, factor_rows, whole, xor_row(whole, 1))
         return (back.transpose(0, 2, 1), remaining)
 
     return shards
@@ -286,23 +335,20 @@
 def solution(mesh):
     R, C = mesh.shape["row"], mesh.shape["col"]
 
-    def shards(factor_rows, solved, inverses, link_tile, right_side):
-        group = solved.shape[0] // R
-        aligned = group == 8 and inverses.shape[1] % 128 == 0 and inverses.shape[2] % 256 == 0
-        build = tiled if aligned and C == 4 else generic
-        return build(R, C)(factor_rows, solved, inverses, link_tile, right_side)
-
-    placed = (
-        P(None, None, ("row", "col")),
-        P(None, ("row", "col")),
-        P(None, "row", "col"),
-        P("col", "row"),
-        P(None, "col", None),
-    )
-    return jax.shard_map(
-        shards,
-        mesh=mesh,
-        in_specs=placed,
-        out_specs=(P(None, "col", None), P(None, ("row", "col"))),
-        check_vma=False,
-    )
+    def whole(factor_rows, solved, inverses, link_tile, right_side):
+        group, size, rows = solved.shape[0] // R, inverses.shape[1] // R, inverses.shape[2] // C
+        if group == 8 and size % 128 == 0 and rows % 256 == 0 and C == 4 and R % 2 == 0:
+            split, row, build = Mesh(mesh.devices.reshape(R // 2, 2, C), ROW + ("col",)), ROW, tiled
+        else:
+            split, row, build = mesh, ("row",), generic
+        both = row + ("col",)
+        placed = (P(None, None, both), P(None, both), P(None, row, "col"), P("col", row), P(None, "col", None))
+        return jax.shard_map(
+            build(R, C),
+            mesh=split,
+            in_specs=placed,
+            out_specs=(P(None, "col", None), P(None, both)),
+            check_vma=False,
+        )(factor_rows, solved, inverses, link_tile, right_side)
+
+    return whole

time: 64.7 us -> 62.9 us (0.972)
  Pallas kernels: 4.81 us -> 7.78 us
  matrix products: 2.38 us -> 0 us
  starting transfers between devices: 24.5 us -> 22.2 us
  waiting for transfers between devices: 17.6 us -> 19.8 us
  blocking collectives: 13.7 us -> 12.1 us
  local copies, waits for them, and re-layouts: 0.76 us -> 0.03 us
    pallas_call x0 -> x4, Pallas kernels: none -> 4.73 us  [the longest x1 2.97 us: shards(): pl.pallas_call(panel_kernel, in_specs=[pl.BlockSpec(memory_space=pl.ANY)]...]
    dot_general x1 -> x0, matrix products: 2.38 us -> none  [shards(): jnp.einsum('nc,kic->nki', held, factor_rows, preferred_element_type=F32)]
    all_to_all x1, starting transfers between devices: 6.26 us -> 3.92 us  [exchange(): return lax.all_to_all(value, axes, 0, 0, tiled=False)]
    ppermute x14 -> x15, waiting for transfers between devices: 3.4 us -> 5.69 us  [xor_row(): return lax.ppermute(value, ROW, [(i, i ^ step) for i in range(R)])]
    pallas_call x6 -> x3, Pallas kernels: 3.67 us -> 1.91 us  [call(): pl.pallas_call(kernel, grid=(1,), in_specs=[whole_spec(one.shape) for one...]
    all_to_all x1, blocking collectives: 13.7 us -> 12.1 us  [exchange(): return lax.all_to_all(value, axes, 0, 0, tiled=False)]
    ppermute x5, starting transfers between devices: 8.05 us -> 9.09 us  [xor_col(): return lax.ppermute(value, 'col', [(i, i ^ step) for i in range(C)])]
    ppermute x14 -> x15, starting transfers between devices: 10.2 us -> 9.15 us  [xor_row(): return lax.ppermute(value, ROW, [(i, i ^ step) for i in range(R)])]
  transfers between devices with their start and end apart: 20 -> 21, of which waited for: 9 -> 11; matrix products, arithmetic and copies ran while one was open for 5% -> 0% of each run, Pallas kernels for 0% -> 5%
where the time goes in v4:
time: 62.9 us; the launch traced here: 62.6 us
  starting transfers between devices  22.2 us (35%)
  waiting for transfers between devices  19.8 us (31%)
  blocking collectives  12.1 us (19%)
  Pallas kernels  7.78 us (12%)
  between operations  0.71 us (1%)
    all_to_all x1, blocking collectives, exchange(): return lax.all_to_all(value, axes, 0, 0, tiled=False)  12.1 us
    ppermute x15, starting transfers between devices, xor_row(): return lax.ppermute(value, ROW, [(i, i ^ step) for i in range(R)])  9.15 us
    ppermute x5, starting transfers between devices, xor_col(): return lax.ppermute(value, 'col', [(i, i ^ step) for i in range(C)])  9.09 us
    ppermute x5, waiting for transfers between devices, xor_col(): return lax.ppermute(value, 'col', [(i, i ^ step) for i in range(C)])  8.41 us
    all_to_all x1, waiting for transfers between devices, exchange(): return lax.all_to_all(value, axes, 0, 0, tiled=False)  5.7 us
    ppermute x15, waiting for transfers between devices, xor_row(): return lax.ppermute(value, ROW, [(i, i ^ step) for i in range(R)])  5.69 us
    all_to_all x1, starting transfers between devices, exchange(): return lax.all_to_all(value, axes, 0, 0, tiled=False)  3.92 us
    pallas_call x1, Pallas kernels, shards(): pl.pallas_call(panel_kernel, in_specs=[pl.BlockSpec(memory_space=pl.ANY)]...  2.97 us
  transfers between devices with their start and end apart: 21, of which 11 were waited for; matrix products, arithmetic and copies ran while one was open for 0% of the time, Pallas kernels for 5%

profile of v4, /device:TPU:0, one launch (start us, length us, event | category | flops | bytes accessed | tf_op | source)
XLA Modules:
  0.0 62.6 jit_solution(263317846219379749)
XLA Ops:
  0.6 1.7 %shard_map.69 = (bf16[1,128,256]{2,1,0:T(8,128)(2,1)}, bf16[2,128,256]{2,1,0:T(8,128)(2,1)}) custom-call(bf16[2,128,256]{2,1,0:T(8,128)(2,1)} %inv_ref.1, bf16[256,128]{1,0:T(8,128)(2,1)} %link_ref.1), custom_call_target="tpu_custom_call" | custom-call | tf_op jit(solution)/shard_map/pallas_call | solution.py:218
  2.3 3.0 %collective-permute-start = (bf16[2,128,256]{2,1,0:T(8,128)(2,1)}, bf16[2,128,256]{2,1,0:T(8,128)(2,1)S(1)}, u32[]{:S(2)}, u32[]{:S(2)}) collective-permute-start(bf16[2,128,256]{2,1,0:T(8,128)(2,1)} %get-tuple-element.15.own_ref), channel_id=1, source_target_pairs={{0,1},{1,0},{2,3},{3,2},{4,5},{5,4},{6,7},{7,6},{8,9},{9,8},{10,11... | collective-permute-start | bytes 393224 | tf_op jit(solution)/shard_map/ppermute | solution.py:253
  5.3 2.4 %collective-permute-start.3 = (bf16[1,128,256]{2,1,0:T(8,128)(2,1)}, bf16[1,128,256]{2,1,0:T(8,128)(2,1)S(1)}, u32[]{:S(2)}, u32[]{:S(2)}) collective-permute-start(bf16[1,128,256]{2,1,0:T(8,128)(2,1)} %get-tuple-element.16.refs_0_.refs_4_), channel_id=1, source_target_pairs={{0,24},{4,28},{8,16},{12,20},{16,8},{20,12},{24,0},{28,4},{1,25},{... | collective-permute-start | bytes 196616 | tf_op jit(solution)/shard_map/ppermute | solution.py:250
  7.8 0.5 collective-permute-start.2
  8.3 0.5 collective-permute-start.1
  8.8 3.0 %shard_map.68 = bf16[8,4,16,256]{3,2,1,0:T(8,128)(2,1)} custom-call(bf16[64,512]{1,0:T(8,128)(2,1)} %solved_ref.3, bf16[2,1024,512]{2,1,0:T(8,128)(2,1)} %factor_ref.3), custom_call_target="tpu_custom_call" | custom-call | tf_op jit(solution)/shard_map/pallas_call | solution.py:271
  11.8 0.4 collective-permute-done.2.refs_4_.refs_8_
  12.3 0.5 collective-permute-done.1.refs_2_.refs_6_
  12.8 3.9 %all-to-all-start = ((bf16[32,16,256]{2,1,0:T(8,128)(2,1)}), bf16[32,16,256]{2,1,0:T(8,128)(2,1)S(1)}, u32[]{:S(2)}, u32[]{:S(2)}) async-start(bf16[32,16,256]{2,1,0:T(8,128)(2,1)} %bitcast.10), calls=%async_computation | async-start | bytes 524288 | tf_op jit(solution)/shard_map/all_to_all | solution.py:31
  16.7 0.3 collective-permute-start.4
  17.8 2.7 %collective-permute-start.15 = (bf16[4,128,256]{2,1,0:T(8,128)(2,1)S(1)}, bf16[4,128,256]{2,1,0:T(8,128)(2,1)S(1)}, u32[]{:S(2)}, u32[]{:S(2)}) collective-permute-start(bf16[4,128,256]{2,1,0:T(8,128)(2,1)S(1)} %shard_map.71.refs_3_.refs_2_), channel_id=1, source_target_pairs={{0,24},{4,28},{8,16},{12,20},{16,8},{20,12},{24,0},{28,4},{1,25},{... | collective-permute-start | bytes 786440 | tf_op jit(solution)/shard_map/ppermute | solution.py:250
  20.6 0.6 collective-permute-start.13
  21.1 0.3 collective-permute-start.11
  21.4 5.7 %all-to-all-done.panel_ref = bf16[32,16,256]{2,1,0:T(8,128)(2,1)S(1)} async-done(((bf16[32,16,256]{2,1,0:T(8,128)(2,1)}), bf16[32,16,256]{2,1,0:T(8,128)(2,1)S(1)}, u32[]{:S(2)}, u32[]{:S(2)}) %all-to-all-start) | async-done | bytes 262176 | tf_op jit(solution)/shard_map/all_to_all | solution.py:31
  27.3 1.0 %collective-permute-start.8 = (bf16[16,640]{1,0:T(8,128)(2,1)S(1)}, bf16[16,640]{1,0:T(8,128)(2,1)S(1)}, u32[]{:S(2)}, u32[]{:S(2)}) collective-permute-start(bf16[16,640]{1,0:T(8,128)(2,1)S(1)} %shard_map.70), channel_id=1, source_target_pairs={{0,1},{1,0},{2,3},{3,2},{4,5},{5,4},{6,7},{7,6},{8,9},{9,8},{10,11... | collective-permute-start | bytes 61448 | tf_op jit(solution)/shard_map/ppermute | solution.py:253
  28.3 2.9 %collective-permute-done.8 = bf16[16,640]{1,0:T(8,128)(2,1)S(1)} collective-permute-done((bf16[16,640]{1,0:T(8,128)(2,1)S(1)}, bf16[16,640]{1,0:T(8,128)(2,1)S(1)}, u32[]{:S(2)}, u32[]{:S(2)}) %collective-permute-start.8) | collective-permute-done | bytes 20512 | tf_op jit(solution)/shard_map/ppermute | solution.py:253
  31.1 0.6 %collective-permute-start.9 = (bf16[16,512]{1,0:T(8,128)(2,1)S(1)}, bf16[16,512]{1,0:T(8,128)(2,1)S(1)}, u32[]{:S(2)}, u32[]{:S(2)}) collective-permute-start(bf16[16,512]{1,0:T(8,128)(2,1)S(1)} %add_convert_fusion.refs_0_), channel_id=1, source_target_pairs={{0,2},{1,3},{2,0},{3,1},{4,6},{5,7},{6,4},{7,5},{8,10},{9,11},{10,... | collective-permute-start | bytes 49160 | tf_op jit(solution)/shard_map/ppermute | solution.py:253
  31.8 0.5 collective-permute-start.16
  32.3 2.5 %collective-permute-done.13.refs_7_.refs_6_ = bf16[4,128,256]{2,1,0:T(8,128)(2,1)S(1)} collective-permute-done((bf16[4,128,256]{2,1,0:T(8,128)(2,1)S(1)}, bf16[4,128,256]{2,1,0:T(8,128)(2,1)S(1)}, u32[]{:S(2)}, u32[]{:S(2)}) %collective-permute-start.13) | collective-permute-done | bytes 262176 | tf_op jit(solution)/shard_map/ppermute | solution.py:250
  34.8 0.5 collective-permute-start.12
  35.3 0.5 collective-permute-done.9.refs_1_
  35.9 0.5 collective-permute-done.14.refs_8_.refs_7_
  36.4 0.4 collective-permute-done.12.refs_6_.refs_5_
  36.7 0.8 %shard_map.72 = (bf16[16,512]{1,0:T(8,128)(2,1)S(1)}, bf16[8,1024]{1,0:T(8,128)(2,1)S(1)}) custom-call(bf16[16,512]{1,0:T(8,128)(2,1)S(1)} %add_convert_fusion.refs_0_, bf16[16,512]{1,0:T(8,128)(2,1)S(1)} %collective-permute-done.9.refs_1_, bf16[2,16,128]{2,1,0:T(8,128)(2,1)S(1)} %pad_maximum_fusion.refs_2_, ...), custom_call_target="tpu_custom_call" | custom-call | tf_op jit(solution)/shard_map/pallas_call | solution.py:241
  37.5 2.3 %collective-permute-start.17 = (bf16[16,512]{1,0:T(8,128)(2,1)S(1)}, bf16[16,512]{1,0:T(8,128)(2,1)S(1)}, u32[]{:S(2)}, u32[]{:S(2)}) collective-permute-start(bf16[16,512]{1,0:T(8,128)(2,1)S(1)} %get-tuple-element.23.refs_0_), channel_id=1, source_target_pairs={{0,2},{1,3},{2,0},{3,1},{4,6},{5,7},{6,4},{7,5},{8,10},{9,11},{10,... | collective-permute-start | bytes 49160 | tf_op jit(solution)/shard_map/ppermute | solution.py:253
  39.8 2.5 %collective-permute-done.17.refs_1_ = bf16[16,512]{1,0:T(8,128)(2,1)S(1)} collective-permute-done((bf16[16,512]{1,0:T(8,128)(2,1)S(1)}, bf16[16,512]{1,0:T(8,128)(2,1)S(1)}, u32[]{:S(2)}, u32[]{:S(2)}) %collective-permute-start.17) | collective-permute-done | bytes 16416 | tf_op jit(solution)/shard_map/ppermute | solution.py:253
  42.3 0.8 %shard_map.73 = (bf16[16,512]{1,0:T(8,128)(2,1)S(1)}, bf16[8,256]{1,0:T(8,128)(2,1)S(1)}) custom-call(bf16[16,512]{1,0:T(8,128)(2,1)S(1)} %get-tuple-element.23.refs_0_, bf16[16,512]{1,0:T(8,128)(2,1)S(1)} %collective-permute-done.17.refs_1_, bf16[4,128,256]{2,1,0:T(8,128)(2,1)S(1)} %shard_map.71.refs_3_.refs_2_, ...), custom_call_target="tpu_custom_call" | custom-call | tf_op jit(solution)/shard_map/pallas_call | solution.py:241
  43.1 2.2 %collective-permute-start.18 = (bf16[16,512]{1,0:T(8,128)(2,1)S(1)}, bf16[16,512]{1,0:T(8,128)(2,1)S(1)}, u32[]{:S(2)}, u32[]{:S(2)}) collective-permute-start(bf16[16,512]{1,0:T(8,128)(2,1)S(1)} %get-tuple-element.25.refs_2_), channel_id=1, source_target_pairs={{0,2},{1,3},{2,0},{3,1},{4,6},{5,7},{6,4},{7,5},{8,10},{9,11},{10,... | collective-permute-start | bytes 49160 | tf_op jit(solution)/shard_map/ppermute | solution.py:253
  45.3 2.5 %collective-permute-done.18.refs_3_ = bf16[16,512]{1,0:T(8,128)(2,1)S(1)} collective-permute-done((bf16[16,512]{1,0:T(8,128)(2,1)S(1)}, bf16[16,512]{1,0:T(8,128)(2,1)S(1)}, u32[]{:S(2)}, u32[]{:S(2)}) %collective-permute-start.18) | collective-permute-done | bytes 16416 | tf_op jit(solution)/shard_map/ppermute | solution.py:253
  48.0 12.1 %all_to_all.10.own_ref = bf16[16,16,256]{2,1,0:T(8,128)(2,1)S(1)} all-to-all(bf16[16,16,256]{2,1,0:T(8,128)(2,1)S(1)} %shard_map.74), channel_id=1, replica_groups=mesh['chip'=4,'core'=2,'col'=4] {'chip','col'}, dimensions={0} | all-to-all | bytes 262144 | tf_op jit(solution)/shard_map/all_to_all | solution.py:31
  60.1 1.3 %collective-permute-done.19.other_ref = bf16[16,16,256]{2,1,0:T(8,128)(2,1)S(1)} collective-permute-done((bf16[16,16,256]{2,1,0:T(8,128)(2,1)S(1)}, bf16[16,16,256]{2,1,0:T(8,128)(2,1)S(1)}, u32[]{:S(2)}, u32[]{:S(2)}) %collective-permute-start.19) | collective-permute-done | bytes 131104 | tf_op jit(solution)/shard_map/ppermute | solution.py:250
  61.5 1.1 %shard_map.75 = (f32[64,512]{1,0:T(8,128)}, f32[2,64,256]{2,1,0:T(8,128)}) custom-call(bf16[64,512]{1,0:T(8,128)(2,1)S(1)} %copy-done.2, bf16[2,1024,512]{2,1,0:T(8,128)(2,1)S(1)} %copy-done.1, bf16[16,16,256]{2,1,0:T(8,128)(2,1)S(1)} %all_to_all.10.own_ref, bf16[16,16,256]{2,1,0:T(8,128)(2,1)S(1)} %collective-permute-done.19.other_ref), custom_call_target="tpu_custom_call" | custom-call | tf_op jit(solution)/shard_map/pallas_call | solution.py:322
  (34 shorter events, 1.3 us)
Async XLA Ops:
  0.6 17.2 %copy-start = (f32[2,256,64]{1,2,0:T(8,128)S(1)}, f32[2,256,64]{1,2,0:T(8,128)}, u32[]{:S(2)}) copy-start(f32[2,256,64]{1,2,0:T(8,128)} %param.9) | copy-start | bytes 393220
  2.3 14.4 %copy-start.3 = (bf16[1,128,256]{2,1,0:T(8,128)(2,1)S(1)}, bf16[1,128,256]{2,1,0:T(8,128)(2,1)}, u32[]{:S(2)}) copy-start(bf16[1,128,256]{2,1,0:T(8,128)(2,1)} %get-tuple-element.16.refs_0_.refs_4_) | copy-start | bytes 196612
  2.3 15.5 %copy-start.4 = (bf16[2,128,256]{2,1,0:T(8,128)(2,1)S(1)}, bf16[2,128,256]{2,1,0:T(8,128)(2,1)}, u32[]{:S(2)}) copy-start(bf16[2,128,256]{2,1,0:T(8,128)(2,1)} %get-tuple-element.15.own_ref) | copy-start | bytes 393220
  2.3 10.5 %collective-permute-start = (bf16[2,128,256]{2,1,0:T(8,128)(2,1)}, bf16[2,128,256]{2,1,0:T(8,128)(2,1)S(1)}, u32[]{:S(2)}, u32[]{:S(2)}) collective-permute-start(bf16[2,128,256]{2,1,0:T(8,128)(2,1)} %get-tuple-element.15.own_ref), channel_id=1, source_target_pairs={{0,1},{1,0},{2,3},{3,2},{4,5},{5,4},{6,7},{7,6},{8,9},{9,8},{10,11... | collective-permute-start | bytes 393224 | tf_op jit(solution)/shard_map/ppermute | solution.py:253
  5.3 6.5 %collective-permute-start.3 = (bf16[1,128,256]{2,1,0:T(8,128)(2,1)}, bf16[1,128,256]{2,1,0:T(8,128)(2,1)S(1)}, u32[]{:S(2)}, u32[]{:S(2)}) collective-permute-start(bf16[1,128,256]{2,1,0:T(8,128)(2,1)} %get-tuple-element.16.refs_0_.refs_4_), channel_id=1, source_target_pairs={{0,24},{4,28},{8,16},{12,20},{16,8},{20,12},{24,0},{28,4},{1,25},{... | collective-permute-start | bytes 196616 | tf_op jit(solution)/shard_map/ppermute | solution.py:250
  7.8 4.5 %collective-permute-start.2 = (bf16[1,128,256]{2,1,0:T(8,128)(2,1)}, bf16[1,128,256]{2,1,0:T(8,128)(2,1)S(1)}, u32[]{:S(2)}, u32[]{:S(2)}) collective-permute-start(bf16[1,128,256]{2,1,0:T(8,128)(2,1)} %get-tuple-element.16.refs_0_.refs_4_), channel_id=1, source_target_pairs={{0,16},{4,20},{8,24},{12,28},{16,0},{20,4},{24,8},{28,12},{1,17},{... | collective-permute-start | bytes 196616 | tf_op jit(solution)/shard_map/ppermute | solution.py:250
  8.3 4.5 %collective-permute-start.1 = (bf16[1,128,256]{2,1,0:T(8,128)(2,1)}, bf16[1,128,256]{2,1,0:T(8,128)(2,1)S(1)}, u32[]{:S(2)}, u32[]{:S(2)}) collective-permute-start(bf16[1,128,256]{2,1,0:T(8,128)(2,1)} %get-tuple-element.16.refs_0_.refs_4_), channel_id=1, source_target_pairs={{0,8},{4,12},{8,0},{12,4},{16,24},{20,28},{24,16},{28,20},{1,9},{5... | collective-permute-start | bytes 196616 | tf_op jit(solution)/shard_map/ppermute | solution.py:250
  12.8 14.3 %all-to-all-start = ((bf16[32,16,256]{2,1,0:T(8,128)(2,1)}), bf16[32,16,256]{2,1,0:T(8,128)(2,1)S(1)}, u32[]{:S(2)}, u32[]{:S(2)}) async-start(bf16[32,16,256]{2,1,0:T(8,128)(2,1)} %bitcast.10), calls=%async_computation | async-start | bytes 524288 | tf_op jit(solution)/shard_map/all_to_all | solution.py:31
  16.7 3.9 %collective-permute-start.4 = (bf16[1,128,256]{2,1,0:T(8,128)(2,1)S(1)}, bf16[1,128,256]{2,1,0:T(8,128)(2,1)S(1)}, u32[]{:S(2)}, u32[]{:S(2)}) collective-permute-start(bf16[1,128,256]{2,1,0:T(8,128)(2,1)S(1)} %copy-done.3), channel_id=1, source_target_pairs={{0,4},{4,0},{8,12},{12,8},{16,20},{20,16},{24,28},{28,24},{1,5},{5... | collective-permute-start | bytes 196616 | tf_op jit(solution)/shard_map/ppermute | solution.py:250
  17.0 4.1 %collective-permute-start.7 = (bf16[1,128,256]{2,1,0:T(8,128)(2,1)S(1)}, bf16[1,128,256]{2,1,0:T(8,128)(2,1)S(1)}, u32[]{:S(2)}, u32[]{:S(2)}) collective-permute-start(bf16[1,128,256]{2,1,0:T(8,128)(2,1)S(1)} %collective-permute-done.3.refs_6_.refs_10_), channel_id=1, source_target_pairs={{0,4},{4,0},{8,12},{12,8},{16,20},{20,16},{24,28},{28,24},{1,5},{5... | collective-permute-start | bytes 196616 | tf_op jit(solution)/shard_map/ppermute | solution.py:250
  17.3 4.1 %collective-permute-start.6 = (bf16[1,128,256]{2,1,0:T(8,128)(2,1)S(1)}, bf16[1,128,256]{2,1,0:T(8,128)(2,1)S(1)}, u32[]{:S(2)}, u32[]{:S(2)}) collective-permute-start(bf16[1,128,256]{2,1,0:T(8,128)(2,1)S(1)} %collective-permute-done.2.refs_4_.refs_8_), channel_id=1, source_target_pairs={{0,4},{4,0},{8,12},{12,8},{16,20},{20,16},{24,28},{28,24},{1,5},{5... | collective-permute-start | bytes 196616 | tf_op jit(solution)/shard_map/ppermute | solution.py:250
  17.5 3.9 %collective-permute-start.5 = (bf16[1,128,256]{2,1,0:T(8,128)(2,1)S(1)}, bf16[1,128,256]{2,1,0:T(8,128)(2,1)S(1)}, u32[]{:S(2)}, u32[]{:S(2)}) collective-permute-start(bf16[1,128,256]{2,1,0:T(8,128)(2,1)S(1)} %collective-permute-done.1.refs_2_.refs_6_), channel_id=1, source_target_pairs={{0,4},{4,0},{8,12},{12,8},{16,20},{20,16},{24,28},{28,24},{1,5},{5... | collective-permute-start | bytes 196616 | tf_op jit(solution)/shard_map/ppermute | solution.py:250
  17.8 14.0 %collective-permute-start.15 = (bf16[4,128,256]{2,1,0:T(8,128)(2,1)S(1)}, bf16[4,128,256]{2,1,0:T(8,128)(2,1)S(1)}, u32[]{:S(2)}, u32[]{:S(2)}) collective-permute-start(bf16[4,128,256]{2,1,0:T(8,128)(2,1)S(1)} %shard_map.71.refs_3_.refs_2_), channel_id=1, source_target_pairs={{0,24},{4,28},{8,16},{12,20},{16,8},{20,12},{24,0},{28,4},{1,25},{... | collective-permute-start | bytes 786440 | tf_op jit(solution)/shard_map/ppermute | solution.py:250
  20.6 14.2 %collective-permute-start.13 = (bf16[4,128,256]{2,1,0:T(8,128)(2,1)S(1)}, bf16[4,128,256]{2,1,0:T(8,128)(2,1)S(1)}, u32[]{:S(2)}, u32[]{:S(2)}) collective-permute-start(bf16[4,128,256]{2,1,0:T(8,128)(2,1)S(1)} %shard_map.71.refs_3_.refs_2_), channel_id=1, source_target_pairs={{0,16},{4,20},{8,24},{12,28},{16,0},{20,4},{24,8},{28,12},{1,17},{... | collective-permute-start | bytes 786440 | tf_op jit(solution)/shard_map/ppermute | solution.py:250
  21.1 13.7 %collective-permute-start.11 = (bf16[4,128,256]{2,1,0:T(8,128)(2,1)S(1)}, bf16[4,128,256]{2,1,0:T(8,128)(2,1)S(1)}, u32[]{:S(2)}, u32[]{:S(2)}) collective-permute-start(bf16[4,128,256]{2,1,0:T(8,128)(2,1)S(1)} %shard_map.71.refs_3_.refs_2_), channel_id=1, source_target_pairs={{0,8},{4,12},{8,0},{12,4},{16,24},{20,28},{24,16},{28,20},{1,9},{5... | collective-permute-start | bytes 786440 | tf_op jit(solution)/shard_map/ppermute | solution.py:250
  27.3 3.8 %collective-permute-start.8 = (bf16[16,640]{1,0:T(8,128)(2,1)S(1)}, bf16[16,640]{1,0:T(8,128)(2,1)S(1)}, u32[]{:S(2)}, u32[]{:S(2)}) collective-permute-start(bf16[16,640]{1,0:T(8,128)(2,1)S(1)} %shard_map.70), channel_id=1, source_target_pairs={{0,1},{1,0},{2,3},{3,2},{4,5},{5,4},{6,7},{7,6},{8,9},{9,8},{10,11... | collective-permute-start | bytes 61448 | tf_op jit(solution)/shard_map/ppermute | solution.py:253
  31.1 4.7 %collective-permute-start.9 = (bf16[16,512]{1,0:T(8,128)(2,1)S(1)}, bf16[16,512]{1,0:T(8,128)(2,1)S(1)}, u32[]{:S(2)}, u32[]{:S(2)}) collective-permute-start(bf16[16,512]{1,0:T(8,128)(2,1)S(1)} %add_convert_fusion.refs_0_), channel_id=1, source_target_pairs={{0,2},{1,3},{2,0},{3,1},{4,6},{5,7},{6,4},{7,5},{8,10},{9,11},{10,... | collective-permute-start | bytes 49160 | tf_op jit(solution)/shard_map/ppermute | solution.py:253
  31.8 4.1 %collective-permute-start.10 = (bf16[4,128,256]{2,1,0:T(8,128)(2,1)S(1)}, bf16[4,128,256]{2,1,0:T(8,128)(2,1)S(1)}, u32[]{:S(2)}, u32[]{:S(2)}) collective-permute-start(bf16[4,128,256]{2,1,0:T(8,128)(2,1)S(1)} %shard_map.71.refs_3_.refs_2_), channel_id=1, source_target_pairs={{0,4},{4,0},{8,12},{12,8},{16,20},{20,16},{24,28},{28,24},{1,5},{5... | collective-permute-start | bytes 786440 | tf_op jit(solution)/shard_map/ppermute | solution.py:250
  31.8 4.1 %collective-permute-start.16 = (bf16[4,128,256]{2,1,0:T(8,128)(2,1)S(1)}, bf16[4,128,256]{2,1,0:T(8,128)(2,1)S(1)}, u32[]{:S(2)}, u32[]{:S(2)}) collective-permute-start(bf16[4,128,256]{2,1,0:T(8,128)(2,1)S(1)} %collective-permute-done.15.refs_9_.refs_8_), channel_id=1, source_target_pairs={{0,4},{4,0},{8,12},{12,8},{16,20},{20,16},{24,28},{28,24},{1,5},{5... | collective-permute-start | bytes 786440 | tf_op jit(solution)/shard_map/ppermute | solution.py:250
  34.8 1.5 %collective-permute-start.14 = (bf16[4,128,256]{2,1,0:T(8,128)(2,1)S(1)}, bf16[4,128,256]{2,1,0:T(8,128)(2,1)S(1)}, u32[]{:S(2)}, u32[]{:S(2)}) collective-permute-start(bf16[4,128,256]{2,1,0:T(8,128)(2,1)S(1)} %collective-permute-done.13.refs_7_.refs_6_), channel_id=1, source_target_pairs={{0,4},{4,0},{8,12},{12,8},{16,20},{20,16},{24,28},{28,24},{1,5},{5... | collective-permute-start | bytes 786440 | tf_op jit(solution)/shard_map/ppermute | solution.py:250
  34.8 1.9 %collective-permute-start.12 = (bf16[4,128,256]{2,1,0:T(8,128)(2,1)S(1)}, bf16[4,128,256]{2,1,0:T(8,128)(2,1)S(1)}, u32[]{:S(2)}, u32[]{:S(2)}) collective-permute-start(bf16[4,128,256]{2,1,0:T(8,128)(2,1)S(1)} %collective-permute-done.11.refs_5_.refs_4_), channel_id=1, source_target_pairs={{0,4},{4,0},{8,12},{12,8},{16,20},{20,16},{24,28},{28,24},{1,5},{5... | collective-permute-start | bytes 786440 | tf_op jit(solution)/shard_map/ppermute | solution.py:250
  35.3 26.1 %copy-start.1 = (bf16[2,1024,512]{2,1,0:T(8,128)(2,1)S(1)}, bf16[2,1024,512]{2,1,0:T(8,128)(2,1)}, u32[]{:S(2)}) copy-start(bf16[2,1024,512]{2,1,0:T(8,128)(2,1)} %factor_ref.3) | copy-start | bytes 6291460
  35.3 26.1 %copy-start.2 = (bf16[64,512]{1,0:T(8,128)(2,1)S(1)}, bf16[64,512]{1,0:T(8,128)(2,1)}, u32[]{:S(2)}) copy-start(bf16[64,512]{1,0:T(8,128)(2,1)} %solved_ref.3) | copy-start | bytes 196612
  37.5 4.8 %collective-permute-start.17 = (bf16[16,512]{1,0:T(8,128)(2,1)S(1)}, bf16[16,512]{1,0:T(8,128)(2,1)S(1)}, u32[]{:S(2)}, u32[]{:S(2)}) collective-permute-start(bf16[16,512]{1,0:T(8,128)(2,1)S(1)} %get-tuple-element.23.refs_0_), channel_id=1, source_target_pairs={{0,2},{1,3},{2,0},{3,1},{4,6},{5,7},{6,4},{7,5},{8,10},{9,11},{10,... | collective-permute-start | bytes 49160 | tf_op jit(solution)/shard_map/ppermute | solution.py:253
  43.1 4.7 %collective-permute-start.18 = (bf16[16,512]{1,0:T(8,128)(2,1)S(1)}, bf16[16,512]{1,0:T(8,128)(2,1)S(1)}, u32[]{:S(2)}, u32[]{:S(2)}) collective-permute-start(bf16[16,512]{1,0:T(8,128)(2,1)S(1)} %get-tuple-element.25.refs_2_), channel_id=1, source_target_pairs={{0,2},{1,3},{2,0},{3,1},{4,6},{5,7},{6,4},{7,5},{8,10},{9,11},{10,... | collective-permute-start | bytes 49160 | tf_op jit(solution)/shard_map/ppermute | solution.py:253
  60.1 1.3 %collective-permute-start.19 = (bf16[16,16,256]{2,1,0:T(8,128)(2,1)S(1)}, bf16[16,16,256]{2,1,0:T(8,128)(2,1)S(1)}, u32[]{:S(2)}, u32[]{:S(2)}) collective-permute-start(bf16[16,16,256]{2,1,0:T(8,128)(2,1)S(1)} %all_to_all.10.own_ref), channel_id=1, source_target_pairs={{0,4},{4,0},{8,12},{12,8},{16,20},{20,16},{24,28},{28,24},{1,5},{5... | collective-permute-start | bytes 393224 | tf_op jit(solution)/shard_map/ppermute | solution.py:250

commit v5 on v4

--- a/solution.py
+++ b/solution.py
@@ -91,15 +91,14 @@
     return jnp.concatenate([value[..., :half, :], value[..., half:, :]], axis=-1)
 
 
-def pack_kernel(inv_ref, link_ref, first_ref, pair_ref):
-    first_ref[0] = inv_ref[0]
+def pack_kernel(inv_ref, link_ref, pair_ref):
     pair_ref[0] = inv_ref[1]
     pair_ref[1] = link_ref[...].T
 
 
 def stack_kernel(own_ref, far_ref, both_ref):
-    both_ref[:2] = own_ref[...]
-    both_ref[2:] = far_ref[...]
+    both_ref[0] = own_ref[1]
+    both_ref[1:] = far_ref[...]
 
 
 def panel_kernel(solved_ref, factor_ref, part_ref, solved, factor, sems):
@@ -266,8 +265,9 @@
         order = rows * C
         cut = (2 * group, rows)
 
-        first_own, pair = call(pack_kernel, [inverses, link_tile], [], [(1, size, rows), (2, size, rows)], WIDE)
+        (pair,) = call(pack_kernel, [inverses, link_tile], [], [(2, size, rows)], WIDE)
         held = solved
+        held, *_ = lax.optimization_barrier((held, pair))
         part = pl.pallas_call(
             panel_kernel,
             in_specs=[pl.BlockSpec(memory_space=pl.ANY)] * 2,
@@ -279,22 +279,23 @@
             ],
             compiler_params=WIDE,
         )(held, factor_rows)
-        far = xor_col(pair, 1)
-        first_in = first_own
+        far = xor_col(pair, 2)
+        first_in = inverses
         evens = in_plane(first_in)
         part, *_ = lax.optimization_barrier((part, far, *evens))
         panel = exchange(part.reshape((R * C,) + cut), ROW + ("col",))
         mine = lax.dynamic_slice_in_dim(right_side, lax.axis_index(ROW) * group, group, 2)
         mine = mine.transpose(0, 2, 1).reshape(cut)
 
-        first_tiles = [(tile, 0) for tile in with_mates(evens)]
+        own = with_mates(evens)
+        first_tiles = [(tile, 0) for tile in own]
         own_pair = pair
-        (both,) = call(stack_kernel, [own_pair, far], [], [(4, size, rows)])
+        (both,) = call(stack_kernel, [own_pair, far], [], [(3, size, rows)])
         wide = order // 2
         summed = (2 * group, wide)
         (sent,) = call(first_kernel, [mine, panel], first_tiles, [(2 * group, wide + rows // 2)])
         evens = in_plane(both)
-        arrived = xor_col(sent, 1)
+        arrived = xor_col(sent, 2)
         mates = []
         spare = evens[0]
         spare, *_ = lax.optimization_barrier((spare, arrived))
@@ -309,15 +310,15 @@
         spare, *_ = lax.optimization_barrier((spare, arrived))
         mates.append(xor_row(spare, 1))
         pairs = [block for one in zip(evens, mates) for block in one]
-        last_tiles = [(tile, i) for i in (0, 2) for tile in pairs]
-        links = [(tile, i) for i in (1, 3) for tile in pairs]
+        last_tiles = [(tile, 1) for tile in own] + [(tile, 1) for tile in pairs]
+        links = [(tile, i) for i in (0, 2) for tile in pairs]
         side = jnp.stack([sent[:, wide:], arrived[:, wide:]])
         sent = (sent[:, :wide].astype(F32) + arrived[:, :wide].astype(F32)).astype(BF)
         link = functools.partial(link_kernel, R)
-        sent, first = call_flat(link, [sent, xor_col(sent, 2), side], links + last_tiles, [summed, (group, order)])
+        sent, first = call_flat(link, [sent, xor_col(sent, 1), side], links + last_tiles, [summed, (group, order)])
         turn = functools.partial(turn_kernel, R)
-        sent, short = call_flat(turn, [sent, xor_col(sent, 2)], last_tiles + links, [summed, (group, rows)])
-        (sent,) = call_flat(last_kernel, [first, short, sent, xor_col(sent, 2)], first_tiles, [(R // 2 * C,) + cut])
+        sent, short = call_flat(turn, [sent, xor_col(sent, 1)], last_tiles + links, [summed, (group, rows)])
+        (sent,) = call_flat(last_kernel, [first, short, sent, xor_col(sent, 1)], first_tiles, [(R // 2 * C,) + cut])
         whole = exchange(sent, ("chip", "col"))
         remaining, back = pl.pallas_call(
             functools.partial(closing_kernel, C),

time: 62.9 us -> 62.2 us (0.989)
  starting transfers between devices: 22.2 us -> 21.3 us
    ppermute x5, waiting for transfers between devices: 8.41 us -> 10.1 us  [xor_col(): return lax.ppermute(value, 'col', [(i, i ^ step) for i in range(C)])]
    ppermute x15, waiting for transfers between devices: 5.69 us -> 4.03 us  [xor_row(): return lax.ppermute(value, ROW, [(i, i ^ step) for i in range(R)])]
where the time goes in v5:
time: 62.2 us; the launch traced here: 62 us
  starting transfers between devices  21.3 us (34%)
  waiting for transfers between devices  19.8 us (32%)
  blocking collectives  12.3 us (20%)
  Pallas kernels  7.8 us (13%)
  between operations  0.72 us (1%)
    all_to_all x1, blocking collectives, exchange(): return lax.all_to_all(value, axes, 0, 0, tiled=False)  12.3 us
    ppermute x5, waiting for transfers between devices, xor_col(): return lax.ppermute(value, 'col', [(i, i ^ step) for i in range(C)])  10.1 us
    ppermute x15, starting transfers between devices, xor_row(): return lax.ppermute(value, ROW, [(i, i ^ step) for i in range(R)])  9.15 us
    ppermute x5, starting transfers between devices, xor_col(): return lax.ppermute(value, 'col', [(i, i ^ step) for i in range(C)])  8.81 us
    all_to_all x1, waiting for transfers between devices, exchange(): return lax.all_to_all(value, axes, 0, 0, tiled=False)  5.7 us
    ppermute x15, waiting for transfers between devices, xor_row(): return lax.ppermute(value, ROW, [(i, i ^ step) for i in range(R)])  4.03 us
    all_to_all x1, starting transfers between devices, exchange(): return lax.all_to_all(value, axes, 0, 0, tiled=False)  3.38 us
    pallas_call x1, Pallas kernels, shards(): pl.pallas_call(panel_kernel, in_specs=[pl.BlockSpec(memory_space=pl.ANY)]...  2.96 us
  transfers between devices with their start and end apart: 21, of which 11 were waited for; matrix products, arithmetic and copies ran while one was open for 0% of the time, Pallas kernels for 5%

profile of v5, /device:TPU:0, one launch (start us, length us, event | category | flops | bytes accessed | tf_op | source)
XLA Modules:
  0.0 62.0 jit_solution(1675810000395174432)
XLA Ops:
  0.7 1.7 %shard_map.68.own_ref = bf16[2,128,256]{2,1,0:T(8,128)(2,1)} custom-call(bf16[2,128,256]{2,1,0:T(8,128)(2,1)} %refs_4_.1, bf16[256,128]{1,0:T(8,128)(2,1)} %link_ref.1), custom_call_target="tpu_custom_call" | custom-call | tf_op jit(solution)/shard_map/pallas_call | solution.py:217
  2.4 4.0 %collective-permute-start = (bf16[2,128,256]{2,1,0:T(8,128)(2,1)}, bf16[2,128,256]{2,1,0:T(8,128)(2,1)S(1)}, u32[]{:S(2)}, u32[]{:S(2)}) collective-permute-start(bf16[2,128,256]{2,1,0:T(8,128)(2,1)} %shard_map.68.own_ref), channel_id=1, source_target_pairs={{0,2},{1,3},{2,0},{3,1},{4,6},{5,7},{6,4},{7,5},{8,10},{9,11},{10,... | collective-permute-start | bytes 393224 | tf_op jit(solution)/shard_map/ppermute | solution.py:252
  6.4 2.4 %collective-permute-start.3 = (bf16[2,128,256]{2,1,0:T(8,128)(2,1)}, bf16[2,128,256]{2,1,0:T(8,128)(2,1)S(1)}, u32[]{:S(2)}, u32[]{:S(2)}) collective-permute-start(bf16[2,128,256]{2,1,0:T(8,128)(2,1)} %refs_4_.1), channel_id=1, source_target_pairs={{0,24},{4,28},{8,16},{12,20},{16,8},{20,12},{24,0},{28,4},{1,25},{... | collective-permute-start | bytes 393224 | tf_op jit(solution)/shard_map/ppermute | solution.py:249
  8.8 0.5 collective-permute-start.2
  9.3 0.5 collective-permute-start.1
  9.9 3.0 %shard_map.69 = bf16[8,4,16,256]{3,2,1,0:T(8,128)(2,1)} custom-call(bf16[64,512]{1,0:T(8,128)(2,1)} %solved_ref.2, bf16[2,1024,512]{2,1,0:T(8,128)(2,1)} %factor_ref.3), custom_call_target="tpu_custom_call" | custom-call | tf_op jit(solution)/shard_map/pallas_call | solution.py:271
  13.1 2.2 %collective-permute-done.2.refs_4_.refs_15_.refs_6_.refs_8_ = bf16[2,128,256]{2,1,0:T(8,128)(2,1)S(1)} collective-permute-done((bf16[2,128,256]{2,1,0:T(8,128)(2,1)}, bf16[2,128,256]{2,1,0:T(8,128)(2,1)S(1)}, u32[]{:S(2)}, u32[]{:S(2)}) %collective-permute-start.2) | collective-permute-done | bytes 131104 | tf_op jit(solution)/shard_map/ppermute | solution.py:249
  15.3 3.4 %all-to-all-start = ((bf16[32,16,256]{2,1,0:T(8,128)(2,1)}), bf16[32,16,256]{2,1,0:T(8,128)(2,1)S(1)}, u32[]{:S(2)}, u32[]{:S(2)}) async-start(bf16[32,16,256]{2,1,0:T(8,128)(2,1)} %bitcast.10), calls=%async_computation | async-start | bytes 524288 | tf_op jit(solution)/shard_map/all_to_all | solution.py:31
  18.7 0.3 collective-permute-start.4
  19.0 0.3 collective-permute-start.7
  19.3 0.3 collective-permute-start.6
  19.6 0.3 collective-permute-start.5
  19.8 2.7 %collective-permute-start.15 = (bf16[3,128,256]{2,1,0:T(8,128)(2,1)S(1)}, bf16[3,128,256]{2,1,0:T(8,128)(2,1)S(1)}, u32[]{:S(2)}, u32[]{:S(2)}) collective-permute-start(bf16[3,128,256]{2,1,0:T(8,128)(2,1)S(1)} %shard_map.71.refs_3_.refs_10_), channel_id=1, source_target_pairs={{0,24},{4,28},{8,16},{12,20},{16,8},{20,12},{24,0},{28,4},{1,25},{... | collective-permute-start | bytes 589832 | tf_op jit(solution)/shard_map/ppermute | solution.py:249
  22.6 0.6 collective-permute-start.13
  23.1 0.3 collective-permute-start.11
  23.4 5.7 %all-to-all-done.panel_ref = bf16[32,16,256]{2,1,0:T(8,128)(2,1)S(1)} async-done(((bf16[32,16,256]{2,1,0:T(8,128)(2,1)}), bf16[32,16,256]{2,1,0:T(8,128)(2,1)S(1)}, u32[]{:S(2)}, u32[]{:S(2)}) %all-to-all-start) | async-done | bytes 262176 | tf_op jit(solution)/shard_map/all_to_all | solution.py:31
  29.3 0.6 collective-permute-start.8
  30.0 0.3 collective-permute-done.15.refs_9_.refs_16_
  30.3 3.8 %collective-permute-done.8 = bf16[16,640]{1,0:T(8,128)(2,1)S(1)} collective-permute-done((bf16[16,640]{1,0:T(8,128)(2,1)S(1)}, bf16[16,640]{1,0:T(8,128)(2,1)S(1)}, u32[]{:S(2)}, u32[]{:S(2)}) %collective-permute-start.8) | collective-permute-done | bytes 20512 | tf_op jit(solution)/shard_map/ppermute | solution.py:252
  34.1 1.4 %collective-permute-start.9 = (bf16[16,512]{1,0:T(8,128)(2,1)S(1)}, bf16[16,512]{1,0:T(8,128)(2,1)S(1)}, u32[]{:S(2)}, u32[]{:S(2)}) collective-permute-start(bf16[16,512]{1,0:T(8,128)(2,1)S(1)} %add_convert_fusion.refs_0_), channel_id=1, source_target_pairs={{0,1},{1,0},{2,3},{3,2},{4,5},{5,4},{6,7},{7,6},{8,9},{9,8},{10,11... | collective-permute-start | bytes 49160 | tf_op jit(solution)/shard_map/ppermute | solution.py:252
  35.5 0.5 collective-permute-start.12
  36.0 0.5 collective-permute-start.16
  36.5 1.4 %collective-permute-done.9.refs_1_ = bf16[16,512]{1,0:T(8,128)(2,1)S(1)} collective-permute-done((bf16[16,512]{1,0:T(8,128)(2,1)S(1)}, bf16[16,512]{1,0:T(8,128)(2,1)S(1)}, u32[]{:S(2)}, u32[]{:S(2)}) %collective-permute-start.9) | collective-permute-done | bytes 16416 | tf_op jit(solution)/shard_map/ppermute | solution.py:252
  37.9 0.8 %shard_map.72 = (bf16[16,512]{1,0:T(8,128)(2,1)S(1)}, bf16[8,1024]{1,0:T(8,128)(2,1)S(1)}) custom-call(bf16[16,512]{1,0:T(8,128)(2,1)S(1)} %add_convert_fusion.refs_0_, bf16[16,512]{1,0:T(8,128)(2,1)S(1)} %collective-permute-done.9.refs_1_, bf16[2,16,128]{2,1,0:T(8,128)(2,1)S(1)} %pad_maximum_fusion.refs_2_, ...), custom_call_target="tpu_custom_call" | custom-call | tf_op jit(solution)/shard_map/pallas_call | solution.py:240
  38.7 1.4 %collective-permute-start.17 = (bf16[16,512]{1,0:T(8,128)(2,1)S(1)}, bf16[16,512]{1,0:T(8,128)(2,1)S(1)}, u32[]{:S(2)}, u32[]{:S(2)}) collective-permute-start(bf16[16,512]{1,0:T(8,128)(2,1)S(1)} %get-tuple-element.21.refs_0_), channel_id=1, source_target_pairs={{0,1},{1,0},{2,3},{3,2},{4,5},{5,4},{6,7},{7,6},{8,9},{9,8},{10,11... | collective-permute-start | bytes 49160 | tf_op jit(solution)/shard_map/ppermute | solution.py:252
  40.1 2.4 %collective-permute-done.17.refs_1_ = bf16[16,512]{1,0:T(8,128)(2,1)S(1)} collective-permute-done((bf16[16,512]{1,0:T(8,128)(2,1)S(1)}, bf16[16,512]{1,0:T(8,128)(2,1)S(1)}, u32[]{:S(2)}, u32[]{:S(2)}) %collective-permute-start.17) | collective-permute-done | bytes 16416 | tf_op jit(solution)/shard_map/ppermute | solution.py:252
  42.5 0.8 %shard_map.73 = (bf16[16,512]{1,0:T(8,128)(2,1)S(1)}, bf16[8,256]{1,0:T(8,128)(2,1)S(1)}) custom-call(bf16[16,512]{1,0:T(8,128)(2,1)S(1)} %get-tuple-element.21.refs_0_, bf16[16,512]{1,0:T(8,128)(2,1)S(1)} %collective-permute-done.17.refs_1_, bf16[2,128,256]{2,1,0:T(8,128)(2,1)S(1)} %copy-done.2, ...), custom_call_target="tpu_custom_call" | custom-call | tf_op jit(solution)/shard_map/pallas_call | solution.py:240
  43.3 1.4 %collective-permute-start.18 = (bf16[16,512]{1,0:T(8,128)(2,1)S(1)}, bf16[16,512]{1,0:T(8,128)(2,1)S(1)}, u32[]{:S(2)}, u32[]{:S(2)}) collective-permute-start(bf16[16,512]{1,0:T(8,128)(2,1)S(1)} %get-tuple-element.23.refs_2_), channel_id=1, source_target_pairs={{0,1},{1,0},{2,3},{3,2},{4,5},{5,4},{6,7},{7,6},{8,9},{9,8},{10,11... | collective-permute-start | bytes 49160 | tf_op jit(solution)/shard_map/ppermute | solution.py:252
  44.7 2.4 %collective-permute-done.18.refs_3_ = bf16[16,512]{1,0:T(8,128)(2,1)S(1)} collective-permute-done((bf16[16,512]{1,0:T(8,128)(2,1)S(1)}, bf16[16,512]{1,0:T(8,128)(2,1)S(1)}, u32[]{:S(2)}, u32[]{:S(2)}) %collective-permute-start.18) | collective-permute-done | bytes 16416 | tf_op jit(solution)/shard_map/ppermute | solution.py:252
  47.2 12.3 %all_to_all.10.own_ref = bf16[16,16,256]{2,1,0:T(8,128)(2,1)S(1)} all-to-all(bf16[16,16,256]{2,1,0:T(8,128)(2,1)S(1)} %shard_map.74), channel_id=1, replica_groups=mesh['chip'=4,'core'=2,'col'=4] {'chip','col'}, dimensions={0} | all-to-all | bytes 262144 | tf_op jit(solution)/shard_map/all_to_all | solution.py:31
  59.5 1.3 %collective-permute-done.19.other_ref = bf16[16,16,256]{2,1,0:T(8,128)(2,1)S(1)} collective-permute-done((bf16[16,16,256]{2,1,0:T(8,128)(2,1)S(1)}, bf16[16,16,256]{2,1,0:T(8,128)(2,1)S(1)}, u32[]{:S(2)}, u32[]{:S(2)}) %collective-permute-start.19) | collective-permute-done | bytes 131104 | tf_op jit(solution)/shard_map/ppermute | solution.py:249
  60.9 1.1 %shard_map.75 = (f32[64,512]{1,0:T(8,128)}, f32[2,64,256]{2,1,0:T(8,128)}) custom-call(bf16[64,512]{1,0:T(8,128)(2,1)S(1)} %copy-done.4, bf16[2,1024,512]{2,1,0:T(8,128)(2,1)S(1)} %copy-done.1, bf16[16,16,256]{2,1,0:T(8,128)(2,1)S(1)} %all_to_all.10.own_ref, bf16[16,16,256]{2,1,0:T(8,128)(2,1)S(1)} %collective-permute-done.19.other_ref), custom_call_target="tpu_custom_call" | custom-call | tf_op jit(solution)/shard_map/pallas_call | solution.py:323
  (34 shorter events, 0.8 us)
Async XLA Ops:
  0.6 19.2 %copy-start = (f32[2,256,64]{1,2,0:T(8,128)S(1)}, f32[2,256,64]{1,2,0:T(8,128)}, u32[]{:S(2)}) copy-start(f32[2,256,64]{1,2,0:T(8,128)} %param.9) | copy-start | bytes 393220
  0.6 18.1 %copy-start.2 = (bf16[2,128,256]{2,1,0:T(8,128)(2,1)S(1)}, bf16[2,128,256]{2,1,0:T(8,128)(2,1)}, u32[]{:S(2)}) copy-start(bf16[2,128,256]{2,1,0:T(8,128)(2,1)} %refs_4_.1) | copy-start | bytes 393220
  2.4 17.5 %copy-start.3 = (bf16[2,128,256]{2,1,0:T(8,128)(2,1)S(1)}, bf16[2,128,256]{2,1,0:T(8,128)(2,1)}, u32[]{:S(2)}) copy-start(bf16[2,128,256]{2,1,0:T(8,128)(2,1)} %shard_map.68.own_ref) | copy-start | bytes 393220
  2.4 10.6 %collective-permute-start = (bf16[2,128,256]{2,1,0:T(8,128)(2,1)}, bf16[2,128,256]{2,1,0:T(8,128)(2,1)S(1)}, u32[]{:S(2)}, u32[]{:S(2)}) collective-permute-start(bf16[2,128,256]{2,1,0:T(8,128)(2,1)} %shard_map.68.own_ref), channel_id=1, source_target_pairs={{0,2},{1,3},{2,0},{3,1},{4,6},{5,7},{6,4},{7,5},{8,10},{9,11},{10,... | collective-permute-start | bytes 393224 | tf_op jit(solution)/shard_map/ppermute | solution.py:252
  6.4 6.7 %collective-permute-start.3 = (bf16[2,128,256]{2,1,0:T(8,128)(2,1)}, bf16[2,128,256]{2,1,0:T(8,128)(2,1)S(1)}, u32[]{:S(2)}, u32[]{:S(2)}) collective-permute-start(bf16[2,128,256]{2,1,0:T(8,128)(2,1)} %refs_4_.1), channel_id=1, source_target_pairs={{0,24},{4,28},{8,16},{12,20},{16,8},{20,12},{24,0},{28,4},{1,25},{... | collective-permute-start | bytes 393224 | tf_op jit(solution)/shard_map/ppermute | solution.py:249
  8.8 6.4 %collective-permute-start.2 = (bf16[2,128,256]{2,1,0:T(8,128)(2,1)}, bf16[2,128,256]{2,1,0:T(8,128)(2,1)S(1)}, u32[]{:S(2)}, u32[]{:S(2)}) collective-permute-start(bf16[2,128,256]{2,1,0:T(8,128)(2,1)} %refs_4_.1), channel_id=1, source_target_pairs={{0,16},{4,20},{8,24},{12,28},{16,0},{20,4},{24,8},{28,12},{1,17},{... | collective-permute-start | bytes 393224 | tf_op jit(solution)/shard_map/ppermute | solution.py:249
  9.3 6.0 %collective-permute-start.1 = (bf16[2,128,256]{2,1,0:T(8,128)(2,1)}, bf16[2,128,256]{2,1,0:T(8,128)(2,1)S(1)}, u32[]{:S(2)}, u32[]{:S(2)}) collective-permute-start(bf16[2,128,256]{2,1,0:T(8,128)(2,1)} %refs_4_.1), channel_id=1, source_target_pairs={{0,8},{4,12},{8,0},{12,4},{16,24},{20,28},{24,16},{28,20},{1,9},{5... | collective-permute-start | bytes 393224 | tf_op jit(solution)/shard_map/ppermute | solution.py:249
  15.3 13.8 %all-to-all-start = ((bf16[32,16,256]{2,1,0:T(8,128)(2,1)}), bf16[32,16,256]{2,1,0:T(8,128)(2,1)S(1)}, u32[]{:S(2)}, u32[]{:S(2)}) async-start(bf16[32,16,256]{2,1,0:T(8,128)(2,1)} %bitcast.10), calls=%async_computation | async-start | bytes 524288 | tf_op jit(solution)/shard_map/all_to_all | solution.py:31
  18.7 3.9 %collective-permute-start.4 = (bf16[2,128,256]{2,1,0:T(8,128)(2,1)S(1)}, bf16[2,128,256]{2,1,0:T(8,128)(2,1)S(1)}, u32[]{:S(2)}, u32[]{:S(2)}) collective-permute-start(bf16[2,128,256]{2,1,0:T(8,128)(2,1)S(1)} %copy-done.2), channel_id=1, source_target_pairs={{0,4},{4,0},{8,12},{12,8},{16,20},{20,16},{24,28},{28,24},{1,5},{5... | collective-permute-start | bytes 393224 | tf_op jit(solution)/shard_map/ppermute | solution.py:249
  19.0 4.1 %collective-permute-start.7 = (bf16[2,128,256]{2,1,0:T(8,128)(2,1)S(1)}, bf16[2,128,256]{2,1,0:T(8,128)(2,1)S(1)}, u32[]{:S(2)}, u32[]{:S(2)}) collective-permute-start(bf16[2,128,256]{2,1,0:T(8,128)(2,1)S(1)} %collective-permute-done.3.refs_6_.refs_17_.refs_8_.refs_10_), channel_id=1, source_target_pairs={{0,4},{4,0},{8,12},{12,8},{16,20},{20,16},{24,28},{28,24},{1,5},{5... | collective-permute-start | bytes 393224 | tf_op jit(solution)/shard_map/ppermute | solution.py:249
  19.3 4.1 %collective-permute-start.6 = (bf16[2,128,256]{2,1,0:T(8,128)(2,1)S(1)}, bf16[2,128,256]{2,1,0:T(8,128)(2,1)S(1)}, u32[]{:S(2)}, u32[]{:S(2)}) collective-permute-start(bf16[2,128,256]{2,1,0:T(8,128)(2,1)S(1)} %collective-permute-done.2.refs_4_.refs_15_.refs_6_.refs_8_), channel_id=1, source_target_pairs={{0,4},{4,0},{8,12},{12,8},{16,20},{20,16},{24,28},{28,24},{1,5},{5... | collective-permute-start | bytes 393224 | tf_op jit(solution)/shard_map/ppermute | solution.py:249
  19.6 3.9 %collective-permute-start.5 = (bf16[2,128,256]{2,1,0:T(8,128)(2,1)S(1)}, bf16[2,128,256]{2,1,0:T(8,128)(2,1)S(1)}, u32[]{:S(2)}, u32[]{:S(2)}) collective-permute-start(bf16[2,128,256]{2,1,0:T(8,128)(2,1)S(1)} %collective-permute-done.1.refs_2_.refs_13_.refs_4_.refs_6_), channel_id=1, source_target_pairs={{0,4},{4,0},{8,12},{12,8},{16,20},{20,16},{24,28},{28,24},{1,5},{5... | collective-permute-start | bytes 393224 | tf_op jit(solution)/shard_map/ppermute | solution.py:249
  19.8 10.4 %collective-permute-start.15 = (bf16[3,128,256]{2,1,0:T(8,128)(2,1)S(1)}, bf16[3,128,256]{2,1,0:T(8,128)(2,1)S(1)}, u32[]{:S(2)}, u32[]{:S(2)}) collective-permute-start(bf16[3,128,256]{2,1,0:T(8,128)(2,1)S(1)} %shard_map.71.refs_3_.refs_10_), channel_id=1, source_target_pairs={{0,24},{4,28},{8,16},{12,20},{16,8},{20,12},{24,0},{28,4},{1,25},{... | collective-permute-start | bytes 589832 | tf_op jit(solution)/shard_map/ppermute | solution.py:249
  22.6 11.5 %collective-permute-start.13 = (bf16[3,128,256]{2,1,0:T(8,128)(2,1)S(1)}, bf16[3,128,256]{2,1,0:T(8,128)(2,1)S(1)}, u32[]{:S(2)}, u32[]{:S(2)}) collective-permute-start(bf16[3,128,256]{2,1,0:T(8,128)(2,1)S(1)} %shard_map.71.refs_3_.refs_10_), channel_id=1, source_target_pairs={{0,16},{4,20},{8,24},{12,28},{16,0},{20,4},{24,8},{28,12},{1,17},{... | collective-permute-start | bytes 589832 | tf_op jit(solution)/shard_map/ppermute | solution.py:249
  23.1 10.9 %collective-permute-start.11 = (bf16[3,128,256]{2,1,0:T(8,128)(2,1)S(1)}, bf16[3,128,256]{2,1,0:T(8,128)(2,1)S(1)}, u32[]{:S(2)}, u32[]{:S(2)}) collective-permute-start(bf16[3,128,256]{2,1,0:T(8,128)(2,1)S(1)} %shard_map.71.refs_3_.refs_10_), channel_id=1, source_target_pairs={{0,8},{4,12},{8,0},{12,4},{16,24},{20,28},{24,16},{28,20},{1,9},{5... | collective-permute-start | bytes 589832 | tf_op jit(solution)/shard_map/ppermute | solution.py:249
  29.3 4.7 %collective-permute-start.8 = (bf16[16,640]{1,0:T(8,128)(2,1)S(1)}, bf16[16,640]{1,0:T(8,128)(2,1)S(1)}, u32[]{:S(2)}, u32[]{:S(2)}) collective-permute-start(bf16[16,640]{1,0:T(8,128)(2,1)S(1)} %shard_map.70), channel_id=1, source_target_pairs={{0,2},{1,3},{2,0},{3,1},{4,6},{5,7},{6,4},{7,5},{8,10},{9,11},{10,... | collective-permute-start | bytes 61448 | tf_op jit(solution)/shard_map/ppermute | solution.py:252
  34.1 3.8 %collective-permute-start.9 = (bf16[16,512]{1,0:T(8,128)(2,1)S(1)}, bf16[16,512]{1,0:T(8,128)(2,1)S(1)}, u32[]{:S(2)}, u32[]{:S(2)}) collective-permute-start(bf16[16,512]{1,0:T(8,128)(2,1)S(1)} %add_convert_fusion.refs_0_), channel_id=1, source_target_pairs={{0,1},{1,0},{2,3},{3,2},{4,5},{5,4},{6,7},{7,6},{8,9},{9,8},{10,11... | collective-permute-start | bytes 49160 | tf_op jit(solution)/shard_map/ppermute | solution.py:252
  35.5 2.4 %collective-permute-start.10 = (bf16[3,128,256]{2,1,0:T(8,128)(2,1)S(1)}, bf16[3,128,256]{2,1,0:T(8,128)(2,1)S(1)}, u32[]{:S(2)}, u32[]{:S(2)}) collective-permute-start(bf16[3,128,256]{2,1,0:T(8,128)(2,1)S(1)} %shard_map.71.refs_3_.refs_10_), channel_id=1, source_target_pairs={{0,4},{4,0},{8,12},{12,8},{16,20},{20,16},{24,28},{28,24},{1,5},{5... | collective-permute-start | bytes 589832 | tf_op jit(solution)/shard_map/ppermute | solution.py:249
  35.5 2.4 %collective-permute-start.12 = (bf16[3,128,256]{2,1,0:T(8,128)(2,1)S(1)}, bf16[3,128,256]{2,1,0:T(8,128)(2,1)S(1)}, u32[]{:S(2)}, u32[]{:S(2)}) collective-permute-start(bf16[3,128,256]{2,1,0:T(8,128)(2,1)S(1)} %collective-permute-done.11.refs_5_.refs_12_), channel_id=1, source_target_pairs={{0,4},{4,0},{8,12},{12,8},{16,20},{20,16},{24,28},{28,24},{1,5},{5... | collective-permute-start | bytes 589832 | tf_op jit(solution)/shard_map/ppermute | solution.py:249
  36.0 1.9 %collective-permute-start.14 = (bf16[3,128,256]{2,1,0:T(8,128)(2,1)S(1)}, bf16[3,128,256]{2,1,0:T(8,128)(2,1)S(1)}, u32[]{:S(2)}, u32[]{:S(2)}) collective-permute-start(bf16[3,128,256]{2,1,0:T(8,128)(2,1)S(1)} %collective-permute-done.13.refs_7_.refs_14_), channel_id=1, source_target_pairs={{0,4},{4,0},{8,12},{12,8},{16,20},{20,16},{24,28},{28,24},{1,5},{5... | collective-permute-start | bytes 589832 | tf_op jit(solution)/shard_map/ppermute | solution.py:249
  36.0 1.9 %collective-permute-start.16 = (bf16[3,128,256]{2,1,0:T(8,128)(2,1)S(1)}, bf16[3,128,256]{2,1,0:T(8,128)(2,1)S(1)}, u32[]{:S(2)}, u32[]{:S(2)}) collective-permute-start(bf16[3,128,256]{2,1,0:T(8,128)(2,1)S(1)} %collective-permute-done.15.refs_9_.refs_16_), channel_id=1, source_target_pairs={{0,4},{4,0},{8,12},{12,8},{16,20},{20,16},{24,28},{28,24},{1,5},{5... | collective-permute-start | bytes 589832 | tf_op jit(solution)/shard_map/ppermute | solution.py:249
  38.7 22.2 %copy-start.1 = (bf16[2,1024,512]{2,1,0:T(8,128)(2,1)S(1)}, bf16[2,1024,512]{2,1,0:T(8,128)(2,1)}, u32[]{:S(2)}) copy-start(bf16[2,1024,512]{2,1,0:T(8,128)(2,1)} %factor_ref.3) | copy-start | bytes 6291460
  38.7 22.2 %copy-start.4 = (bf16[64,512]{1,0:T(8,128)(2,1)S(1)}, bf16[64,512]{1,0:T(8,128)(2,1)}, u32[]{:S(2)}) copy-start(bf16[64,512]{1,0:T(8,128)(2,1)} %solved_ref.2) | copy-start | bytes 196612
  38.7 3.8 %collective-permute-start.17 = (bf16[16,512]{1,0:T(8,128)(2,1)S(1)}, bf16[16,512]{1,0:T(8,128)(2,1)S(1)}, u32[]{:S(2)}, u32[]{:S(2)}) collective-permute-start(bf16[16,512]{1,0:T(8,128)(2,1)S(1)} %get-tuple-element.21.refs_0_), channel_id=1, source_target_pairs={{0,1},{1,0},{2,3},{3,2},{4,5},{5,4},{6,7},{7,6},{8,9},{9,8},{10,11... | collective-permute-start | bytes 49160 | tf_op jit(solution)/shard_map/ppermute | solution.py:252
  43.3 3.8 %collective-permute-start.18 = (bf16[16,512]{1,0:T(8,128)(2,1)S(1)}, bf16[16,512]{1,0:T(8,128)(2,1)S(1)}, u32[]{:S(2)}, u32[]{:S(2)}) collective-permute-start(bf16[16,512]{1,0:T(8,128)(2,1)S(1)} %get-tuple-element.23.refs_2_), channel_id=1, source_target_pairs={{0,1},{1,0},{2,3},{3,2},{4,5},{5,4},{6,7},{7,6},{8,9},{9,8},{10,11... | collective-permute-start | bytes 49160 | tf_op jit(solution)/shard_map/ppermute | solution.py:252
  59.5 1.3 %collective-permute-start.19 = (bf16[16,16,256]{2,1,0:T(8,128)(2,1)S(1)}, bf16[16,16,256]{2,1,0:T(8,128)(2,1)S(1)}, u32[]{:S(2)}, u32[]{:S(2)}) collective-permute-start(bf16[16,16,256]{2,1,0:T(8,128)(2,1)S(1)} %all_to_all.10.own_ref), channel_id=1, source_target_pairs={{0,4},{4,0},{8,12},{12,8},{16,20},{20,16},{24,28},{28,24},{1,5},{5... | collective-permute-start | bytes 393224 | tf_op jit(solution)/shard_map/ppermute | solution.py:249

commit v6 on v5

--- a/solution.py
+++ b/solution.py
@@ -143,17 +143,16 @@
     remaining_ref[...] = solved_ref[...].astype(F32) - update
 
 
+def stacked(tiles):
+    return jnp.concatenate([tile[0] for tile in tiles], axis=0)
+
+
 def across(value, tiles):
-    return jnp.concatenate([flipped(value, tile[0]) for tile in tiles], axis=1)
+    return flipped(value, stacked(tiles))
 
 
 def along(value, tiles):
-    size = tiles[0].shape[1]
-    total = None
-    for s, tile in enumerate(tiles):
-        term = plain(value[:, s * size : (s + 1) * size], tile[0])
-        total = term if total is None else total + term
-    return total
+    return plain(value, stacked(tiles))
 
 
 def first_kernel(side_ref, panel_ref, *refs):

time: 62.2 us -> 61.7 us (level)
  no operation moved by 1% of the time
where the time goes in v6:
time: 61.7 us; the launch traced here: 61.5 us
  starting transfers between devices  21.3 us (35%)
  waiting for transfers between devices  19.8 us (32%)
  blocking collectives  12.3 us (20%)
  Pallas kernels  7.32 us (12%)
  between operations  0.72 us (1%)
    all_to_all x1, blocking collectives, exchange(): return lax.all_to_all(value, axes, 0, 0, tiled=False)  12.3 us
    ppermute x5, waiting for transfers between devices, xor_col(): return lax.ppermute(value, 'col', [(i, i ^ step) for i in range(C)])  10.1 us
    ppermute x15, starting transfers between devices, xor_row(): return lax.ppermute(value, ROW, [(i, i ^ step) for i in range(R)])  9.15 us
    ppermute x5, starting transfers between devices, xor_col(): return lax.ppermute(value, 'col', [(i, i ^ step) for i in range(C)])  8.77 us
    all_to_all x1, waiting for transfers between devices, exchange(): return lax.all_to_all(value, axes, 0, 0, tiled=False)  5.7 us
    ppermute x15, waiting for transfers between devices, xor_row(): return lax.ppermute(value, ROW, [(i, i ^ step) for i in range(R)])  4.03 us
    all_to_all x1, starting transfers between devices, exchange(): return lax.all_to_all(value, axes, 0, 0, tiled=False)  3.38 us
    pallas_call x1, Pallas kernels, shards(): pl.pallas_call(panel_kernel, in_specs=[pl.BlockSpec(memory_space=pl.ANY)]...  2.96 us
  transfers between devices with their start and end apart: 21, of which 11 were waited for; matrix products, arithmetic and copies ran while one was open for 0% of the time, Pallas kernels for 5%

profile of v6, /device:TPU:0, one launch (start us, length us, event | category | flops | bytes accessed | tf_op | source)
XLA Modules:
  0.0 61.5 jit_solution(7981594213891856170)
XLA Ops:
  0.7 1.7 %shard_map.68.own_ref = bf16[2,128,256]{2,1,0:T(8,128)(2,1)} custom-call(bf16[2,128,256]{2,1,0:T(8,128)(2,1)} %refs_4_.1, bf16[256,128]{1,0:T(8,128)(2,1)} %link_ref.1), custom_call_target="tpu_custom_call" | custom-call | tf_op jit(solution)/shard_map/pallas_call | solution.py:216
  2.4 4.0 %collective-permute-start = (bf16[2,128,256]{2,1,0:T(8,128)(2,1)}, bf16[2,128,256]{2,1,0:T(8,128)(2,1)S(1)}, u32[]{:S(2)}, u32[]{:S(2)}) collective-permute-start(bf16[2,128,256]{2,1,0:T(8,128)(2,1)} %shard_map.68.own_ref), channel_id=1, source_target_pairs={{0,2},{1,3},{2,0},{3,1},{4,6},{5,7},{6,4},{7,5},{8,10},{9,11},{10,... | collective-permute-start | bytes 393224 | tf_op jit(solution)/shard_map/ppermute | solution.py:251
  6.4 2.4 %collective-permute-start.3 = (bf16[2,128,256]{2,1,0:T(8,128)(2,1)}, bf16[2,128,256]{2,1,0:T(8,128)(2,1)S(1)}, u32[]{:S(2)}, u32[]{:S(2)}) collective-permute-start(bf16[2,128,256]{2,1,0:T(8,128)(2,1)} %refs_4_.1), channel_id=1, source_target_pairs={{0,24},{4,28},{8,16},{12,20},{16,8},{20,12},{24,0},{28,4},{1,25},{... | collective-permute-start | bytes 393224 | tf_op jit(solution)/shard_map/ppermute | solution.py:248
  8.8 0.5 collective-permute-start.2
  9.3 0.5 collective-permute-start.1
  9.9 3.0 %shard_map.69 = bf16[8,4,16,256]{3,2,1,0:T(8,128)(2,1)} custom-call(bf16[64,512]{1,0:T(8,128)(2,1)} %solved_ref.2, bf16[2,1024,512]{2,1,0:T(8,128)(2,1)} %factor_ref.3), custom_call_target="tpu_custom_call" | custom-call | tf_op jit(solution)/shard_map/pallas_call | solution.py:270
  13.1 2.2 %collective-permute-done.2.refs_4_.refs_15_.refs_6_.refs_8_ = bf16[2,128,256]{2,1,0:T(8,128)(2,1)S(1)} collective-permute-done((bf16[2,128,256]{2,1,0:T(8,128)(2,1)}, bf16[2,128,256]{2,1,0:T(8,128)(2,1)S(1)}, u32[]{:S(2)}, u32[]{:S(2)}) %collective-permute-start.2) | collective-permute-done | bytes 131104 | tf_op jit(solution)/shard_map/ppermute | solution.py:248
  15.3 3.4 %all-to-all-start = ((bf16[32,16,256]{2,1,0:T(8,128)(2,1)}), bf16[32,16,256]{2,1,0:T(8,128)(2,1)S(1)}, u32[]{:S(2)}, u32[]{:S(2)}) async-start(bf16[32,16,256]{2,1,0:T(8,128)(2,1)} %bitcast.10), calls=%async_computation | async-start | bytes 524288 | tf_op jit(solution)/shard_map/all_to_all | solution.py:31
  18.7 0.3 collective-permute-start.4
  19.0 0.3 collective-permute-start.7
  19.3 0.3 collective-permute-start.6
  19.6 0.3 collective-permute-start.5
  19.8 2.7 %collective-permute-start.15 = (bf16[3,128,256]{2,1,0:T(8,128)(2,1)S(1)}, bf16[3,128,256]{2,1,0:T(8,128)(2,1)S(1)}, u32[]{:S(2)}, u32[]{:S(2)}) collective-permute-start(bf16[3,128,256]{2,1,0:T(8,128)(2,1)S(1)} %shard_map.71.refs_3_.refs_10_), channel_id=1, source_target_pairs={{0,24},{4,28},{8,16},{12,20},{16,8},{20,12},{24,0},{28,4},{1,25},{... | collective-permute-start | bytes 589832 | tf_op jit(solution)/shard_map/ppermute | solution.py:248
  22.6 0.6 collective-permute-start.13
  23.1 0.3 collective-permute-start.11
  23.4 5.7 %all-to-all-done.panel_ref = bf16[32,16,256]{2,1,0:T(8,128)(2,1)S(1)} async-done(((bf16[32,16,256]{2,1,0:T(8,128)(2,1)}), bf16[32,16,256]{2,1,0:T(8,128)(2,1)S(1)}, u32[]{:S(2)}, u32[]{:S(2)}) %all-to-all-start) | async-done | bytes 262176 | tf_op jit(solution)/shard_map/all_to_all | solution.py:31
  29.3 0.6 %collective-permute-start.8 = (bf16[16,640]{1,0:T(8,128)(2,1)S(1)}, bf16[16,640]{1,0:T(8,128)(2,1)S(1)}, u32[]{:S(2)}, u32[]{:S(2)}) collective-permute-start(bf16[16,640]{1,0:T(8,128)(2,1)S(1)} %shard_map.70), channel_id=1, source_target_pairs={{0,2},{1,3},{2,0},{3,1},{4,6},{5,7},{6,4},{7,5},{8,10},{9,11},{10,... | collective-permute-start | bytes 61448 | tf_op jit(solution)/shard_map/ppermute | solution.py:251
  30.0 0.3 collective-permute-done.15.refs_9_.refs_16_
  30.3 3.8 %collective-permute-done.8 = bf16[16,640]{1,0:T(8,128)(2,1)S(1)} collective-permute-done((bf16[16,640]{1,0:T(8,128)(2,1)S(1)}, bf16[16,640]{1,0:T(8,128)(2,1)S(1)}, u32[]{:S(2)}, u32[]{:S(2)}) %collective-permute-start.8) | collective-permute-done | bytes 20512 | tf_op jit(solution)/shard_map/ppermute | solution.py:251
  34.1 1.4 %collective-permute-start.9 = (bf16[16,512]{1,0:T(8,128)(2,1)S(1)}, bf16[16,512]{1,0:T(8,128)(2,1)S(1)}, u32[]{:S(2)}, u32[]{:S(2)}) collective-permute-start(bf16[16,512]{1,0:T(8,128)(2,1)S(1)} %add_convert_fusion.refs_0_), channel_id=1, source_target_pairs={{0,1},{1,0},{2,3},{3,2},{4,5},{5,4},{6,7},{7,6},{8,9},{9,8},{10,11... | collective-permute-start | bytes 49160 | tf_op jit(solution)/shard_map/ppermute | solution.py:251
  35.5 0.5 collective-permute-start.12
  36.0 0.5 collective-permute-start.16
  36.5 1.4 %collective-permute-done.9.refs_1_ = bf16[16,512]{1,0:T(8,128)(2,1)S(1)} collective-permute-done((bf16[16,512]{1,0:T(8,128)(2,1)S(1)}, bf16[16,512]{1,0:T(8,128)(2,1)S(1)}, u32[]{:S(2)}, u32[]{:S(2)}) %collective-permute-start.9) | collective-permute-done | bytes 16416 | tf_op jit(solution)/shard_map/ppermute | solution.py:251
  37.9 0.6 shard_map.72
  38.5 1.4 %collective-permute-start.17 = (bf16[16,512]{1,0:T(8,128)(2,1)S(1)}, bf16[16,512]{1,0:T(8,128)(2,1)S(1)}, u32[]{:S(2)}, u32[]{:S(2)}) collective-permute-start(bf16[16,512]{1,0:T(8,128)(2,1)S(1)} %get-tuple-element.21.refs_0_), channel_id=1, source_target_pairs={{0,1},{1,0},{2,3},{3,2},{4,5},{5,4},{6,7},{7,6},{8,9},{9,8},{10,11... | collective-permute-start | bytes 49160 | tf_op jit(solution)/shard_map/ppermute | solution.py:251
  39.8 2.4 %collective-permute-done.17.refs_1_ = bf16[16,512]{1,0:T(8,128)(2,1)S(1)} collective-permute-done((bf16[16,512]{1,0:T(8,128)(2,1)S(1)}, bf16[16,512]{1,0:T(8,128)(2,1)S(1)}, u32[]{:S(2)}, u32[]{:S(2)}) %collective-permute-start.17) | collective-permute-done | bytes 16416 | tf_op jit(solution)/shard_map/ppermute | solution.py:251
  42.2 0.6 shard_map.73
  42.8 1.4 %collective-permute-start.18 = (bf16[16,512]{1,0:T(8,128)(2,1)S(1)}, bf16[16,512]{1,0:T(8,128)(2,1)S(1)}, u32[]{:S(2)}, u32[]{:S(2)}) collective-permute-start(bf16[16,512]{1,0:T(8,128)(2,1)S(1)} %get-tuple-element.23.refs_2_), channel_id=1, source_target_pairs={{0,1},{1,0},{2,3},{3,2},{4,5},{5,4},{6,7},{7,6},{8,9},{9,8},{10,11... | collective-permute-start | bytes 49160 | tf_op jit(solution)/shard_map/ppermute | solution.py:251
  44.1 2.4 %collective-permute-done.18.refs_3_ = bf16[16,512]{1,0:T(8,128)(2,1)S(1)} collective-permute-done((bf16[16,512]{1,0:T(8,128)(2,1)S(1)}, bf16[16,512]{1,0:T(8,128)(2,1)S(1)}, u32[]{:S(2)}, u32[]{:S(2)}) %collective-permute-start.18) | collective-permute-done | bytes 16416 | tf_op jit(solution)/shard_map/ppermute | solution.py:251
  46.7 12.3 %all_to_all.10.own_ref = bf16[16,16,256]{2,1,0:T(8,128)(2,1)S(1)} all-to-all(bf16[16,16,256]{2,1,0:T(8,128)(2,1)S(1)} %shard_map.74), channel_id=1, replica_groups=mesh['chip'=4,'core'=2,'col'=4] {'chip','col'}, dimensions={0} | all-to-all | bytes 262144 | tf_op jit(solution)/shard_map/all_to_all | solution.py:31
  59.0 1.3 %collective-permute-done.19.other_ref = bf16[16,16,256]{2,1,0:T(8,128)(2,1)S(1)} collective-permute-done((bf16[16,16,256]{2,1,0:T(8,128)(2,1)S(1)}, bf16[16,16,256]{2,1,0:T(8,128)(2,1)S(1)}, u32[]{:S(2)}, u32[]{:S(2)}) %collective-permute-start.19) | collective-permute-done | bytes 131104 | tf_op jit(solution)/shard_map/ppermute | solution.py:248
  60.3 1.1 %shard_map.75 = (f32[64,512]{1,0:T(8,128)}, f32[2,64,256]{2,1,0:T(8,128)}) custom-call(bf16[64,512]{1,0:T(8,128)(2,1)S(1)} %copy-done.4, bf16[2,1024,512]{2,1,0:T(8,128)(2,1)S(1)} %copy-done.1, bf16[16,16,256]{2,1,0:T(8,128)(2,1)S(1)} %all_to_all.10.own_ref, bf16[16,16,256]{2,1,0:T(8,128)(2,1)S(1)} %collective-permute-done.19.other_ref), custom_call_target="tpu_custom_call" | custom-call | tf_op jit(solution)/shard_map/pallas_call | solution.py:322
  (34 shorter events, 0.8 us)
Async XLA Ops:
  0.6 19.2 %copy-start = (f32[2,256,64]{1,2,0:T(8,128)S(1)}, f32[2,256,64]{1,2,0:T(8,128)}, u32[]{:S(2)}) copy-start(f32[2,256,64]{1,2,0:T(8,128)} %param.9) | copy-start | bytes 393220
  0.6 18.1 %copy-start.2 = (bf16[2,128,256]{2,1,0:T(8,128)(2,1)S(1)}, bf16[2,128,256]{2,1,0:T(8,128)(2,1)}, u32[]{:S(2)}) copy-start(bf16[2,128,256]{2,1,0:T(8,128)(2,1)} %refs_4_.1) | copy-start | bytes 393220
  2.4 17.5 %copy-start.3 = (bf16[2,128,256]{2,1,0:T(8,128)(2,1)S(1)}, bf16[2,128,256]{2,1,0:T(8,128)(2,1)}, u32[]{:S(2)}) copy-start(bf16[2,128,256]{2,1,0:T(8,128)(2,1)} %shard_map.68.own_ref) | copy-start | bytes 393220
  2.4 10.6 %collective-permute-start = (bf16[2,128,256]{2,1,0:T(8,128)(2,1)}, bf16[2,128,256]{2,1,0:T(8,128)(2,1)S(1)}, u32[]{:S(2)}, u32[]{:S(2)}) collective-permute-start(bf16[2,128,256]{2,1,0:T(8,128)(2,1)} %shard_map.68.own_ref), channel_id=1, source_target_pairs={{0,2},{1,3},{2,0},{3,1},{4,6},{5,7},{6,4},{7,5},{8,10},{9,11},{10,... | collective-permute-start | bytes 393224 | tf_op jit(solution)/shard_map/ppermute | solution.py:251
  6.4 6.7 %collective-permute-start.3 = (bf16[2,128,256]{2,1,0:T(8,128)(2,1)}, bf16[2,128,256]{2,1,0:T(8,128)(2,1)S(1)}, u32[]{:S(2)}, u32[]{:S(2)}) collective-permute-start(bf16[2,128,256]{2,1,0:T(8,128)(2,1)} %refs_4_.1), channel_id=1, source_target_pairs={{0,24},{4,28},{8,16},{12,20},{16,8},{20,12},{24,0},{28,4},{1,25},{... | collective-permute-start | bytes 393224 | tf_op jit(solution)/shard_map/ppermute | solution.py:248
  8.8 6.4 %collective-permute-start.2 = (bf16[2,128,256]{2,1,0:T(8,128)(2,1)}, bf16[2,128,256]{2,1,0:T(8,128)(2,1)S(1)}, u32[]{:S(2)}, u32[]{:S(2)}) collective-permute-start(bf16[2,128,256]{2,1,0:T(8,128)(2,1)} %refs_4_.1), channel_id=1, source_target_pairs={{0,16},{4,20},{8,24},{12,28},{16,0},{20,4},{24,8},{28,12},{1,17},{... | collective-permute-start | bytes 393224 | tf_op jit(solution)/shard_map/ppermute | solution.py:248
  9.3 6.0 %collective-permute-start.1 = (bf16[2,128,256]{2,1,0:T(8,128)(2,1)}, bf16[2,128,256]{2,1,0:T(8,128)(2,1)S(1)}, u32[]{:S(2)}, u32[]{:S(2)}) collective-permute-start(bf16[2,128,256]{2,1,0:T(8,128)(2,1)} %refs_4_.1), channel_id=1, source_target_pairs={{0,8},{4,12},{8,0},{12,4},{16,24},{20,28},{24,16},{28,20},{1,9},{5... | collective-permute-start | bytes 393224 | tf_op jit(solution)/shard_map/ppermute | solution.py:248
  15.3 13.8 %all-to-all-start = ((bf16[32,16,256]{2,1,0:T(8,128)(2,1)}), bf16[32,16,256]{2,1,0:T(8,128)(2,1)S(1)}, u32[]{:S(2)}, u32[]{:S(2)}) async-start(bf16[32,16,256]{2,1,0:T(8,128)(2,1)} %bitcast.10), calls=%async_computation | async-start | bytes 524288 | tf_op jit(solution)/shard_map/all_to_all | solution.py:31
  18.7 3.9 %collective-permute-start.4 = (bf16[2,128,256]{2,1,0:T(8,128)(2,1)S(1)}, bf16[2,128,256]{2,1,0:T(8,128)(2,1)S(1)}, u32[]{:S(2)}, u32[]{:S(2)}) collective-permute-start(bf16[2,128,256]{2,1,0:T(8,128)(2,1)S(1)} %copy-done.2), channel_id=1, source_target_pairs={{0,4},{4,0},{8,12},{12,8},{16,20},{20,16},{24,28},{28,24},{1,5},{5... | collective-permute-start | bytes 393224 | tf_op jit(solution)/shard_map/ppermute | solution.py:248
  19.0 4.1 %collective-permute-start.7 = (bf16[2,128,256]{2,1,0:T(8,128)(2,1)S(1)}, bf16[2,128,256]{2,1,0:T(8,128)(2,1)S(1)}, u32[]{:S(2)}, u32[]{:S(2)}) collective-permute-start(bf16[2,128,256]{2,1,0:T(8,128)(2,1)S(1)} %collective-permute-done.3.refs_6_.refs_17_.refs_8_.refs_10_), channel_id=1, source_target_pairs={{0,4},{4,0},{8,12},{12,8},{16,20},{20,16},{24,28},{28,24},{1,5},{5... | collective-permute-start | bytes 393224 | tf_op jit(solution)/shard_map/ppermute | solution.py:248
  19.3 4.1 %collective-permute-start.6 = (bf16[2,128,256]{2,1,0:T(8,128)(2,1)S(1)}, bf16[2,128,256]{2,1,0:T(8,128)(2,1)S(1)}, u32[]{:S(2)}, u32[]{:S(2)}) collective-permute-start(bf16[2,128,256]{2,1,0:T(8,128)(2,1)S(1)} %collective-permute-done.2.refs_4_.refs_15_.refs_6_.refs_8_), channel_id=1, source_target_pairs={{0,4},{4,0},{8,12},{12,8},{16,20},{20,16},{24,28},{28,24},{1,5},{5... | collective-permute-start | bytes 393224 | tf_op jit(solution)/shard_map/ppermute | solution.py:248
  19.6 3.9 %collective-permute-start.5 = (bf16[2,128,256]{2,1,0:T(8,128)(2,1)S(1)}, bf16[2,128,256]{2,1,0:T(8,128)(2,1)S(1)}, u32[]{:S(2)}, u32[]{:S(2)}) collective-permute-start(bf16[2,128,256]{2,1,0:T(8,128)(2,1)S(1)} %collective-permute-done.1.refs_2_.refs_13_.refs_4_.refs_6_), channel_id=1, source_target_pairs={{0,4},{4,0},{8,12},{12,8},{16,20},{20,16},{24,28},{28,24},{1,5},{5... | collective-permute-start | bytes 393224 | tf_op jit(solution)/shard_map/ppermute | solution.py:248
  19.8 10.4 %collective-permute-start.15 = (bf16[3,128,256]{2,1,0:T(8,128)(2,1)S(1)}, bf16[3,128,256]{2,1,0:T(8,128)(2,1)S(1)}, u32[]{:S(2)}, u32[]{:S(2)}) collective-permute-start(bf16[3,128,256]{2,1,0:T(8,128)(2,1)S(1)} %shard_map.71.refs_3_.refs_10_), channel_id=1, source_target_pairs={{0,24},{4,28},{8,16},{12,20},{16,8},{20,12},{24,0},{28,4},{1,25},{... | collective-permute-start | bytes 589832 | tf_op jit(solution)/shard_map/ppermute | solution.py:248
  22.6 11.5 %collective-permute-start.13 = (bf16[3,128,256]{2,1,0:T(8,128)(2,1)S(1)}, bf16[3,128,256]{2,1,0:T(8,128)(2,1)S(1)}, u32[]{:S(2)}, u32[]{:S(2)}) collective-permute-start(bf16[3,128,256]{2,1,0:T(8,128)(2,1)S(1)} %shard_map.71.refs_3_.refs_10_), channel_id=1, source_target_pairs={{0,16},{4,20},{8,24},{12,28},{16,0},{20,4},{24,8},{28,12},{1,17},{... | collective-permute-start | bytes 589832 | tf_op jit(solution)/shard_map/ppermute | solution.py:248
  23.1 10.9 %collective-permute-start.11 = (bf16[3,128,256]{2,1,0:T(8,128)(2,1)S(1)}, bf16[3,128,256]{2,1,0:T(8,128)(2,1)S(1)}, u32[]{:S(2)}, u32[]{:S(2)}) collective-permute-start(bf16[3,128,256]{2,1,0:T(8,128)(2,1)S(1)} %shard_map.71.refs_3_.refs_10_), channel_id=1, source_target_pairs={{0,8},{4,12},{8,0},{12,4},{16,24},{20,28},{24,16},{28,20},{1,9},{5... | collective-permute-start | bytes 589832 | tf_op jit(solution)/shard_map/ppermute | solution.py:248
  29.3 4.7 %collective-permute-start.8 = (bf16[16,640]{1,0:T(8,128)(2,1)S(1)}, bf16[16,640]{1,0:T(8,128)(2,1)S(1)}, u32[]{:S(2)}, u32[]{:S(2)}) collective-permute-start(bf16[16,640]{1,0:T(8,128)(2,1)S(1)} %shard_map.70), channel_id=1, source_target_pairs={{0,2},{1,3},{2,0},{3,1},{4,6},{5,7},{6,4},{7,5},{8,10},{9,11},{10,... | collective-permute-start | bytes 61448 | tf_op jit(solution)/shard_map/ppermute | solution.py:251
  34.1 3.8 %collective-permute-start.9 = (bf16[16,512]{1,0:T(8,128)(2,1)S(1)}, bf16[16,512]{1,0:T(8,128)(2,1)S(1)}, u32[]{:S(2)}, u32[]{:S(2)}) collective-permute-start(bf16[16,512]{1,0:T(8,128)(2,1)S(1)} %add_convert_fusion.refs_0_), channel_id=1, source_target_pairs={{0,1},{1,0},{2,3},{3,2},{4,5},{5,4},{6,7},{7,6},{8,9},{9,8},{10,11... | collective-permute-start | bytes 49160 | tf_op jit(solution)/shard_map/ppermute | solution.py:251
  35.5 2.4 %collective-permute-start.10 = (bf16[3,128,256]{2,1,0:T(8,128)(2,1)S(1)}, bf16[3,128,256]{2,1,0:T(8,128)(2,1)S(1)}, u32[]{:S(2)}, u32[]{:S(2)}) collective-permute-start(bf16[3,128,256]{2,1,0:T(8,128)(2,1)S(1)} %shard_map.71.refs_3_.refs_10_), channel_id=1, source_target_pairs={{0,4},{4,0},{8,12},{12,8},{16,20},{20,16},{24,28},{28,24},{1,5},{5... | collective-permute-start | bytes 589832 | tf_op jit(solution)/shard_map/ppermute | solution.py:248
  35.5 2.4 %collective-permute-start.12 = (bf16[3,128,256]{2,1,0:T(8,128)(2,1)S(1)}, bf16[3,128,256]{2,1,0:T(8,128)(2,1)S(1)}, u32[]{:S(2)}, u32[]{:S(2)}) collective-permute-start(bf16[3,128,256]{2,1,0:T(8,128)(2,1)S(1)} %collective-permute-done.11.refs_5_.refs_12_), channel_id=1, source_target_pairs={{0,4},{4,0},{8,12},{12,8},{16,20},{20,16},{24,28},{28,24},{1,5},{5... | collective-permute-start | bytes 589832 | tf_op jit(solution)/shard_map/ppermute | solution.py:248
  36.0 1.9 %collective-permute-start.14 = (bf16[3,128,256]{2,1,0:T(8,128)(2,1)S(1)}, bf16[3,128,256]{2,1,0:T(8,128)(2,1)S(1)}, u32[]{:S(2)}, u32[]{:S(2)}) collective-permute-start(bf16[3,128,256]{2,1,0:T(8,128)(2,1)S(1)} %collective-permute-done.13.refs_7_.refs_14_), channel_id=1, source_target_pairs={{0,4},{4,0},{8,12},{12,8},{16,20},{20,16},{24,28},{28,24},{1,5},{5... | collective-permute-start | bytes 589832 | tf_op jit(solution)/shard_map/ppermute | solution.py:248
  36.0 1.9 %collective-permute-start.16 = (bf16[3,128,256]{2,1,0:T(8,128)(2,1)S(1)}, bf16[3,128,256]{2,1,0:T(8,128)(2,1)S(1)}, u32[]{:S(2)}, u32[]{:S(2)}) collective-permute-start(bf16[3,128,256]{2,1,0:T(8,128)(2,1)S(1)} %collective-permute-done.15.refs_9_.refs_16_), channel_id=1, source_target_pairs={{0,4},{4,0},{8,12},{12,8},{16,20},{20,16},{24,28},{28,24},{1,5},{5... | collective-permute-start | bytes 589832 | tf_op jit(solution)/shard_map/ppermute | solution.py:248
  38.5 21.9 %copy-start.1 = (bf16[2,1024,512]{2,1,0:T(8,128)(2,1)S(1)}, bf16[2,1024,512]{2,1,0:T(8,128)(2,1)}, u32[]{:S(2)}) copy-start(bf16[2,1024,512]{2,1,0:T(8,128)(2,1)} %factor_ref.3) | copy-start | bytes 6291460
  38.5 21.9 %copy-start.4 = (bf16[64,512]{1,0:T(8,128)(2,1)S(1)}, bf16[64,512]{1,0:T(8,128)(2,1)}, u32[]{:S(2)}) copy-start(bf16[64,512]{1,0:T(8,128)(2,1)} %solved_ref.2) | copy-start | bytes 196612
  38.5 3.8 %collective-permute-start.17 = (bf16[16,512]{1,0:T(8,128)(2,1)S(1)}, bf16[16,512]{1,0:T(8,128)(2,1)S(1)}, u32[]{:S(2)}, u32[]{:S(2)}) collective-permute-start(bf16[16,512]{1,0:T(8,128)(2,1)S(1)} %get-tuple-element.21.refs_0_), channel_id=1, source_target_pairs={{0,1},{1,0},{2,3},{3,2},{4,5},{5,4},{6,7},{7,6},{8,9},{9,8},{10,11... | collective-permute-start | bytes 49160 | tf_op jit(solution)/shard_map/ppermute | solution.py:251
  42.8 3.8 %collective-permute-start.18 = (bf16[16,512]{1,0:T(8,128)(2,1)S(1)}, bf16[16,512]{1,0:T(8,128)(2,1)S(1)}, u32[]{:S(2)}, u32[]{:S(2)}) collective-permute-start(bf16[16,512]{1,0:T(8,128)(2,1)S(1)} %get-tuple-element.23.refs_2_), channel_id=1, source_target_pairs={{0,1},{1,0},{2,3},{3,2},{4,5},{5,4},{6,7},{7,6},{8,9},{9,8},{10,11... | collective-permute-start | bytes 49160 | tf_op jit(solution)/shard_map/ppermute | solution.py:251
  59.0 1.3 %collective-permute-start.19 = (bf16[16,16,256]{2,1,0:T(8,128)(2,1)S(1)}, bf16[16,16,256]{2,1,0:T(8,128)(2,1)S(1)}, u32[]{:S(2)}, u32[]{:S(2)}) collective-permute-start(bf16[16,16,256]{2,1,0:T(8,128)(2,1)S(1)} %all_to_all.10.own_ref), channel_id=1, source_target_pairs={{0,4},{4,0},{8,12},{12,8},{16,20},{20,16},{24,28},{28,24},{1,5},{5... | collective-permute-start | bytes 393224 | tf_op jit(solution)/shard_map/ppermute | solution.py:248

commit v7 on v6

--- a/solution.py
+++ b/solution.py
@@ -279,8 +279,7 @@
             compiler_params=WIDE,
         )(held, factor_rows)
         far = xor_col(pair, 2)
-        first_in = inverses
-        evens = in_plane(first_in)
+        evens = in_plane(inverses)
         part, *_ = lax.optimization_barrier((part, far, *evens))
         panel = exchange(part.reshape((R * C,) + cut), ROW + ("col",))
         mine = lax.dynamic_slice_in_dim(right_side, lax.axis_index(ROW) * group, group, 2)
@@ -288,33 +287,24 @@
 
         own = with_mates(evens)
         first_tiles = [(tile, 0) for tile in own]
-        own_pair = pair
-        (both,) = call(stack_kernel, [own_pair, far], [], [(3, size, rows)])
+        (both,) = call(stack_kernel, [pair, far], [], [(3, size, rows)])
         wide = order // 2
         summed = (2 * group, wide)
         (sent,) = call(first_kernel, [mine, panel], first_tiles, [(2 * group, wide + rows // 2)])
         evens = in_plane(both)
         arrived = xor_col(sent, 2)
+        side = jnp.stack([sent[:, wide:], arrived[:, wide:]])
+        sent = (sent[:, :wide].astype(F32) + arrived[:, :wide].astype(F32)).astype(BF)
+        other = xor_col(sent, 1)
         mates = []
-        spare = evens[0]
-        spare, *_ = lax.optimization_barrier((spare, arrived))
-        mates.append(xor_row(spare, 1))
-        spare = evens[1]
-        spare, *_ = lax.optimization_barrier((spare, arrived))
-        mates.append(xor_row(spare, 1))
-        spare = evens[2]
-        spare, *_ = lax.optimization_barrier((spare, arrived))
-        mates.append(xor_row(spare, 1))
-        spare = evens[3]
-        spare, *_ = lax.optimization_barrier((spare, arrived))
-        mates.append(xor_row(spare, 1))
+        for even in evens:
+            even, _ = lax.optimization_barrier((even, sent))
+            mates.append(xor_row(even, 1))
         pairs = [block for one in zip(evens, mates) for block in one]
         last_tiles = [(tile, 1) for tile in own] + [(tile, 1) for tile in pairs]
         links = [(tile, i) for i in (0, 2) for tile in pairs]
-        side = jnp.stack([sent[:, wide:], arrived[:, wide:]])
-        sent = (sent[:, :wide].astype(F32) + arrived[:, :wide].astype(F32)).astype(BF)
         link = functools.partial(link_kernel, R)
-        sent, first = call_flat(link, [sent, xor_col(sent, 1), side], links + last_tiles, [summed, (group, order)])
+        sent, first = call_flat(link, [sent, other, side], links + last_tiles, [summed, (group, order)])
         turn = functools.partial(turn_kernel, R)
         sent, short = call_flat(turn, [sent, xor_col(sent, 1)], last_tiles + links, [summed, (group, rows)])
         (sent,) = call_flat(last_kernel, [first, short, sent, xor_col(sent, 1)], first_tiles, [(R // 2 * C,) + cut])

time: 61.7 us -> 60.7 us (0.984)
  starting transfers between devices: 21.3 us -> 20.1 us
  waiting for transfers between devices: 19.8 us -> 21 us
  blocking collectives: 12.3 us -> 11.3 us
    ppermute x5, waiting for transfers between devices: 10.1 us -> 11.6 us  [xor_col(): return lax.ppermute(value, 'col', [(i, i ^ step) for i in range(C)])]
    ppermute x5, starting transfers between devices: 8.77 us -> 7.54 us  [xor_col(): return lax.ppermute(value, 'col', [(i, i ^ step) for i in range(C)])]
    all_to_all x1, blocking collectives: 12.3 us -> 11.3 us  [exchange(): return lax.all_to_all(value, axes, 0, 0, tiled=False)]
  transfers between devices with their start and end apart: 21 -> 21, of which waited for: 11 -> 10; matrix products, arithmetic and copies ran while one was open for 0% -> 0% of each run, Pallas kernels for 5% -> 5%
where the time goes in v7:
time: 60.7 us; the launch traced here: 60.5 us
  waiting for transfers between devices  21 us (35%)
  starting transfers between devices  20.1 us (33%)
  blocking collectives  11.3 us (19%)
  Pallas kernels  7.32 us (12%)
  between operations  0.73 us (1%)
    ppermute x5, waiting for transfers between devices, xor_col(): return lax.ppermute(value, 'col', [(i, i ^ step) for i in range(C)])  11.6 us
    all_to_all x1, blocking collectives, exchange(): return lax.all_to_all(value, axes, 0, 0, tiled=False)  11.3 us
    ppermute x15, starting transfers between devices, xor_row(): return lax.ppermute(value, ROW, [(i, i ^ step) for i in range(R)])  9.21 us
    ppermute x5, starting transfers between devices, xor_col(): return lax.ppermute(value, 'col', [(i, i ^ step) for i in range(C)])  7.54 us
    all_to_all x1, waiting for transfers between devices, exchange(): return lax.all_to_all(value, axes, 0, 0, tiled=False)  5.7 us
    ppermute x15, waiting for transfers between devices, xor_row(): return lax.ppermute(value, ROW, [(i, i ^ step) for i in range(R)])  3.73 us
    all_to_all x1, starting transfers between devices, exchange(): return lax.all_to_all(value, axes, 0, 0, tiled=False)  3.38 us
    pallas_call x1, Pallas kernels, shards(): pl.pallas_call(panel_kernel, in_specs=[pl.BlockSpec(memory_space=pl.ANY)]...  2.96 us
  transfers between devices with their start and end apart: 21, of which 10 were waited for; matrix products, arithmetic and copies ran while one was open for 0% of the time, Pallas kernels for 5%

profile of v7, /device:TPU:0, one launch (start us, length us, event | category | flops | bytes accessed | tf_op | source)
XLA Modules:
  0.0 60.5 jit_solution(7927797370548726741)
XLA Ops:
  0.7 1.7 %shard_map.68.own_ref = bf16[2,128,256]{2,1,0:T(8,128)(2,1)} custom-call(bf16[2,128,256]{2,1,0:T(8,128)(2,1)} %refs_4_.1, bf16[256,128]{1,0:T(8,128)(2,1)} %link_ref.1), custom_call_target="tpu_custom_call" | custom-call | tf_op jit(solution)/shard_map/pallas_call | solution.py:216
  2.4 4.0 %collective-permute-start = (bf16[2,128,256]{2,1,0:T(8,128)(2,1)}, bf16[2,128,256]{2,1,0:T(8,128)(2,1)S(1)}, u32[]{:S(2)}, u32[]{:S(2)}) collective-permute-start(bf16[2,128,256]{2,1,0:T(8,128)(2,1)} %shard_map.68.own_ref), channel_id=1, source_target_pairs={{0,2},{1,3},{2,0},{3,1},{4,6},{5,7},{6,4},{7,5},{8,10},{9,11},{10,... | collective-permute-start | bytes 393224 | tf_op jit(solution)/shard_map/ppermute | solution.py:251
  6.4 2.4 %collective-permute-start.3 = (bf16[2,128,256]{2,1,0:T(8,128)(2,1)}, bf16[2,128,256]{2,1,0:T(8,128)(2,1)S(1)}, u32[]{:S(2)}, u32[]{:S(2)}) collective-permute-start(bf16[2,128,256]{2,1,0:T(8,128)(2,1)} %refs_4_.1), channel_id=1, source_target_pairs={{0,24},{4,28},{8,16},{12,20},{16,8},{20,12},{24,0},{28,4},{1,25},{... | collective-permute-start | bytes 393224 | tf_op jit(solution)/shard_map/ppermute | solution.py:248
  8.8 0.5 collective-permute-start.2
  9.3 0.5 collective-permute-start.1
  9.9 3.0 %shard_map.69 = bf16[8,4,16,256]{3,2,1,0:T(8,128)(2,1)} custom-call(bf16[64,512]{1,0:T(8,128)(2,1)} %solved_ref.2, bf16[2,1024,512]{2,1,0:T(8,128)(2,1)} %factor_ref.3), custom_call_target="tpu_custom_call" | custom-call | tf_op jit(solution)/shard_map/pallas_call | solution.py:270
  13.1 2.2 %collective-permute-done.2.refs_4_.refs_15_.refs_6_.refs_8_ = bf16[2,128,256]{2,1,0:T(8,128)(2,1)S(1)} collective-permute-done((bf16[2,128,256]{2,1,0:T(8,128)(2,1)}, bf16[2,128,256]{2,1,0:T(8,128)(2,1)S(1)}, u32[]{:S(2)}, u32[]{:S(2)}) %collective-permute-start.2) | collective-permute-done | bytes 131104 | tf_op jit(solution)/shard_map/ppermute | solution.py:248
  15.3 3.4 %all-to-all-start = ((bf16[32,16,256]{2,1,0:T(8,128)(2,1)}), bf16[32,16,256]{2,1,0:T(8,128)(2,1)S(1)}, u32[]{:S(2)}, u32[]{:S(2)}) async-start(bf16[32,16,256]{2,1,0:T(8,128)(2,1)} %bitcast.10), calls=%async_computation | async-start | bytes 524288 | tf_op jit(solution)/shard_map/all_to_all | solution.py:31
  18.7 0.3 collective-permute-start.4
  19.0 0.3 collective-permute-start.7
  19.3 0.3 collective-permute-start.6
  19.6 0.3 collective-permute-start.5
  19.8 2.7 %collective-permute-start.15 = (bf16[3,128,256]{2,1,0:T(8,128)(2,1)S(1)}, bf16[3,128,256]{2,1,0:T(8,128)(2,1)S(1)}, u32[]{:S(2)}, u32[]{:S(2)}) collective-permute-start(bf16[3,128,256]{2,1,0:T(8,128)(2,1)S(1)} %shard_map.71.refs_3_.refs_10_), channel_id=1, source_target_pairs={{0,24},{4,28},{8,16},{12,20},{16,8},{20,12},{24,0},{28,4},{1,25},{... | collective-permute-start | bytes 589832 | tf_op jit(solution)/shard_map/ppermute | solution.py:248
  22.6 0.6 collective-permute-start.13
  23.1 0.3 collective-permute-start.11
  23.4 5.7 %all-to-all-done.panel_ref = bf16[32,16,256]{2,1,0:T(8,128)(2,1)S(1)} async-done(((bf16[32,16,256]{2,1,0:T(8,128)(2,1)}), bf16[32,16,256]{2,1,0:T(8,128)(2,1)S(1)}, u32[]{:S(2)}, u32[]{:S(2)}) %all-to-all-start) | async-done | bytes 262176 | tf_op jit(solution)/shard_map/all_to_all | solution.py:31
  29.1 0.2 shard_map.70
  29.3 0.6 %collective-permute-start.8 = (bf16[16,640]{1,0:T(8,128)(2,1)S(1)}, bf16[16,640]{1,0:T(8,128)(2,1)S(1)}, u32[]{:S(2)}, u32[]{:S(2)}) collective-permute-start(bf16[16,640]{1,0:T(8,128)(2,1)S(1)} %shard_map.70), channel_id=1, source_target_pairs={{0,2},{1,3},{2,0},{3,1},{4,6},{5,7},{6,4},{7,5},{8,10},{9,11},{10,... | collective-permute-start | bytes 61448 | tf_op jit(solution)/shard_map/ppermute | solution.py:251
  30.0 4.1 %collective-permute-done.8 = bf16[16,640]{1,0:T(8,128)(2,1)S(1)} collective-permute-done((bf16[16,640]{1,0:T(8,128)(2,1)S(1)}, bf16[16,640]{1,0:T(8,128)(2,1)S(1)}, u32[]{:S(2)}, u32[]{:S(2)}) %collective-permute-start.8) | collective-permute-done | bytes 20512 | tf_op jit(solution)/shard_map/ppermute | solution.py:251
  34.1 1.0 %collective-permute-start.9 = (bf16[16,512]{1,0:T(8,128)(2,1)S(1)}, bf16[16,512]{1,0:T(8,128)(2,1)S(1)}, u32[]{:S(2)}, u32[]{:S(2)}) collective-permute-start(bf16[16,512]{1,0:T(8,128)(2,1)S(1)} %add_convert_fusion.refs_0_), channel_id=1, source_target_pairs={{0,1},{1,0},{2,3},{3,2},{4,5},{5,4},{6,7},{7,6},{8,9},{9,8},{10,11... | collective-permute-start | bytes 49160 | tf_op jit(solution)/shard_map/ppermute | solution.py:251
  35.1 0.5 collective-permute-start.12
  35.7 0.4 collective-permute-start.16
  36.2 1.7 %collective-permute-done.9.refs_1_ = bf16[16,512]{1,0:T(8,128)(2,1)S(1)} collective-permute-done((bf16[16,512]{1,0:T(8,128)(2,1)S(1)}, bf16[16,512]{1,0:T(8,128)(2,1)S(1)}, u32[]{:S(2)}, u32[]{:S(2)}) %collective-permute-start.9) | collective-permute-done | bytes 16416 | tf_op jit(solution)/shard_map/ppermute | solution.py:251
  37.9 0.6 shard_map.72
  38.5 0.9 %collective-permute-start.17 = (bf16[16,512]{1,0:T(8,128)(2,1)S(1)}, bf16[16,512]{1,0:T(8,128)(2,1)S(1)}, u32[]{:S(2)}, u32[]{:S(2)}) collective-permute-start(bf16[16,512]{1,0:T(8,128)(2,1)S(1)} %get-tuple-element.21.refs_0_), channel_id=1, source_target_pairs={{0,1},{1,0},{2,3},{3,2},{4,5},{5,4},{6,7},{7,6},{8,9},{9,8},{10,11... | collective-permute-start | bytes 49160 | tf_op jit(solution)/shard_map/ppermute | solution.py:251
  39.4 2.8 %collective-permute-done.17.refs_1_ = bf16[16,512]{1,0:T(8,128)(2,1)S(1)} collective-permute-done((bf16[16,512]{1,0:T(8,128)(2,1)S(1)}, bf16[16,512]{1,0:T(8,128)(2,1)S(1)}, u32[]{:S(2)}, u32[]{:S(2)}) %collective-permute-start.17) | collective-permute-done | bytes 16416 | tf_op jit(solution)/shard_map/ppermute | solution.py:251
  42.2 0.6 shard_map.73
  42.8 0.9 %collective-permute-start.18 = (bf16[16,512]{1,0:T(8,128)(2,1)S(1)}, bf16[16,512]{1,0:T(8,128)(2,1)S(1)}, u32[]{:S(2)}, u32[]{:S(2)}) collective-permute-start(bf16[16,512]{1,0:T(8,128)(2,1)S(1)} %get-tuple-element.23.refs_2_), channel_id=1, source_target_pairs={{0,1},{1,0},{2,3},{3,2},{4,5},{5,4},{6,7},{7,6},{8,9},{9,8},{10,11... | collective-permute-start | bytes 49160 | tf_op jit(solution)/shard_map/ppermute | solution.py:251
  43.7 2.8 %collective-permute-done.18.refs_3_ = bf16[16,512]{1,0:T(8,128)(2,1)S(1)} collective-permute-done((bf16[16,512]{1,0:T(8,128)(2,1)S(1)}, bf16[16,512]{1,0:T(8,128)(2,1)S(1)}, u32[]{:S(2)}, u32[]{:S(2)}) %collective-permute-start.18) | collective-permute-done | bytes 16416 | tf_op jit(solution)/shard_map/ppermute | solution.py:251
  46.7 11.3 %all_to_all.10.own_ref = bf16[16,16,256]{2,1,0:T(8,128)(2,1)S(1)} all-to-all(bf16[16,16,256]{2,1,0:T(8,128)(2,1)S(1)} %shard_map.74), channel_id=1, replica_groups=mesh['chip'=4,'core'=2,'col'=4] {'chip','col'}, dimensions={0} | all-to-all | bytes 262144 | tf_op jit(solution)/shard_map/all_to_all | solution.py:31
  58.0 1.3 %collective-permute-done.19.other_ref = bf16[16,16,256]{2,1,0:T(8,128)(2,1)S(1)} collective-permute-done((bf16[16,16,256]{2,1,0:T(8,128)(2,1)S(1)}, bf16[16,16,256]{2,1,0:T(8,128)(2,1)S(1)}, u32[]{:S(2)}, u32[]{:S(2)}) %collective-permute-start.19) | collective-permute-done | bytes 131104 | tf_op jit(solution)/shard_map/ppermute | solution.py:248
  59.3 1.1 %shard_map.75 = (f32[64,512]{1,0:T(8,128)}, f32[2,64,256]{2,1,0:T(8,128)}) custom-call(bf16[64,512]{1,0:T(8,128)(2,1)S(1)} %copy-done.4, bf16[2,1024,512]{2,1,0:T(8,128)(2,1)S(1)} %copy-done.1, bf16[16,16,256]{2,1,0:T(8,128)(2,1)S(1)} %all_to_all.10.own_ref, bf16[16,16,256]{2,1,0:T(8,128)(2,1)S(1)} %collective-permute-done.19.other_ref), custom_call_target="tpu_custom_call" | custom-call | tf_op jit(solution)/shard_map/pallas_call | solution.py:312
  (34 shorter events, 0.7 us)
Async XLA Ops:
  0.6 19.2 %copy-start = (f32[2,256,64]{1,2,0:T(8,128)S(1)}, f32[2,256,64]{1,2,0:T(8,128)}, u32[]{:S(2)}) copy-start(f32[2,256,64]{1,2,0:T(8,128)} %param.9) | copy-start | bytes 393220
  0.6 18.1 %copy-start.2 = (bf16[2,128,256]{2,1,0:T(8,128)(2,1)S(1)}, bf16[2,128,256]{2,1,0:T(8,128)(2,1)}, u32[]{:S(2)}) copy-start(bf16[2,128,256]{2,1,0:T(8,128)(2,1)} %refs_4_.1) | copy-start | bytes 393220
  2.4 17.5 %copy-start.3 = (bf16[2,128,256]{2,1,0:T(8,128)(2,1)S(1)}, bf16[2,128,256]{2,1,0:T(8,128)(2,1)}, u32[]{:S(2)}) copy-start(bf16[2,128,256]{2,1,0:T(8,128)(2,1)} %shard_map.68.own_ref) | copy-start | bytes 393220
  2.4 10.6 %collective-permute-start = (bf16[2,128,256]{2,1,0:T(8,128)(2,1)}, bf16[2,128,256]{2,1,0:T(8,128)(2,1)S(1)}, u32[]{:S(2)}, u32[]{:S(2)}) collective-permute-start(bf16[2,128,256]{2,1,0:T(8,128)(2,1)} %shard_map.68.own_ref), channel_id=1, source_target_pairs={{0,2},{1,3},{2,0},{3,1},{4,6},{5,7},{6,4},{7,5},{8,10},{9,11},{10,... | collective-permute-start | bytes 393224 | tf_op jit(solution)/shard_map/ppermute | solution.py:251
  6.4 6.7 %collective-permute-start.3 = (bf16[2,128,256]{2,1,0:T(8,128)(2,1)}, bf16[2,128,256]{2,1,0:T(8,128)(2,1)S(1)}, u32[]{:S(2)}, u32[]{:S(2)}) collective-permute-start(bf16[2,128,256]{2,1,0:T(8,128)(2,1)} %refs_4_.1), channel_id=1, source_target_pairs={{0,24},{4,28},{8,16},{12,20},{16,8},{20,12},{24,0},{28,4},{1,25},{... | collective-permute-start | bytes 393224 | tf_op jit(solution)/shard_map/ppermute | solution.py:248
  8.8 6.4 %collective-permute-start.2 = (bf16[2,128,256]{2,1,0:T(8,128)(2,1)}, bf16[2,128,256]{2,1,0:T(8,128)(2,1)S(1)}, u32[]{:S(2)}, u32[]{:S(2)}) collective-permute-start(bf16[2,128,256]{2,1,0:T(8,128)(2,1)} %refs_4_.1), channel_id=1, source_target_pairs={{0,16},{4,20},{8,24},{12,28},{16,0},{20,4},{24,8},{28,12},{1,17},{... | collective-permute-start | bytes 393224 | tf_op jit(solution)/shard_map/ppermute | solution.py:248
  9.3 6.0 %collective-permute-start.1 = (bf16[2,128,256]{2,1,0:T(8,128)(2,1)}, bf16[2,128,256]{2,1,0:T(8,128)(2,1)S(1)}, u32[]{:S(2)}, u32[]{:S(2)}) collective-permute-start(bf16[2,128,256]{2,1,0:T(8,128)(2,1)} %refs_4_.1), channel_id=1, source_target_pairs={{0,8},{4,12},{8,0},{12,4},{16,24},{20,28},{24,16},{28,20},{1,9},{5... | collective-permute-start | bytes 393224 | tf_op jit(solution)/shard_map/ppermute | solution.py:248
  15.3 13.8 %all-to-all-start = ((bf16[32,16,256]{2,1,0:T(8,128)(2,1)}), bf16[32,16,256]{2,1,0:T(8,128)(2,1)S(1)}, u32[]{:S(2)}, u32[]{:S(2)}) async-start(bf16[32,16,256]{2,1,0:T(8,128)(2,1)} %bitcast.10), calls=%async_computation | async-start | bytes 524288 | tf_op jit(solution)/shard_map/all_to_all | solution.py:31
  18.7 3.9 %collective-permute-start.4 = (bf16[2,128,256]{2,1,0:T(8,128)(2,1)S(1)}, bf16[2,128,256]{2,1,0:T(8,128)(2,1)S(1)}, u32[]{:S(2)}, u32[]{:S(2)}) collective-permute-start(bf16[2,128,256]{2,1,0:T(8,128)(2,1)S(1)} %copy-done.2), channel_id=1, source_target_pairs={{0,4},{4,0},{8,12},{12,8},{16,20},{20,16},{24,28},{28,24},{1,5},{5... | collective-permute-start | bytes 393224 | tf_op jit(solution)/shard_map/ppermute | solution.py:248
  19.0 4.1 %collective-permute-start.7 = (bf16[2,128,256]{2,1,0:T(8,128)(2,1)S(1)}, bf16[2,128,256]{2,1,0:T(8,128)(2,1)S(1)}, u32[]{:S(2)}, u32[]{:S(2)}) collective-permute-start(bf16[2,128,256]{2,1,0:T(8,128)(2,1)S(1)} %collective-permute-done.3.refs_6_.refs_17_.refs_8_.refs_10_), channel_id=1, source_target_pairs={{0,4},{4,0},{8,12},{12,8},{16,20},{20,16},{24,28},{28,24},{1,5},{5... | collective-permute-start | bytes 393224 | tf_op jit(solution)/shard_map/ppermute | solution.py:248
  19.3 4.1 %collective-permute-start.6 = (bf16[2,128,256]{2,1,0:T(8,128)(2,1)S(1)}, bf16[2,128,256]{2,1,0:T(8,128)(2,1)S(1)}, u32[]{:S(2)}, u32[]{:S(2)}) collective-permute-start(bf16[2,128,256]{2,1,0:T(8,128)(2,1)S(1)} %collective-permute-done.2.refs_4_.refs_15_.refs_6_.refs_8_), channel_id=1, source_target_pairs={{0,4},{4,0},{8,12},{12,8},{16,20},{20,16},{24,28},{28,24},{1,5},{5... | collective-permute-start | bytes 393224 | tf_op jit(solution)/shard_map/ppermute | solution.py:248
  19.6 3.9 %collective-permute-start.5 = (bf16[2,128,256]{2,1,0:T(8,128)(2,1)S(1)}, bf16[2,128,256]{2,1,0:T(8,128)(2,1)S(1)}, u32[]{:S(2)}, u32[]{:S(2)}) collective-permute-start(bf16[2,128,256]{2,1,0:T(8,128)(2,1)S(1)} %collective-permute-done.1.refs_2_.refs_13_.refs_4_.refs_6_), channel_id=1, source_target_pairs={{0,4},{4,0},{8,12},{12,8},{16,20},{20,16},{24,28},{28,24},{1,5},{5... | collective-permute-start | bytes 393224 | tf_op jit(solution)/shard_map/ppermute | solution.py:248
  19.8 15.2 %collective-permute-start.15 = (bf16[3,128,256]{2,1,0:T(8,128)(2,1)S(1)}, bf16[3,128,256]{2,1,0:T(8,128)(2,1)S(1)}, u32[]{:S(2)}, u32[]{:S(2)}) collective-permute-start(bf16[3,128,256]{2,1,0:T(8,128)(2,1)S(1)} %shard_map.71.refs_3_.refs_10_), channel_id=1, source_target_pairs={{0,24},{4,28},{8,16},{12,20},{16,8},{20,12},{24,0},{28,4},{1,25},{... | collective-permute-start | bytes 589832 | tf_op jit(solution)/shard_map/ppermute | solution.py:248
  22.6 12.5 %collective-permute-start.13 = (bf16[3,128,256]{2,1,0:T(8,128)(2,1)S(1)}, bf16[3,128,256]{2,1,0:T(8,128)(2,1)S(1)}, u32[]{:S(2)}, u32[]{:S(2)}) collective-permute-start(bf16[3,128,256]{2,1,0:T(8,128)(2,1)S(1)} %shard_map.71.refs_3_.refs_10_), channel_id=1, source_target_pairs={{0,16},{4,20},{8,24},{12,28},{16,0},{20,4},{24,8},{28,12},{1,17},{... | collective-permute-start | bytes 589832 | tf_op jit(solution)/shard_map/ppermute | solution.py:248
  23.1 11.9 %collective-permute-start.11 = (bf16[3,128,256]{2,1,0:T(8,128)(2,1)S(1)}, bf16[3,128,256]{2,1,0:T(8,128)(2,1)S(1)}, u32[]{:S(2)}, u32[]{:S(2)}) collective-permute-start(bf16[3,128,256]{2,1,0:T(8,128)(2,1)S(1)} %shard_map.71.refs_3_.refs_10_), channel_id=1, source_target_pairs={{0,8},{4,12},{8,0},{12,4},{16,24},{20,28},{24,16},{28,20},{1,9},{5... | collective-permute-start | bytes 589832 | tf_op jit(solution)/shard_map/ppermute | solution.py:248
  29.3 4.7 %collective-permute-start.8 = (bf16[16,640]{1,0:T(8,128)(2,1)S(1)}, bf16[16,640]{1,0:T(8,128)(2,1)S(1)}, u32[]{:S(2)}, u32[]{:S(2)}) collective-permute-start(bf16[16,640]{1,0:T(8,128)(2,1)S(1)} %shard_map.70), channel_id=1, source_target_pairs={{0,2},{1,3},{2,0},{3,1},{4,6},{5,7},{6,4},{7,5},{8,10},{9,11},{10,... | collective-permute-start | bytes 61448 | tf_op jit(solution)/shard_map/ppermute | solution.py:251
  34.1 3.8 %collective-permute-start.9 = (bf16[16,512]{1,0:T(8,128)(2,1)S(1)}, bf16[16,512]{1,0:T(8,128)(2,1)S(1)}, u32[]{:S(2)}, u32[]{:S(2)}) collective-permute-start(bf16[16,512]{1,0:T(8,128)(2,1)S(1)} %add_convert_fusion.refs_0_), channel_id=1, source_target_pairs={{0,1},{1,0},{2,3},{3,2},{4,5},{5,4},{6,7},{7,6},{8,9},{9,8},{10,11... | collective-permute-start | bytes 49160 | tf_op jit(solution)/shard_map/ppermute | solution.py:251
  35.1 2.8 %collective-permute-start.10 = (bf16[3,128,256]{2,1,0:T(8,128)(2,1)S(1)}, bf16[3,128,256]{2,1,0:T(8,128)(2,1)S(1)}, u32[]{:S(2)}, u32[]{:S(2)}) collective-permute-start(bf16[3,128,256]{2,1,0:T(8,128)(2,1)S(1)} %shard_map.71.refs_3_.refs_10_), channel_id=1, source_target_pairs={{0,4},{4,0},{8,12},{12,8},{16,20},{20,16},{24,28},{28,24},{1,5},{5... | collective-permute-start | bytes 589832 | tf_op jit(solution)/shard_map/ppermute | solution.py:248
  35.1 2.7 %collective-permute-start.12 = (bf16[3,128,256]{2,1,0:T(8,128)(2,1)S(1)}, bf16[3,128,256]{2,1,0:T(8,128)(2,1)S(1)}, u32[]{:S(2)}, u32[]{:S(2)}) collective-permute-start(bf16[3,128,256]{2,1,0:T(8,128)(2,1)S(1)} %collective-permute-done.11.refs_5_.refs_12_), channel_id=1, source_target_pairs={{0,4},{4,0},{8,12},{12,8},{16,20},{20,16},{24,28},{28,24},{1,5},{5... | collective-permute-start | bytes 589832 | tf_op jit(solution)/shard_map/ppermute | solution.py:248
  35.6 2.2 %collective-permute-start.14 = (bf16[3,128,256]{2,1,0:T(8,128)(2,1)S(1)}, bf16[3,128,256]{2,1,0:T(8,128)(2,1)S(1)}, u32[]{:S(2)}, u32[]{:S(2)}) collective-permute-start(bf16[3,128,256]{2,1,0:T(8,128)(2,1)S(1)} %collective-permute-done.13.refs_7_.refs_14_), channel_id=1, source_target_pairs={{0,4},{4,0},{8,12},{12,8},{16,20},{20,16},{24,28},{28,24},{1,5},{5... | collective-permute-start | bytes 589832 | tf_op jit(solution)/shard_map/ppermute | solution.py:248
  35.7 2.2 %collective-permute-start.16 = (bf16[3,128,256]{2,1,0:T(8,128)(2,1)S(1)}, bf16[3,128,256]{2,1,0:T(8,128)(2,1)S(1)}, u32[]{:S(2)}, u32[]{:S(2)}) collective-permute-start(bf16[3,128,256]{2,1,0:T(8,128)(2,1)S(1)} %collective-permute-done.15.refs_9_.refs_16_), channel_id=1, source_target_pairs={{0,4},{4,0},{8,12},{12,8},{16,20},{20,16},{24,28},{28,24},{1,5},{5... | collective-permute-start | bytes 589832 | tf_op jit(solution)/shard_map/ppermute | solution.py:248
  38.5 20.9 %copy-start.1 = (bf16[2,1024,512]{2,1,0:T(8,128)(2,1)S(1)}, bf16[2,1024,512]{2,1,0:T(8,128)(2,1)}, u32[]{:S(2)}) copy-start(bf16[2,1024,512]{2,1,0:T(8,128)(2,1)} %factor_ref.3) | copy-start | bytes 6291460
  38.5 20.9 %copy-start.4 = (bf16[64,512]{1,0:T(8,128)(2,1)S(1)}, bf16[64,512]{1,0:T(8,128)(2,1)}, u32[]{:S(2)}) copy-start(bf16[64,512]{1,0:T(8,128)(2,1)} %solved_ref.2) | copy-start | bytes 196612
  38.5 3.8 %collective-permute-start.17 = (bf16[16,512]{1,0:T(8,128)(2,1)S(1)}, bf16[16,512]{1,0:T(8,128)(2,1)S(1)}, u32[]{:S(2)}, u32[]{:S(2)}) collective-permute-start(bf16[16,512]{1,0:T(8,128)(2,1)S(1)} %get-tuple-element.21.refs_0_), channel_id=1, source_target_pairs={{0,1},{1,0},{2,3},{3,2},{4,5},{5,4},{6,7},{7,6},{8,9},{9,8},{10,11... | collective-permute-start | bytes 49160 | tf_op jit(solution)/shard_map/ppermute | solution.py:251
  42.8 3.8 %collective-permute-start.18 = (bf16[16,512]{1,0:T(8,128)(2,1)S(1)}, bf16[16,512]{1,0:T(8,128)(2,1)S(1)}, u32[]{:S(2)}, u32[]{:S(2)}) collective-permute-start(bf16[16,512]{1,0:T(8,128)(2,1)S(1)} %get-tuple-element.23.refs_2_), channel_id=1, source_target_pairs={{0,1},{1,0},{2,3},{3,2},{4,5},{5,4},{6,7},{7,6},{8,9},{9,8},{10,11... | collective-permute-start | bytes 49160 | tf_op jit(solution)/shard_map/ppermute | solution.py:251
  58.0 1.3 %collective-permute-start.19 = (bf16[16,16,256]{2,1,0:T(8,128)(2,1)S(1)}, bf16[16,16,256]{2,1,0:T(8,128)(2,1)S(1)}, u32[]{:S(2)}, u32[]{:S(2)}) collective-permute-start(bf16[16,16,256]{2,1,0:T(8,128)(2,1)S(1)} %all_to_all.10.own_ref), channel_id=1, source_target_pairs={{0,4},{4,0},{8,12},{12,8},{16,20},{20,16},{24,28},{28,24},{1,5},{5... | collective-permute-start | bytes 393224 | tf_op jit(solution)/shard_map/ppermute | solution.py:248

commit v8 on v7

--- a/solution.py
+++ b/solution.py
@@ -137,9 +137,9 @@
     update = None
     for k in range(2):
         back_ref[k] = columns(k, here)
-        for c in range(C):
-            term = plain(columns(k, c).astype(BF), factor_ref[k, c * rows : (c + 1) * rows])
-            update = term if update is None else update + term
+        whole = jnp.concatenate([columns(k, c).astype(BF) for c in range(C)], axis=1)
+        term = plain(whole, factor_ref[k])
+        update = term if update is None else update + term
     remaining_ref[...] = solved_ref[...].astype(F32) - update
 
 

time: 60.7 us -> 60.7 us (level)
  no operation moved by 1% of the time
where the time goes in v8:
time: 60.7 us; the launch traced here: 60.5 us
  waiting for transfers between devices  21 us (35%)
  starting transfers between devices  20.1 us (33%)
  blocking collectives  11.3 us (19%)
  Pallas kernels  7.32 us (12%)
  between operations  0.73 us (1%)
    ppermute x5, waiting for transfers between devices, xor_col(): return lax.ppermute(value, 'col', [(i, i ^ step) for i in range(C)])  11.6 us
    all_to_all x1, blocking collectives, exchange(): return lax.all_to_all(value, axes, 0, 0, tiled=False)  11.3 us
    ppermute x15, starting transfers between devices, xor_row(): return lax.ppermute(value, ROW, [(i, i ^ step) for i in range(R)])  9.21 us
    ppermute x5, starting transfers between devices, xor_col(): return lax.ppermute(value, 'col', [(i, i ^ step) for i in range(C)])  7.54 us
    all_to_all x1, waiting for transfers between devices, exchange(): return lax.all_to_all(value, axes, 0, 0, tiled=False)  5.7 us
    ppermute x15, waiting for transfers between devices, xor_row(): return lax.ppermute(value, ROW, [(i, i ^ step) for i in range(R)])  3.73 us
    all_to_all x1, starting transfers between devices, exchange(): return lax.all_to_all(value, axes, 0, 0, tiled=False)  3.38 us
    pallas_call x1, Pallas kernels, shards(): pl.pallas_call(panel_kernel, in_specs=[pl.BlockSpec(memory_space=pl.ANY)]...  2.96 us
  transfers between devices with their start and end apart: 21, of which 10 were waited for; matrix products, arithmetic and copies ran while one was open for 0% of the time, Pallas kernels for 5%

profile of v8, /device:TPU:0, one launch (start us, length us, event | category | flops | bytes accessed | tf_op | source)
XLA Modules:
  0.0 60.5 jit_solution(213850947044007264)
XLA Ops:
  0.7 1.7 %shard_map.68.own_ref = bf16[2,128,256]{2,1,0:T(8,128)(2,1)} custom-call(bf16[2,128,256]{2,1,0:T(8,128)(2,1)} %refs_4_.1, bf16[256,128]{1,0:T(8,128)(2,1)} %link_ref.1), custom_call_target="tpu_custom_call" | custom-call | tf_op jit(solution)/shard_map/pallas_call | solution.py:216
  2.4 4.0 %collective-permute-start = (bf16[2,128,256]{2,1,0:T(8,128)(2,1)}, bf16[2,128,256]{2,1,0:T(8,128)(2,1)S(1)}, u32[]{:S(2)}, u32[]{:S(2)}) collective-permute-start(bf16[2,128,256]{2,1,0:T(8,128)(2,1)} %shard_map.68.own_ref), channel_id=1, source_target_pairs={{0,2},{1,3},{2,0},{3,1},{4,6},{5,7},{6,4},{7,5},{8,10},{9,11},{10,... | collective-permute-start | bytes 393224 | tf_op jit(solution)/shard_map/ppermute | solution.py:251
  6.4 2.4 %collective-permute-start.3 = (bf16[2,128,256]{2,1,0:T(8,128)(2,1)}, bf16[2,128,256]{2,1,0:T(8,128)(2,1)S(1)}, u32[]{:S(2)}, u32[]{:S(2)}) collective-permute-start(bf16[2,128,256]{2,1,0:T(8,128)(2,1)} %refs_4_.1), channel_id=1, source_target_pairs={{0,24},{4,28},{8,16},{12,20},{16,8},{20,12},{24,0},{28,4},{1,25},{... | collective-permute-start | bytes 393224 | tf_op jit(solution)/shard_map/ppermute | solution.py:248
  8.8 0.5 collective-permute-start.2
  9.3 0.5 collective-permute-start.1
  9.9 3.0 %shard_map.69 = bf16[8,4,16,256]{3,2,1,0:T(8,128)(2,1)} custom-call(bf16[64,512]{1,0:T(8,128)(2,1)} %solved_ref.2, bf16[2,1024,512]{2,1,0:T(8,128)(2,1)} %factor_ref.3), custom_call_target="tpu_custom_call" | custom-call | tf_op jit(solution)/shard_map/pallas_call | solution.py:270
  13.1 2.2 %collective-permute-done.2.refs_4_.refs_15_.refs_6_.refs_8_ = bf16[2,128,256]{2,1,0:T(8,128)(2,1)S(1)} collective-permute-done((bf16[2,128,256]{2,1,0:T(8,128)(2,1)}, bf16[2,128,256]{2,1,0:T(8,128)(2,1)S(1)}, u32[]{:S(2)}, u32[]{:S(2)}) %collective-permute-start.2) | collective-permute-done | bytes 131104 | tf_op jit(solution)/shard_map/ppermute | solution.py:248
  15.3 3.4 %all-to-all-start = ((bf16[32,16,256]{2,1,0:T(8,128)(2,1)}), bf16[32,16,256]{2,1,0:T(8,128)(2,1)S(1)}, u32[]{:S(2)}, u32[]{:S(2)}) async-start(bf16[32,16,256]{2,1,0:T(8,128)(2,1)} %bitcast.10), calls=%async_computation | async-start | bytes 524288 | tf_op jit(solution)/shard_map/all_to_all | solution.py:31
  18.7 0.3 collective-permute-start.4
  19.0 0.3 collective-permute-start.7
  19.3 0.3 collective-permute-start.6
  19.6 0.3 collective-permute-start.5
  19.8 2.7 %collective-permute-start.15 = (bf16[3,128,256]{2,1,0:T(8,128)(2,1)S(1)}, bf16[3,128,256]{2,1,0:T(8,128)(2,1)S(1)}, u32[]{:S(2)}, u32[]{:S(2)}) collective-permute-start(bf16[3,128,256]{2,1,0:T(8,128)(2,1)S(1)} %shard_map.71.refs_3_.refs_10_), channel_id=1, source_target_pairs={{0,24},{4,28},{8,16},{12,20},{16,8},{20,12},{24,0},{28,4},{1,25},{... | collective-permute-start | bytes 589832 | tf_op jit(solution)/shard_map/ppermute | solution.py:248
  22.6 0.6 collective-permute-start.13
  23.1 0.3 collective-permute-start.11
  23.4 5.7 %all-to-all-done.panel_ref = bf16[32,16,256]{2,1,0:T(8,128)(2,1)S(1)} async-done(((bf16[32,16,256]{2,1,0:T(8,128)(2,1)}), bf16[32,16,256]{2,1,0:T(8,128)(2,1)S(1)}, u32[]{:S(2)}, u32[]{:S(2)}) %all-to-all-start) | async-done | bytes 262176 | tf_op jit(solution)/shard_map/all_to_all | solution.py:31
  29.1 0.2 shard_map.70
  29.3 0.6 %collective-permute-start.8 = (bf16[16,640]{1,0:T(8,128)(2,1)S(1)}, bf16[16,640]{1,0:T(8,128)(2,1)S(1)}, u32[]{:S(2)}, u32[]{:S(2)}) collective-permute-start(bf16[16,640]{1,0:T(8,128)(2,1)S(1)} %shard_map.70), channel_id=1, source_target_pairs={{0,2},{1,3},{2,0},{3,1},{4,6},{5,7},{6,4},{7,5},{8,10},{9,11},{10,... | collective-permute-start | bytes 61448 | tf_op jit(solution)/shard_map/ppermute | solution.py:251
  30.0 4.1 %collective-permute-done.8 = bf16[16,640]{1,0:T(8,128)(2,1)S(1)} collective-permute-done((bf16[16,640]{1,0:T(8,128)(2,1)S(1)}, bf16[16,640]{1,0:T(8,128)(2,1)S(1)}, u32[]{:S(2)}, u32[]{:S(2)}) %collective-permute-start.8) | collective-permute-done | bytes 20512 | tf_op jit(solution)/shard_map/ppermute | solution.py:251
  34.1 1.0 %collective-permute-start.9 = (bf16[16,512]{1,0:T(8,128)(2,1)S(1)}, bf16[16,512]{1,0:T(8,128)(2,1)S(1)}, u32[]{:S(2)}, u32[]{:S(2)}) collective-permute-start(bf16[16,512]{1,0:T(8,128)(2,1)S(1)} %add_convert_fusion.refs_0_), channel_id=1, source_target_pairs={{0,1},{1,0},{2,3},{3,2},{4,5},{5,4},{6,7},{7,6},{8,9},{9,8},{10,11... | collective-permute-start | bytes 49160 | tf_op jit(solution)/shard_map/ppermute | solution.py:251
  35.1 0.5 collective-permute-start.12
  35.7 0.4 collective-permute-start.16
  36.2 1.7 %collective-permute-done.9.refs_1_ = bf16[16,512]{1,0:T(8,128)(2,1)S(1)} collective-permute-done((bf16[16,512]{1,0:T(8,128)(2,1)S(1)}, bf16[16,512]{1,0:T(8,128)(2,1)S(1)}, u32[]{:S(2)}, u32[]{:S(2)}) %collective-permute-start.9) | collective-permute-done | bytes 16416 | tf_op jit(solution)/shard_map/ppermute | solution.py:251
  37.9 0.6 shard_map.72
  38.5 0.9 %collective-permute-start.17 = (bf16[16,512]{1,0:T(8,128)(2,1)S(1)}, bf16[16,512]{1,0:T(8,128)(2,1)S(1)}, u32[]{:S(2)}, u32[]{:S(2)}) collective-permute-start(bf16[16,512]{1,0:T(8,128)(2,1)S(1)} %get-tuple-element.21.refs_0_), channel_id=1, source_target_pairs={{0,1},{1,0},{2,3},{3,2},{4,5},{5,4},{6,7},{7,6},{8,9},{9,8},{10,11... | collective-permute-start | bytes 49160 | tf_op jit(solution)/shard_map/ppermute | solution.py:251
  39.4 2.8 %collective-permute-done.17.refs_1_ = bf16[16,512]{1,0:T(8,128)(2,1)S(1)} collective-permute-done((bf16[16,512]{1,0:T(8,128)(2,1)S(1)}, bf16[16,512]{1,0:T(8,128)(2,1)S(1)}, u32[]{:S(2)}, u32[]{:S(2)}) %collective-permute-start.17) | collective-permute-done | bytes 16416 | tf_op jit(solution)/shard_map/ppermute | solution.py:251
  42.2 0.6 shard_map.73
  42.8 0.9 %collective-permute-start.18 = (bf16[16,512]{1,0:T(8,128)(2,1)S(1)}, bf16[16,512]{1,0:T(8,128)(2,1)S(1)}, u32[]{:S(2)}, u32[]{:S(2)}) collective-permute-start(bf16[16,512]{1,0:T(8,128)(2,1)S(1)} %get-tuple-element.23.refs_2_), channel_id=1, source_target_pairs={{0,1},{1,0},{2,3},{3,2},{4,5},{5,4},{6,7},{7,6},{8,9},{9,8},{10,11... | collective-permute-start | bytes 49160 | tf_op jit(solution)/shard_map/ppermute | solution.py:251
  43.7 2.8 %collective-permute-done.18.refs_3_ = bf16[16,512]{1,0:T(8,128)(2,1)S(1)} collective-permute-done((bf16[16,512]{1,0:T(8,128)(2,1)S(1)}, bf16[16,512]{1,0:T(8,128)(2,1)S(1)}, u32[]{:S(2)}, u32[]{:S(2)}) %collective-permute-start.18) | collective-permute-done | bytes 16416 | tf_op jit(solution)/shard_map/ppermute | solution.py:251
  46.7 11.3 %all_to_all.10.own_ref = bf16[16,16,256]{2,1,0:T(8,128)(2,1)S(1)} all-to-all(bf16[16,16,256]{2,1,0:T(8,128)(2,1)S(1)} %shard_map.74), channel_id=1, replica_groups=mesh['chip'=4,'core'=2,'col'=4] {'chip','col'}, dimensions={0} | all-to-all | bytes 262144 | tf_op jit(solution)/shard_map/all_to_all | solution.py:31
  58.0 1.3 %collective-permute-done.19.other_ref = bf16[16,16,256]{2,1,0:T(8,128)(2,1)S(1)} collective-permute-done((bf16[16,16,256]{2,1,0:T(8,128)(2,1)S(1)}, bf16[16,16,256]{2,1,0:T(8,128)(2,1)S(1)}, u32[]{:S(2)}, u32[]{:S(2)}) %collective-permute-start.19) | collective-permute-done | bytes 131104 | tf_op jit(solution)/shard_map/ppermute | solution.py:248
  59.3 1.1 %shard_map.75 = (f32[64,512]{1,0:T(8,128)}, f32[2,64,256]{2,1,0:T(8,128)}) custom-call(bf16[64,512]{1,0:T(8,128)(2,1)S(1)} %copy-done.4, bf16[2,1024,512]{2,1,0:T(8,128)(2,1)S(1)} %copy-done.1, bf16[16,16,256]{2,1,0:T(8,128)(2,1)S(1)} %all_to_all.10.own_ref, bf16[16,16,256]{2,1,0:T(8,128)(2,1)S(1)} %collective-permute-done.19.other_ref), custom_call_target="tpu_custom_call" | custom-call | tf_op jit(solution)/shard_map/pallas_call | solution.py:312
  (34 shorter events, 0.7 us)
Async XLA Ops:
  0.6 19.2 %copy-start = (f32[2,256,64]{1,2,0:T(8,128)S(1)}, f32[2,256,64]{1,2,0:T(8,128)}, u32[]{:S(2)}) copy-start(f32[2,256,64]{1,2,0:T(8,128)} %param.9) | copy-start | bytes 393220
  0.6 18.1 %copy-start.2 = (bf16[2,128,256]{2,1,0:T(8,128)(2,1)S(1)}, bf16[2,128,256]{2,1,0:T(8,128)(2,1)}, u32[]{:S(2)}) copy-start(bf16[2,128,256]{2,1,0:T(8,128)(2,1)} %refs_4_.1) | copy-start | bytes 393220
  2.4 17.5 %copy-start.3 = (bf16[2,128,256]{2,1,0:T(8,128)(2,1)S(1)}, bf16[2,128,256]{2,1,0:T(8,128)(2,1)}, u32[]{:S(2)}) copy-start(bf16[2,128,256]{2,1,0:T(8,128)(2,1)} %shard_map.68.own_ref) | copy-start | bytes 393220
  2.4 10.6 %collective-permute-start = (bf16[2,128,256]{2,1,0:T(8,128)(2,1)}, bf16[2,128,256]{2,1,0:T(8,128)(2,1)S(1)}, u32[]{:S(2)}, u32[]{:S(2)}) collective-permute-start(bf16[2,128,256]{2,1,0:T(8,128)(2,1)} %shard_map.68.own_ref), channel_id=1, source_target_pairs={{0,2},{1,3},{2,0},{3,1},{4,6},{5,7},{6,4},{7,5},{8,10},{9,11},{10,... | collective-permute-start | bytes 393224 | tf_op jit(solution)/shard_map/ppermute | solution.py:251
  6.4 6.7 %collective-permute-start.3 = (bf16[2,128,256]{2,1,0:T(8,128)(2,1)}, bf16[2,128,256]{2,1,0:T(8,128)(2,1)S(1)}, u32[]{:S(2)}, u32[]{:S(2)}) collective-permute-start(bf16[2,128,256]{2,1,0:T(8,128)(2,1)} %refs_4_.1), channel_id=1, source_target_pairs={{0,24},{4,28},{8,16},{12,20},{16,8},{20,12},{24,0},{28,4},{1,25},{... | collective-permute-start | bytes 393224 | tf_op jit(solution)/shard_map/ppermute | solution.py:248
  8.8 6.4 %collective-permute-start.2 = (bf16[2,128,256]{2,1,0:T(8,128)(2,1)}, bf16[2,128,256]{2,1,0:T(8,128)(2,1)S(1)}, u32[]{:S(2)}, u32[]{:S(2)}) collective-permute-start(bf16[2,128,256]{2,1,0:T(8,128)(2,1)} %refs_4_.1), channel_id=1, source_target_pairs={{0,16},{4,20},{8,24},{12,28},{16,0},{20,4},{24,8},{28,12},{1,17},{... | collective-permute-start | bytes 393224 | tf_op jit(solution)/shard_map/ppermute | solution.py:248
  9.3 6.0 %collective-permute-start.1 = (bf16[2,128,256]{2,1,0:T(8,128)(2,1)}, bf16[2,128,256]{2,1,0:T(8,128)(2,1)S(1)}, u32[]{:S(2)}, u32[]{:S(2)}) collective-permute-start(bf16[2,128,256]{2,1,0:T(8,128)(2,1)} %refs_4_.1), channel_id=1, source_target_pairs={{0,8},{4,12},{8,0},{12,4},{16,24},{20,28},{24,16},{28,20},{1,9},{5... | collective-permute-start | bytes 393224 | tf_op jit(solution)/shard_map/ppermute | solution.py:248
  15.3 13.8 %all-to-all-start = ((bf16[32,16,256]{2,1,0:T(8,128)(2,1)}), bf16[32,16,256]{2,1,0:T(8,128)(2,1)S(1)}, u32[]{:S(2)}, u32[]{:S(2)}) async-start(bf16[32,16,256]{2,1,0:T(8,128)(2,1)} %bitcast.10), calls=%async_computation | async-start | bytes 524288 | tf_op jit(solution)/shard_map/all_to_all | solution.py:31
  18.7 3.9 %collective-permute-start.4 = (bf16[2,128,256]{2,1,0:T(8,128)(2,1)S(1)}, bf16[2,128,256]{2,1,0:T(8,128)(2,1)S(1)}, u32[]{:S(2)}, u32[]{:S(2)}) collective-permute-start(bf16[2,128,256]{2,1,0:T(8,128)(2,1)S(1)} %copy-done.2), channel_id=1, source_target_pairs={{0,4},{4,0},{8,12},{12,8},{16,20},{20,16},{24,28},{28,24},{1,5},{5... | collective-permute-start | bytes 393224 | tf_op jit(solution)/shard_map/ppermute | solution.py:248
  19.0 4.1 %collective-permute-start.7 = (bf16[2,128,256]{2,1,0:T(8,128)(2,1)S(1)}, bf16[2,128,256]{2,1,0:T(8,128)(2,1)S(1)}, u32[]{:S(2)}, u32[]{:S(2)}) collective-permute-start(bf16[2,128,256]{2,1,0:T(8,128)(2,1)S(1)} %collective-permute-done.3.refs_6_.refs_17_.refs_8_.refs_10_), channel_id=1, source_target_pairs={{0,4},{4,0},{8,12},{12,8},{16,20},{20,16},{24,28},{28,24},{1,5},{5... | collective-permute-start | bytes 393224 | tf_op jit(solution)/shard_map/ppermute | solution.py:248
  19.3 4.1 %collective-permute-start.6 = (bf16[2,128,256]{2,1,0:T(8,128)(2,1)S(1)}, bf16[2,128,256]{2,1,0:T(8,128)(2,1)S(1)}, u32[]{:S(2)}, u32[]{:S(2)}) collective-permute-start(bf16[2,128,256]{2,1,0:T(8,128)(2,1)S(1)} %collective-permute-done.2.refs_4_.refs_15_.refs_6_.refs_8_), channel_id=1, source_target_pairs={{0,4},{4,0},{8,12},{12,8},{16,20},{20,16},{24,28},{28,24},{1,5},{5... | collective-permute-start | bytes 393224 | tf_op jit(solution)/shard_map/ppermute | solution.py:248
  19.6 3.9 %collective-permute-start.5 = (bf16[2,128,256]{2,1,0:T(8,128)(2,1)S(1)}, bf16[2,128,256]{2,1,0:T(8,128)(2,1)S(1)}, u32[]{:S(2)}, u32[]{:S(2)}) collective-permute-start(bf16[2,128,256]{2,1,0:T(8,128)(2,1)S(1)} %collective-permute-done.1.refs_2_.refs_13_.refs_4_.refs_6_), channel_id=1, source_target_pairs={{0,4},{4,0},{8,12},{12,8},{16,20},{20,16},{24,28},{28,24},{1,5},{5... | collective-permute-start | bytes 393224 | tf_op jit(solution)/shard_map/ppermute | solution.py:248
  19.8 15.2 %collective-permute-start.15 = (bf16[3,128,256]{2,1,0:T(8,128)(2,1)S(1)}, bf16[3,128,256]{2,1,0:T(8,128)(2,1)S(1)}, u32[]{:S(2)}, u32[]{:S(2)}) collective-permute-start(bf16[3,128,256]{2,1,0:T(8,128)(2,1)S(1)} %shard_map.71.refs_3_.refs_10_), channel_id=1, source_target_pairs={{0,24},{4,28},{8,16},{12,20},{16,8},{20,12},{24,0},{28,4},{1,25},{... | collective-permute-start | bytes 589832 | tf_op jit(solution)/shard_map/ppermute | solution.py:248
  22.6 12.5 %collective-permute-start.13 = (bf16[3,128,256]{2,1,0:T(8,128)(2,1)S(1)}, bf16[3,128,256]{2,1,0:T(8,128)(2,1)S(1)}, u32[]{:S(2)}, u32[]{:S(2)}) collective-permute-start(bf16[3,128,256]{2,1,0:T(8,128)(2,1)S(1)} %shard_map.71.refs_3_.refs_10_), channel_id=1, source_target_pairs={{0,16},{4,20},{8,24},{12,28},{16,0},{20,4},{24,8},{28,12},{1,17},{... | collective-permute-start | bytes 589832 | tf_op jit(solution)/shard_map/ppermute | solution.py:248
  23.1 11.9 %collective-permute-start.11 = (bf16[3,128,256]{2,1,0:T(8,128)(2,1)S(1)}, bf16[3,128,256]{2,1,0:T(8,128)(2,1)S(1)}, u32[]{:S(2)}, u32[]{:S(2)}) collective-permute-start(bf16[3,128,256]{2,1,0:T(8,128)(2,1)S(1)} %shard_map.71.refs_3_.refs_10_), channel_id=1, source_target_pairs={{0,8},{4,12},{8,0},{12,4},{16,24},{20,28},{24,16},{28,20},{1,9},{5... | collective-permute-start | bytes 589832 | tf_op jit(solution)/shard_map/ppermute | solution.py:248
  29.3 4.7 %collective-permute-start.8 = (bf16[16,640]{1,0:T(8,128)(2,1)S(1)}, bf16[16,640]{1,0:T(8,128)(2,1)S(1)}, u32[]{:S(2)}, u32[]{:S(2)}) collective-permute-start(bf16[16,640]{1,0:T(8,128)(2,1)S(1)} %shard_map.70), channel_id=1, source_target_pairs={{0,2},{1,3},{2,0},{3,1},{4,6},{5,7},{6,4},{7,5},{8,10},{9,11},{10,... | collective-permute-start | bytes 61448 | tf_op jit(solution)/shard_map/ppermute | solution.py:251
  34.1 3.8 %collective-permute-start.9 = (bf16[16,512]{1,0:T(8,128)(2,1)S(1)}, bf16[16,512]{1,0:T(8,128)(2,1)S(1)}, u32[]{:S(2)}, u32[]{:S(2)}) collective-permute-start(bf16[16,512]{1,0:T(8,128)(2,1)S(1)} %add_convert_fusion.refs_0_), channel_id=1, source_target_pairs={{0,1},{1,0},{2,3},{3,2},{4,5},{5,4},{6,7},{7,6},{8,9},{9,8},{10,11... | collective-permute-start | bytes 49160 | tf_op jit(solution)/shard_map/ppermute | solution.py:251
  35.1 2.8 %collective-permute-start.10 = (bf16[3,128,256]{2,1,0:T(8,128)(2,1)S(1)}, bf16[3,128,256]{2,1,0:T(8,128)(2,1)S(1)}, u32[]{:S(2)}, u32[]{:S(2)}) collective-permute-start(bf16[3,128,256]{2,1,0:T(8,128)(2,1)S(1)} %shard_map.71.refs_3_.refs_10_), channel_id=1, source_target_pairs={{0,4},{4,0},{8,12},{12,8},{16,20},{20,16},{24,28},{28,24},{1,5},{5... | collective-permute-start | bytes 589832 | tf_op jit(solution)/shard_map/ppermute | solution.py:248
  35.1 2.7 %collective-permute-start.12 = (bf16[3,128,256]{2,1,0:T(8,128)(2,1)S(1)}, bf16[3,128,256]{2,1,0:T(8,128)(2,1)S(1)}, u32[]{:S(2)}, u32[]{:S(2)}) collective-permute-start(bf16[3,128,256]{2,1,0:T(8,128)(2,1)S(1)} %collective-permute-done.11.refs_5_.refs_12_), channel_id=1, source_target_pairs={{0,4},{4,0},{8,12},{12,8},{16,20},{20,16},{24,28},{28,24},{1,5},{5... | collective-permute-start | bytes 589832 | tf_op jit(solution)/shard_map/ppermute | solution.py:248
  35.6 2.2 %collective-permute-start.14 = (bf16[3,128,256]{2,1,0:T(8,128)(2,1)S(1)}, bf16[3,128,256]{2,1,0:T(8,128)(2,1)S(1)}, u32[]{:S(2)}, u32[]{:S(2)}) collective-permute-start(bf16[3,128,256]{2,1,0:T(8,128)(2,1)S(1)} %collective-permute-done.13.refs_7_.refs_14_), channel_id=1, source_target_pairs={{0,4},{4,0},{8,12},{12,8},{16,20},{20,16},{24,28},{28,24},{1,5},{5... | collective-permute-start | bytes 589832 | tf_op jit(solution)/shard_map/ppermute | solution.py:248
  35.7 2.2 %collective-permute-start.16 = (bf16[3,128,256]{2,1,0:T(8,128)(2,1)S(1)}, bf16[3,128,256]{2,1,0:T(8,128)(2,1)S(1)}, u32[]{:S(2)}, u32[]{:S(2)}) collective-permute-start(bf16[3,128,256]{2,1,0:T(8,128)(2,1)S(1)} %collective-permute-done.15.refs_9_.refs_16_), channel_id=1, source_target_pairs={{0,4},{4,0},{8,12},{12,8},{16,20},{20,16},{24,28},{28,24},{1,5},{5... | collective-permute-start | bytes 589832 | tf_op jit(solution)/shard_map/ppermute | solution.py:248
  38.5 20.9 %copy-start.1 = (bf16[2,1024,512]{2,1,0:T(8,128)(2,1)S(1)}, bf16[2,1024,512]{2,1,0:T(8,128)(2,1)}, u32[]{:S(2)}) copy-start(bf16[2,1024,512]{2,1,0:T(8,128)(2,1)} %factor_ref.3) | copy-start | bytes 6291460
  38.5 20.9 %copy-start.4 = (bf16[64,512]{1,0:T(8,128)(2,1)S(1)}, bf16[64,512]{1,0:T(8,128)(2,1)}, u32[]{:S(2)}) copy-start(bf16[64,512]{1,0:T(8,128)(2,1)} %solved_ref.2) | copy-start | bytes 196612
  38.5 3.8 %collective-permute-start.17 = (bf16[16,512]{1,0:T(8,128)(2,1)S(1)}, bf16[16,512]{1,0:T(8,128)(2,1)S(1)}, u32[]{:S(2)}, u32[]{:S(2)}) collective-permute-start(bf16[16,512]{1,0:T(8,128)(2,1)S(1)} %get-tuple-element.21.refs_0_), channel_id=1, source_target_pairs={{0,1},{1,0},{2,3},{3,2},{4,5},{5,4},{6,7},{7,6},{8,9},{9,8},{10,11... | collective-permute-start | bytes 49160 | tf_op jit(solution)/shard_map/ppermute | solution.py:251
  42.8 3.8 %collective-permute-start.18 = (bf16[16,512]{1,0:T(8,128)(2,1)S(1)}, bf16[16,512]{1,0:T(8,128)(2,1)S(1)}, u32[]{:S(2)}, u32[]{:S(2)}) collective-permute-start(bf16[16,512]{1,0:T(8,128)(2,1)S(1)} %get-tuple-element.23.refs_2_), channel_id=1, source_target_pairs={{0,1},{1,0},{2,3},{3,2},{4,5},{5,4},{6,7},{7,6},{8,9},{9,8},{10,11... | collective-permute-start | bytes 49160 | tf_op jit(solution)/shard_map/ppermute | solution.py:251
  58.0 1.3 %collective-permute-start.19 = (bf16[16,16,256]{2,1,0:T(8,128)(2,1)S(1)}, bf16[16,16,256]{2,1,0:T(8,128)(2,1)S(1)}, u32[]{:S(2)}, u32[]{:S(2)}) collective-permute-start(bf16[16,16,256]{2,1,0:T(8,128)(2,1)S(1)} %all_to_all.10.own_ref), channel_id=1, source_target_pairs={{0,4},{4,0},{8,12},{12,8},{16,20},{20,16},{24,28},{28,24},{1,5},{5... | collective-permute-start | bytes 393224 | tf_op jit(solution)/shard_map/ppermute | solution.py:248

commit v9 on v7

--- a/solution.py
+++ b/solution.py
@@ -103,9 +103,9 @@
 
 def panel_kernel(solved_ref, factor_ref, part_ref, solved, factor, sems):
     R, C, double, rows = part_ref.shape
-    step = C // 4
+    step = C // 2
     copies = [pltpu.make_async_copy(solved_ref, solved, sems.at[0])]
-    for i in range(4):
+    for i in range(2):
         chunk = pl.ds(i * step * rows, step * rows)
         copies.append(pltpu.make_async_copy(factor_ref.at[:, chunk], factor.at[:, chunk], sems.at[1 + i]))
     for copy in copies:
@@ -274,7 +274,7 @@
             scratch_shapes=[
                 pltpu.VMEM(solved.shape, BF),
                 pltpu.VMEM(factor_rows.shape, BF),
-                pltpu.SemaphoreType.DMA((5,)),
+                pltpu.SemaphoreType.DMA((3,)),
             ],
             compiler_params=WIDE,
         )(held, factor_rows)

time: 60.7 us -> 60.7 us (level)
  no operation moved by 1% of the time
where the time goes in v9:
time: 60.7 us; the launch traced here: 60.5 us
  waiting for transfers between devices  21.1 us (35%)
  starting transfers between devices  20.1 us (33%)
  blocking collectives  11.3 us (19%)
  Pallas kernels  7.23 us (12%)
  between operations  0.73 us (1%)
    ppermute x5, waiting for transfers between devices, xor_col(): return lax.ppermute(value, 'col', [(i, i ^ step) for i in range(C)])  11.7 us
    all_to_all x1, blocking collectives, exchange(): return lax.all_to_all(value, axes, 0, 0, tiled=False)  11.3 us
    ppermute x15, starting transfers between devices, xor_row(): return lax.ppermute(value, ROW, [(i, i ^ step) for i in range(R)])  9.21 us
    ppermute x5, starting transfers between devices, xor_col(): return lax.ppermute(value, 'col', [(i, i ^ step) for i in range(C)])  7.54 us
    all_to_all x1, waiting for transfers between devices, exchange(): return lax.all_to_all(value, axes, 0, 0, tiled=False)  5.7 us
    ppermute x15, waiting for transfers between devices, xor_row(): return lax.ppermute(value, ROW, [(i, i ^ step) for i in range(R)])  3.73 us
    all_to_all x1, starting transfers between devices, exchange(): return lax.all_to_all(value, axes, 0, 0, tiled=False)  3.38 us
    pallas_call x1, Pallas kernels, shards(): pl.pallas_call(panel_kernel, in_specs=[pl.BlockSpec(memory_space=pl.ANY)]...  2.87 us
  transfers between devices with their start and end apart: 21, of which 10 were waited for; matrix products, arithmetic and copies ran while one was open for 0% of the time, Pallas kernels for 5%

profile of v9, /device:TPU:0, one launch (start us, length us, event | category | flops | bytes accessed | tf_op | source)
XLA Modules:
  0.0 60.5 jit_solution(10829468112755954083)
XLA Ops:
  0.7 1.7 %shard_map.68.own_ref = bf16[2,128,256]{2,1,0:T(8,128)(2,1)} custom-call(bf16[2,128,256]{2,1,0:T(8,128)(2,1)} %refs_4_.1, bf16[256,128]{1,0:T(8,128)(2,1)} %link_ref.1), custom_call_target="tpu_custom_call" | custom-call | tf_op jit(solution)/shard_map/pallas_call | solution.py:216
  2.4 4.0 %collective-permute-start = (bf16[2,128,256]{2,1,0:T(8,128)(2,1)}, bf16[2,128,256]{2,1,0:T(8,128)(2,1)S(1)}, u32[]{:S(2)}, u32[]{:S(2)}) collective-permute-start(bf16[2,128,256]{2,1,0:T(8,128)(2,1)} %shard_map.68.own_ref), channel_id=1, source_target_pairs={{0,2},{1,3},{2,0},{3,1},{4,6},{5,7},{6,4},{7,5},{8,10},{9,11},{10,... | collective-permute-start | bytes 393224 | tf_op jit(solution)/shard_map/ppermute | solution.py:251
  6.4 2.4 %collective-permute-start.3 = (bf16[2,128,256]{2,1,0:T(8,128)(2,1)}, bf16[2,128,256]{2,1,0:T(8,128)(2,1)S(1)}, u32[]{:S(2)}, u32[]{:S(2)}) collective-permute-start(bf16[2,128,256]{2,1,0:T(8,128)(2,1)} %refs_4_.1), channel_id=1, source_target_pairs={{0,24},{4,28},{8,16},{12,20},{16,8},{20,12},{24,0},{28,4},{1,25},{... | collective-permute-start | bytes 393224 | tf_op jit(solution)/shard_map/ppermute | solution.py:248
  8.8 0.5 collective-permute-start.2
  9.3 0.5 collective-permute-start.1
  9.9 2.9 %shard_map.69 = bf16[8,4,16,256]{3,2,1,0:T(8,128)(2,1)} custom-call(bf16[64,512]{1,0:T(8,128)(2,1)} %solved_ref.2, bf16[2,1024,512]{2,1,0:T(8,128)(2,1)} %factor_ref.3), custom_call_target="tpu_custom_call" | custom-call | tf_op jit(solution)/shard_map/pallas_call | solution.py:270
  13.1 2.2 %collective-permute-done.2.refs_4_.refs_15_.refs_6_.refs_8_ = bf16[2,128,256]{2,1,0:T(8,128)(2,1)S(1)} collective-permute-done((bf16[2,128,256]{2,1,0:T(8,128)(2,1)}, bf16[2,128,256]{2,1,0:T(8,128)(2,1)S(1)}, u32[]{:S(2)}, u32[]{:S(2)}) %collective-permute-start.2) | collective-permute-done | bytes 131104 | tf_op jit(solution)/shard_map/ppermute | solution.py:248
  15.3 3.4 %all-to-all-start = ((bf16[32,16,256]{2,1,0:T(8,128)(2,1)}), bf16[32,16,256]{2,1,0:T(8,128)(2,1)S(1)}, u32[]{:S(2)}, u32[]{:S(2)}) async-start(bf16[32,16,256]{2,1,0:T(8,128)(2,1)} %bitcast.10), calls=%async_computation | async-start | bytes 524288 | tf_op jit(solution)/shard_map/all_to_all | solution.py:31
  18.7 0.3 collective-permute-start.4
  19.0 0.3 collective-permute-start.7
  19.3 0.3 collective-permute-start.6
  19.6 0.3 collective-permute-start.5
  19.8 2.7 %collective-permute-start.15 = (bf16[3,128,256]{2,1,0:T(8,128)(2,1)S(1)}, bf16[3,128,256]{2,1,0:T(8,128)(2,1)S(1)}, u32[]{:S(2)}, u32[]{:S(2)}) collective-permute-start(bf16[3,128,256]{2,1,0:T(8,128)(2,1)S(1)} %shard_map.71.refs_3_.refs_10_), channel_id=1, source_target_pairs={{0,24},{4,28},{8,16},{12,20},{16,8},{20,12},{24,0},{28,4},{1,25},{... | collective-permute-start | bytes 589832 | tf_op jit(solution)/shard_map/ppermute | solution.py:248
  22.6 0.6 collective-permute-start.13
  23.1 0.3 collective-permute-start.11
  23.4 5.7 %all-to-all-done.panel_ref = bf16[32,16,256]{2,1,0:T(8,128)(2,1)S(1)} async-done(((bf16[32,16,256]{2,1,0:T(8,128)(2,1)}), bf16[32,16,256]{2,1,0:T(8,128)(2,1)S(1)}, u32[]{:S(2)}, u32[]{:S(2)}) %all-to-all-start) | async-done | bytes 262176 | tf_op jit(solution)/shard_map/all_to_all | solution.py:31
  29.1 0.2 shard_map.70
  29.3 0.6 %collective-permute-start.8 = (bf16[16,640]{1,0:T(8,128)(2,1)S(1)}, bf16[16,640]{1,0:T(8,128)(2,1)S(1)}, u32[]{:S(2)}, u32[]{:S(2)}) collective-permute-start(bf16[16,640]{1,0:T(8,128)(2,1)S(1)} %shard_map.70), channel_id=1, source_target_pairs={{0,2},{1,3},{2,0},{3,1},{4,6},{5,7},{6,4},{7,5},{8,10},{9,11},{10,... | collective-permute-start | bytes 61448 | tf_op jit(solution)/shard_map/ppermute | solution.py:251
  30.0 4.1 %collective-permute-done.8 = bf16[16,640]{1,0:T(8,128)(2,1)S(1)} collective-permute-done((bf16[16,640]{1,0:T(8,128)(2,1)S(1)}, bf16[16,640]{1,0:T(8,128)(2,1)S(1)}, u32[]{:S(2)}, u32[]{:S(2)}) %collective-permute-start.8) | collective-permute-done | bytes 20512 | tf_op jit(solution)/shard_map/ppermute | solution.py:251
  34.1 1.0 %collective-permute-start.9 = (bf16[16,512]{1,0:T(8,128)(2,1)S(1)}, bf16[16,512]{1,0:T(8,128)(2,1)S(1)}, u32[]{:S(2)}, u32[]{:S(2)}) collective-permute-start(bf16[16,512]{1,0:T(8,128)(2,1)S(1)} %add_convert_fusion.refs_0_), channel_id=1, source_target_pairs={{0,1},{1,0},{2,3},{3,2},{4,5},{5,4},{6,7},{7,6},{8,9},{9,8},{10,11... | collective-permute-start | bytes 49160 | tf_op jit(solution)/shard_map/ppermute | solution.py:251
  35.1 0.5 collective-permute-start.12
  35.7 0.4 collective-permute-start.16
  36.2 1.7 %collective-permute-done.9.refs_1_ = bf16[16,512]{1,0:T(8,128)(2,1)S(1)} collective-permute-done((bf16[16,512]{1,0:T(8,128)(2,1)S(1)}, bf16[16,512]{1,0:T(8,128)(2,1)S(1)}, u32[]{:S(2)}, u32[]{:S(2)}) %collective-permute-start.9) | collective-permute-done | bytes 16416 | tf_op jit(solution)/shard_map/ppermute | solution.py:251
  37.9 0.6 shard_map.72
  38.5 0.9 %collective-permute-start.17 = (bf16[16,512]{1,0:T(8,128)(2,1)S(1)}, bf16[16,512]{1,0:T(8,128)(2,1)S(1)}, u32[]{:S(2)}, u32[]{:S(2)}) collective-permute-start(bf16[16,512]{1,0:T(8,128)(2,1)S(1)} %get-tuple-element.21.refs_0_), channel_id=1, source_target_pairs={{0,1},{1,0},{2,3},{3,2},{4,5},{5,4},{6,7},{7,6},{8,9},{9,8},{10,11... | collective-permute-start | bytes 49160 | tf_op jit(solution)/shard_map/ppermute | solution.py:251
  39.4 2.8 %collective-permute-done.17.refs_1_ = bf16[16,512]{1,0:T(8,128)(2,1)S(1)} collective-permute-done((bf16[16,512]{1,0:T(8,128)(2,1)S(1)}, bf16[16,512]{1,0:T(8,128)(2,1)S(1)}, u32[]{:S(2)}, u32[]{:S(2)}) %collective-permute-start.17) | collective-permute-done | bytes 16416 | tf_op jit(solution)/shard_map/ppermute | solution.py:251
  42.2 0.6 shard_map.73
  42.8 0.9 %collective-permute-start.18 = (bf16[16,512]{1,0:T(8,128)(2,1)S(1)}, bf16[16,512]{1,0:T(8,128)(2,1)S(1)}, u32[]{:S(2)}, u32[]{:S(2)}) collective-permute-start(bf16[16,512]{1,0:T(8,128)(2,1)S(1)} %get-tuple-element.23.refs_2_), channel_id=1, source_target_pairs={{0,1},{1,0},{2,3},{3,2},{4,5},{5,4},{6,7},{7,6},{8,9},{9,8},{10,11... | collective-permute-start | bytes 49160 | tf_op jit(solution)/shard_map/ppermute | solution.py:251
  43.7 2.8 %collective-permute-done.18.refs_3_ = bf16[16,512]{1,0:T(8,128)(2,1)S(1)} collective-permute-done((bf16[16,512]{1,0:T(8,128)(2,1)S(1)}, bf16[16,512]{1,0:T(8,128)(2,1)S(1)}, u32[]{:S(2)}, u32[]{:S(2)}) %collective-permute-start.18) | collective-permute-done | bytes 16416 | tf_op jit(solution)/shard_map/ppermute | solution.py:251
  46.7 11.3 %all_to_all.10.own_ref = bf16[16,16,256]{2,1,0:T(8,128)(2,1)S(1)} all-to-all(bf16[16,16,256]{2,1,0:T(8,128)(2,1)S(1)} %shard_map.74), channel_id=1, replica_groups=mesh['chip'=4,'core'=2,'col'=4] {'chip','col'}, dimensions={0} | all-to-all | bytes 262144 | tf_op jit(solution)/shard_map/all_to_all | solution.py:31
  58.0 1.3 %collective-permute-done.19.other_ref = bf16[16,16,256]{2,1,0:T(8,128)(2,1)S(1)} collective-permute-done((bf16[16,16,256]{2,1,0:T(8,128)(2,1)S(1)}, bf16[16,16,256]{2,1,0:T(8,128)(2,1)S(1)}, u32[]{:S(2)}, u32[]{:S(2)}) %collective-permute-start.19) | collective-permute-done | bytes 131104 | tf_op jit(solution)/shard_map/ppermute | solution.py:248
  59.3 1.1 %shard_map.75 = (f32[64,512]{1,0:T(8,128)}, f32[2,64,256]{2,1,0:T(8,128)}) custom-call(bf16[64,512]{1,0:T(8,128)(2,1)S(1)} %copy-done.4, bf16[2,1024,512]{2,1,0:T(8,128)(2,1)S(1)} %copy-done.1, bf16[16,16,256]{2,1,0:T(8,128)(2,1)S(1)} %all_to_all.10.own_ref, bf16[16,16,256]{2,1,0:T(8,128)(2,1)S(1)} %collective-permute-done.19.other_ref), custom_call_target="tpu_custom_call" | custom-call | tf_op jit(solution)/shard_map/pallas_call | solution.py:312
  (34 shorter events, 0.8 us)
Async XLA Ops:
  0.6 19.2 %copy-start = (f32[2,256,64]{1,2,0:T(8,128)S(1)}, f32[2,256,64]{1,2,0:T(8,128)}, u32[]{:S(2)}) copy-start(f32[2,256,64]{1,2,0:T(8,128)} %param.9) | copy-start | bytes 393220
  0.6 18.1 %copy-start.2 = (bf16[2,128,256]{2,1,0:T(8,128)(2,1)S(1)}, bf16[2,128,256]{2,1,0:T(8,128)(2,1)}, u32[]{:S(2)}) copy-start(bf16[2,128,256]{2,1,0:T(8,128)(2,1)} %refs_4_.1) | copy-start | bytes 393220
  2.4 17.5 %copy-start.3 = (bf16[2,128,256]{2,1,0:T(8,128)(2,1)S(1)}, bf16[2,128,256]{2,1,0:T(8,128)(2,1)}, u32[]{:S(2)}) copy-start(bf16[2,128,256]{2,1,0:T(8,128)(2,1)} %shard_map.68.own_ref) | copy-start | bytes 393220
  2.4 10.6 %collective-permute-start = (bf16[2,128,256]{2,1,0:T(8,128)(2,1)}, bf16[2,128,256]{2,1,0:T(8,128)(2,1)S(1)}, u32[]{:S(2)}, u32[]{:S(2)}) collective-permute-start(bf16[2,128,256]{2,1,0:T(8,128)(2,1)} %shard_map.68.own_ref), channel_id=1, source_target_pairs={{0,2},{1,3},{2,0},{3,1},{4,6},{5,7},{6,4},{7,5},{8,10},{9,11},{10,... | collective-permute-start | bytes 393224 | tf_op jit(solution)/shard_map/ppermute | solution.py:251
  6.4 6.7 %collective-permute-start.3 = (bf16[2,128,256]{2,1,0:T(8,128)(2,1)}, bf16[2,128,256]{2,1,0:T(8,128)(2,1)S(1)}, u32[]{:S(2)}, u32[]{:S(2)}) collective-permute-start(bf16[2,128,256]{2,1,0:T(8,128)(2,1)} %refs_4_.1), channel_id=1, source_target_pairs={{0,24},{4,28},{8,16},{12,20},{16,8},{20,12},{24,0},{28,4},{1,25},{... | collective-permute-start | bytes 393224 | tf_op jit(solution)/shard_map/ppermute | solution.py:248
  8.8 6.4 %collective-permute-start.2 = (bf16[2,128,256]{2,1,0:T(8,128)(2,1)}, bf16[2,128,256]{2,1,0:T(8,128)(2,1)S(1)}, u32[]{:S(2)}, u32[]{:S(2)}) collective-permute-start(bf16[2,128,256]{2,1,0:T(8,128)(2,1)} %refs_4_.1), channel_id=1, source_target_pairs={{0,16},{4,20},{8,24},{12,28},{16,0},{20,4},{24,8},{28,12},{1,17},{... | collective-permute-start | bytes 393224 | tf_op jit(solution)/shard_map/ppermute | solution.py:248
  9.3 6.0 %collective-permute-start.1 = (bf16[2,128,256]{2,1,0:T(8,128)(2,1)}, bf16[2,128,256]{2,1,0:T(8,128)(2,1)S(1)}, u32[]{:S(2)}, u32[]{:S(2)}) collective-permute-start(bf16[2,128,256]{2,1,0:T(8,128)(2,1)} %refs_4_.1), channel_id=1, source_target_pairs={{0,8},{4,12},{8,0},{12,4},{16,24},{20,28},{24,16},{28,20},{1,9},{5... | collective-permute-start | bytes 393224 | tf_op jit(solution)/shard_map/ppermute | solution.py:248
  15.3 13.8 %all-to-all-start = ((bf16[32,16,256]{2,1,0:T(8,128)(2,1)}), bf16[32,16,256]{2,1,0:T(8,128)(2,1)S(1)}, u32[]{:S(2)}, u32[]{:S(2)}) async-start(bf16[32,16,256]{2,1,0:T(8,128)(2,1)} %bitcast.10), calls=%async_computation | async-start | bytes 524288 | tf_op jit(solution)/shard_map/all_to_all | solution.py:31
  18.7 3.9 %collective-permute-start.4 = (bf16[2,128,256]{2,1,0:T(8,128)(2,1)S(1)}, bf16[2,128,256]{2,1,0:T(8,128)(2,1)S(1)}, u32[]{:S(2)}, u32[]{:S(2)}) collective-permute-start(bf16[2,128,256]{2,1,0:T(8,128)(2,1)S(1)} %copy-done.2), channel_id=1, source_target_pairs={{0,4},{4,0},{8,12},{12,8},{16,20},{20,16},{24,28},{28,24},{1,5},{5... | collective-permute-start | bytes 393224 | tf_op jit(solution)/shard_map/ppermute | solution.py:248
  19.0 4.1 %collective-permute-start.7 = (bf16[2,128,256]{2,1,0:T(8,128)(2,1)S(1)}, bf16[2,128,256]{2,1,0:T(8,128)(2,1)S(1)}, u32[]{:S(2)}, u32[]{:S(2)}) collective-permute-start(bf16[2,128,256]{2,1,0:T(8,128)(2,1)S(1)} %collective-permute-done.3.refs_6_.refs_17_.refs_8_.refs_10_), channel_id=1, source_target_pairs={{0,4},{4,0},{8,12},{12,8},{16,20},{20,16},{24,28},{28,24},{1,5},{5... | collective-permute-start | bytes 393224 | tf_op jit(solution)/shard_map/ppermute | solution.py:248
  19.3 4.1 %collective-permute-start.6 = (bf16[2,128,256]{2,1,0:T(8,128)(2,1)S(1)}, bf16[2,128,256]{2,1,0:T(8,128)(2,1)S(1)}, u32[]{:S(2)}, u32[]{:S(2)}) collective-permute-start(bf16[2,128,256]{2,1,0:T(8,128)(2,1)S(1)} %collective-permute-done.2.refs_4_.refs_15_.refs_6_.refs_8_), channel_id=1, source_target_pairs={{0,4},{4,0},{8,12},{12,8},{16,20},{20,16},{24,28},{28,24},{1,5},{5... | collective-permute-start | bytes 393224 | tf_op jit(solution)/shard_map/ppermute | solution.py:248
  19.6 3.9 %collective-permute-start.5 = (bf16[2,128,256]{2,1,0:T(8,128)(2,1)S(1)}, bf16[2,128,256]{2,1,0:T(8,128)(2,1)S(1)}, u32[]{:S(2)}, u32[]{:S(2)}) collective-permute-start(bf16[2,128,256]{2,1,0:T(8,128)(2,1)S(1)} %collective-permute-done.1.refs_2_.refs_13_.refs_4_.refs_6_), channel_id=1, source_target_pairs={{0,4},{4,0},{8,12},{12,8},{16,20},{20,16},{24,28},{28,24},{1,5},{5... | collective-permute-start | bytes 393224 | tf_op jit(solution)/shard_map/ppermute | solution.py:248
  19.8 15.2 %collective-permute-start.15 = (bf16[3,128,256]{2,1,0:T(8,128)(2,1)S(1)}, bf16[3,128,256]{2,1,0:T(8,128)(2,1)S(1)}, u32[]{:S(2)}, u32[]{:S(2)}) collective-permute-start(bf16[3,128,256]{2,1,0:T(8,128)(2,1)S(1)} %shard_map.71.refs_3_.refs_10_), channel_id=1, source_target_pairs={{0,24},{4,28},{8,16},{12,20},{16,8},{20,12},{24,0},{28,4},{1,25},{... | collective-permute-start | bytes 589832 | tf_op jit(solution)/shard_map/ppermute | solution.py:248
  22.6 12.5 %collective-permute-start.13 = (bf16[3,128,256]{2,1,0:T(8,128)(2,1)S(1)}, bf16[3,128,256]{2,1,0:T(8,128)(2,1)S(1)}, u32[]{:S(2)}, u32[]{:S(2)}) collective-permute-start(bf16[3,128,256]{2,1,0:T(8,128)(2,1)S(1)} %shard_map.71.refs_3_.refs_10_), channel_id=1, source_target_pairs={{0,16},{4,20},{8,24},{12,28},{16,0},{20,4},{24,8},{28,12},{1,17},{... | collective-permute-start | bytes 589832 | tf_op jit(solution)/shard_map/ppermute | solution.py:248
  23.1 11.9 %collective-permute-start.11 = (bf16[3,128,256]{2,1,0:T(8,128)(2,1)S(1)}, bf16[3,128,256]{2,1,0:T(8,128)(2,1)S(1)}, u32[]{:S(2)}, u32[]{:S(2)}) collective-permute-start(bf16[3,128,256]{2,1,0:T(8,128)(2,1)S(1)} %shard_map.71.refs_3_.refs_10_), channel_id=1, source_target_pairs={{0,8},{4,12},{8,0},{12,4},{16,24},{20,28},{24,16},{28,20},{1,9},{5... | collective-permute-start | bytes 589832 | tf_op jit(solution)/shard_map/ppermute | solution.py:248
  29.3 4.7 %collective-permute-start.8 = (bf16[16,640]{1,0:T(8,128)(2,1)S(1)}, bf16[16,640]{1,0:T(8,128)(2,1)S(1)}, u32[]{:S(2)}, u32[]{:S(2)}) collective-permute-start(bf16[16,640]{1,0:T(8,128)(2,1)S(1)} %shard_map.70), channel_id=1, source_target_pairs={{0,2},{1,3},{2,0},{3,1},{4,6},{5,7},{6,4},{7,5},{8,10},{9,11},{10,... | collective-permute-start | bytes 61448 | tf_op jit(solution)/shard_map/ppermute | solution.py:251
  34.1 3.8 %collective-permute-start.9 = (bf16[16,512]{1,0:T(8,128)(2,1)S(1)}, bf16[16,512]{1,0:T(8,128)(2,1)S(1)}, u32[]{:S(2)}, u32[]{:S(2)}) collective-permute-start(bf16[16,512]{1,0:T(8,128)(2,1)S(1)} %add_convert_fusion.refs_0_), channel_id=1, source_target_pairs={{0,1},{1,0},{2,3},{3,2},{4,5},{5,4},{6,7},{7,6},{8,9},{9,8},{10,11... | collective-permute-start | bytes 49160 | tf_op jit(solution)/shard_map/ppermute | solution.py:251
  35.1 2.8 %collective-permute-start.10 = (bf16[3,128,256]{2,1,0:T(8,128)(2,1)S(1)}, bf16[3,128,256]{2,1,0:T(8,128)(2,1)S(1)}, u32[]{:S(2)}, u32[]{:S(2)}) collective-permute-start(bf16[3,128,256]{2,1,0:T(8,128)(2,1)S(1)} %shard_map.71.refs_3_.refs_10_), channel_id=1, source_target_pairs={{0,4},{4,0},{8,12},{12,8},{16,20},{20,16},{24,28},{28,24},{1,5},{5... | collective-permute-start | bytes 589832 | tf_op jit(solution)/shard_map/ppermute | solution.py:248
  35.1 2.7 %collective-permute-start.12 = (bf16[3,128,256]{2,1,0:T(8,128)(2,1)S(1)}, bf16[3,128,256]{2,1,0:T(8,128)(2,1)S(1)}, u32[]{:S(2)}, u32[]{:S(2)}) collective-permute-start(bf16[3,128,256]{2,1,0:T(8,128)(2,1)S(1)} %collective-permute-done.11.refs_5_.refs_12_), channel_id=1, source_target_pairs={{0,4},{4,0},{8,12},{12,8},{16,20},{20,16},{24,28},{28,24},{1,5},{5... | collective-permute-start | bytes 589832 | tf_op jit(solution)/shard_map/ppermute | solution.py:248
  35.6 2.2 %collective-permute-start.14 = (bf16[3,128,256]{2,1,0:T(8,128)(2,1)S(1)}, bf16[3,128,256]{2,1,0:T(8,128)(2,1)S(1)}, u32[]{:S(2)}, u32[]{:S(2)}) collective-permute-start(bf16[3,128,256]{2,1,0:T(8,128)(2,1)S(1)} %collective-permute-done.13.refs_7_.refs_14_), channel_id=1, source_target_pairs={{0,4},{4,0},{8,12},{12,8},{16,20},{20,16},{24,28},{28,24},{1,5},{5... | collective-permute-start | bytes 589832 | tf_op jit(solution)/shard_map/ppermute | solution.py:248
  35.7 2.2 %collective-permute-start.16 = (bf16[3,128,256]{2,1,0:T(8,128)(2,1)S(1)}, bf16[3,128,256]{2,1,0:T(8,128)(2,1)S(1)}, u32[]{:S(2)}, u32[]{:S(2)}) collective-permute-start(bf16[3,128,256]{2,1,0:T(8,128)(2,1)S(1)} %collective-permute-done.15.refs_9_.refs_16_), channel_id=1, source_target_pairs={{0,4},{4,0},{8,12},{12,8},{16,20},{20,16},{24,28},{28,24},{1,5},{5... | collective-permute-start | bytes 589832 | tf_op jit(solution)/shard_map/ppermute | solution.py:248
  38.5 20.9 %copy-start.1 = (bf16[2,1024,512]{2,1,0:T(8,128)(2,1)S(1)}, bf16[2,1024,512]{2,1,0:T(8,128)(2,1)}, u32[]{:S(2)}) copy-start(bf16[2,1024,512]{2,1,0:T(8,128)(2,1)} %factor_ref.3) | copy-start | bytes 6291460
  38.5 20.9 %copy-start.4 = (bf16[64,512]{1,0:T(8,128)(2,1)S(1)}, bf16[64,512]{1,0:T(8,128)(2,1)}, u32[]{:S(2)}) copy-start(bf16[64,512]{1,0:T(8,128)(2,1)} %solved_ref.2) | copy-start | bytes 196612
  38.5 3.8 %collective-permute-start.17 = (bf16[16,512]{1,0:T(8,128)(2,1)S(1)}, bf16[16,512]{1,0:T(8,128)(2,1)S(1)}, u32[]{:S(2)}, u32[]{:S(2)}) collective-permute-start(bf16[16,512]{1,0:T(8,128)(2,1)S(1)} %get-tuple-element.21.refs_0_), channel_id=1, source_target_pairs={{0,1},{1,0},{2,3},{3,2},{4,5},{5,4},{6,7},{7,6},{8,9},{9,8},{10,11... | collective-permute-start | bytes 49160 | tf_op jit(solution)/shard_map/ppermute | solution.py:251
  42.8 3.8 %collective-permute-start.18 = (bf16[16,512]{1,0:T(8,128)(2,1)S(1)}, bf16[16,512]{1,0:T(8,128)(2,1)S(1)}, u32[]{:S(2)}, u32[]{:S(2)}) collective-permute-start(bf16[16,512]{1,0:T(8,128)(2,1)S(1)} %get-tuple-element.23.refs_2_), channel_id=1, source_target_pairs={{0,1},{1,0},{2,3},{3,2},{4,5},{5,4},{6,7},{7,6},{8,9},{9,8},{10,11... | collective-permute-start | bytes 49160 | tf_op jit(solution)/shard_map/ppermute | solution.py:251
  58.0 1.3 %collective-permute-start.19 = (bf16[16,16,256]{2,1,0:T(8,128)(2,1)S(1)}, bf16[16,16,256]{2,1,0:T(8,128)(2,1)S(1)}, u32[]{:S(2)}, u32[]{:S(2)}) collective-permute-start(bf16[16,16,256]{2,1,0:T(8,128)(2,1)S(1)} %all_to_all.10.own_ref), channel_id=1, source_target_pairs={{0,4},{4,0},{8,12},{12,8},{16,20},{20,16},{24,28},{28,24},{1,5},{5... | collective-permute-start | bytes 393224 | tf_op jit(solution)/shard_map/ppermute | solution.py:248

commit v10 on v9

--- a/solution.py
+++ b/solution.py
@@ -137,9 +137,9 @@
     update = None
     for k in range(2):
         back_ref[k] = columns(k, here)
-        for c in range(C):
-            term = plain(columns(k, c).astype(BF), factor_ref[k, c * rows : (c + 1) * rows])
-            update = term if update is None else update + term
+        whole = jnp.concatenate([columns(k, c).astype(BF) for c in range(C)], axis=1)
+        term = plain(whole, factor_ref[k])
+        update = term if update is None else update + term
     remaining_ref[...] = solved_ref[...].astype(F32) - update
 
 

time: 60.7 us -> 60.7 us (level)
  no operation moved by 1% of the time
where the time goes in v10:
time: 60.7 us; the launch traced here: 60.5 us
  waiting for transfers between devices  21.1 us (35%)
  starting transfers between devices  20.1 us (33%)
  blocking collectives  11.3 us (19%)
  Pallas kernels  7.23 us (12%)
  between operations  0.73 us (1%)
    ppermute x5, waiting for transfers between devices, xor_col(): return lax.ppermute(value, 'col', [(i, i ^ step) for i in range(C)])  11.7 us
    all_to_all x1, blocking collectives, exchange(): return lax.all_to_all(value, axes, 0, 0, tiled=False)  11.3 us
    ppermute x15, starting transfers between devices, xor_row(): return lax.ppermute(value, ROW, [(i, i ^ step) for i in range(R)])  9.21 us
    ppermute x5, starting transfers between devices, xor_col(): return lax.ppermute(value, 'col', [(i, i ^ step) for i in range(C)])  7.54 us
    all_to_all x1, waiting for transfers between devices, exchange(): return lax.all_to_all(value, axes, 0, 0, tiled=False)  5.7 us
    ppermute x15, waiting for transfers between devices, xor_row(): return lax.ppermute(value, ROW, [(i, i ^ step) for i in range(R)])  3.73 us
    all_to_all x1, starting transfers between devices, exchange(): return lax.all_to_all(value, axes, 0, 0, tiled=False)  3.38 us
    pallas_call x1, Pallas kernels, shards(): pl.pallas_call(panel_kernel, in_specs=[pl.BlockSpec(memory_space=pl.ANY)]...  2.87 us
  transfers between devices with their start and end apart: 21, of which 10 were waited for; matrix products, arithmetic and copies ran while one was open for 0% of the time, Pallas kernels for 5%

profile of v10, /device:TPU:0, one launch (start us, length us, event | category | flops | bytes accessed | tf_op | source)
XLA Modules:
  0.0 60.5 jit_solution(3155791332436025063)
XLA Ops:
  0.7 1.7 %shard_map.68.own_ref = bf16[2,128,256]{2,1,0:T(8,128)(2,1)} custom-call(bf16[2,128,256]{2,1,0:T(8,128)(2,1)} %refs_4_.1, bf16[256,128]{1,0:T(8,128)(2,1)} %link_ref.1), custom_call_target="tpu_custom_call" | custom-call | tf_op jit(solution)/shard_map/pallas_call | solution.py:216
  2.4 4.0 %collective-permute-start = (bf16[2,128,256]{2,1,0:T(8,128)(2,1)}, bf16[2,128,256]{2,1,0:T(8,128)(2,1)S(1)}, u32[]{:S(2)}, u32[]{:S(2)}) collective-permute-start(bf16[2,128,256]{2,1,0:T(8,128)(2,1)} %shard_map.68.own_ref), channel_id=1, source_target_pairs={{0,2},{1,3},{2,0},{3,1},{4,6},{5,7},{6,4},{7,5},{8,10},{9,11},{10,... | collective-permute-start | bytes 393224 | tf_op jit(solution)/shard_map/ppermute | solution.py:251
  6.4 2.4 %collective-permute-start.3 = (bf16[2,128,256]{2,1,0:T(8,128)(2,1)}, bf16[2,128,256]{2,1,0:T(8,128)(2,1)S(1)}, u32[]{:S(2)}, u32[]{:S(2)}) collective-permute-start(bf16[2,128,256]{2,1,0:T(8,128)(2,1)} %refs_4_.1), channel_id=1, source_target_pairs={{0,24},{4,28},{8,16},{12,20},{16,8},{20,12},{24,0},{28,4},{1,25},{... | collective-permute-start | bytes 393224 | tf_op jit(solution)/shard_map/ppermute | solution.py:248
  8.8 0.5 collective-permute-start.2
  9.3 0.5 collective-permute-start.1
  9.9 2.9 %shard_map.69 = bf16[8,4,16,256]{3,2,1,0:T(8,128)(2,1)} custom-call(bf16[64,512]{1,0:T(8,128)(2,1)} %solved_ref.2, bf16[2,1024,512]{2,1,0:T(8,128)(2,1)} %factor_ref.3), custom_call_target="tpu_custom_call" | custom-call | tf_op jit(solution)/shard_map/pallas_call | solution.py:270
  13.1 2.2 %collective-permute-done.2.refs_4_.refs_15_.refs_6_.refs_8_ = bf16[2,128,256]{2,1,0:T(8,128)(2,1)S(1)} collective-permute-done((bf16[2,128,256]{2,1,0:T(8,128)(2,1)}, bf16[2,128,256]{2,1,0:T(8,128)(2,1)S(1)}, u32[]{:S(2)}, u32[]{:S(2)}) %collective-permute-start.2) | collective-permute-done | bytes 131104 | tf_op jit(solution)/shard_map/ppermute | solution.py:248
  15.3 3.4 %all-to-all-start = ((bf16[32,16,256]{2,1,0:T(8,128)(2,1)}), bf16[32,16,256]{2,1,0:T(8,128)(2,1)S(1)}, u32[]{:S(2)}, u32[]{:S(2)}) async-start(bf16[32,16,256]{2,1,0:T(8,128)(2,1)} %bitcast.10), calls=%async_computation | async-start | bytes 524288 | tf_op jit(solution)/shard_map/all_to_all | solution.py:31
  18.7 0.3 collective-permute-start.4
  19.0 0.3 collective-permute-start.7
  19.3 0.3 collective-permute-start.6
  19.6 0.3 collective-permute-start.5
  19.8 2.7 %collective-permute-start.15 = (bf16[3,128,256]{2,1,0:T(8,128)(2,1)S(1)}, bf16[3,128,256]{2,1,0:T(8,128)(2,1)S(1)}, u32[]{:S(2)}, u32[]{:S(2)}) collective-permute-start(bf16[3,128,256]{2,1,0:T(8,128)(2,1)S(1)} %shard_map.71.refs_3_.refs_10_), channel_id=1, source_target_pairs={{0,24},{4,28},{8,16},{12,20},{16,8},{20,12},{24,0},{28,4},{1,25},{... | collective-permute-start | bytes 589832 | tf_op jit(solution)/shard_map/ppermute | solution.py:248
  22.6 0.6 collective-permute-start.13
  23.1 0.3 collective-permute-start.11
  23.4 5.7 %all-to-all-done.panel_ref = bf16[32,16,256]{2,1,0:T(8,128)(2,1)S(1)} async-done(((bf16[32,16,256]{2,1,0:T(8,128)(2,1)}), bf16[32,16,256]{2,1,0:T(8,128)(2,1)S(1)}, u32[]{:S(2)}, u32[]{:S(2)}) %all-to-all-start) | async-done | bytes 262176 | tf_op jit(solution)/shard_map/all_to_all | solution.py:31
  29.1 0.2 shard_map.70
  29.3 0.6 %collective-permute-start.8 = (bf16[16,640]{1,0:T(8,128)(2,1)S(1)}, bf16[16,640]{1,0:T(8,128)(2,1)S(1)}, u32[]{:S(2)}, u32[]{:S(2)}) collective-permute-start(bf16[16,640]{1,0:T(8,128)(2,1)S(1)} %shard_map.70), channel_id=1, source_target_pairs={{0,2},{1,3},{2,0},{3,1},{4,6},{5,7},{6,4},{7,5},{8,10},{9,11},{10,... | collective-permute-start | bytes 61448 | tf_op jit(solution)/shard_map/ppermute | solution.py:251
  30.0 4.1 %collective-permute-done.8 = bf16[16,640]{1,0:T(8,128)(2,1)S(1)} collective-permute-done((bf16[16,640]{1,0:T(8,128)(2,1)S(1)}, bf16[16,640]{1,0:T(8,128)(2,1)S(1)}, u32[]{:S(2)}, u32[]{:S(2)}) %collective-permute-start.8) | collective-permute-done | bytes 20512 | tf_op jit(solution)/shard_map/ppermute | solution.py:251
  34.1 1.0 %collective-permute-start.9 = (bf16[16,512]{1,0:T(8,128)(2,1)S(1)}, bf16[16,512]{1,0:T(8,128)(2,1)S(1)}, u32[]{:S(2)}, u32[]{:S(2)}) collective-permute-start(bf16[16,512]{1,0:T(8,128)(2,1)S(1)} %add_convert_fusion.refs_0_), channel_id=1, source_target_pairs={{0,1},{1,0},{2,3},{3,2},{4,5},{5,4},{6,7},{7,6},{8,9},{9,8},{10,11... | collective-permute-start | bytes 49160 | tf_op jit(solution)/shard_map/ppermute | solution.py:251
  35.1 0.5 collective-permute-start.12
  35.7 0.4 collective-permute-start.16
  36.2 1.7 %collective-permute-done.9.refs_1_ = bf16[16,512]{1,0:T(8,128)(2,1)S(1)} collective-permute-done((bf16[16,512]{1,0:T(8,128)(2,1)S(1)}, bf16[16,512]{1,0:T(8,128)(2,1)S(1)}, u32[]{:S(2)}, u32[]{:S(2)}) %collective-permute-start.9) | collective-permute-done | bytes 16416 | tf_op jit(solution)/shard_map/ppermute | solution.py:251
  37.9 0.6 shard_map.72
  38.5 0.9 %collective-permute-start.17 = (bf16[16,512]{1,0:T(8,128)(2,1)S(1)}, bf16[16,512]{1,0:T(8,128)(2,1)S(1)}, u32[]{:S(2)}, u32[]{:S(2)}) collective-permute-start(bf16[16,512]{1,0:T(8,128)(2,1)S(1)} %get-tuple-element.21.refs_0_), channel_id=1, source_target_pairs={{0,1},{1,0},{2,3},{3,2},{4,5},{5,4},{6,7},{7,6},{8,9},{9,8},{10,11... | collective-permute-start | bytes 49160 | tf_op jit(solution)/shard_map/ppermute | solution.py:251
  39.4 2.8 %collective-permute-done.17.refs_1_ = bf16[16,512]{1,0:T(8,128)(2,1)S(1)} collective-permute-done((bf16[16,512]{1,0:T(8,128)(2,1)S(1)}, bf16[16,512]{1,0:T(8,128)(2,1)S(1)}, u32[]{:S(2)}, u32[]{:S(2)}) %collective-permute-start.17) | collective-permute-done | bytes 16416 | tf_op jit(solution)/shard_map/ppermute | solution.py:251
  42.2 0.6 shard_map.73
  42.8 0.9 %collective-permute-start.18 = (bf16[16,512]{1,0:T(8,128)(2,1)S(1)}, bf16[16,512]{1,0:T(8,128)(2,1)S(1)}, u32[]{:S(2)}, u32[]{:S(2)}) collective-permute-start(bf16[16,512]{1,0:T(8,128)(2,1)S(1)} %get-tuple-element.23.refs_2_), channel_id=1, source_target_pairs={{0,1},{1,0},{2,3},{3,2},{4,5},{5,4},{6,7},{7,6},{8,9},{9,8},{10,11... | collective-permute-start | bytes 49160 | tf_op jit(solution)/shard_map/ppermute | solution.py:251
  43.7 2.8 %collective-permute-done.18.refs_3_ = bf16[16,512]{1,0:T(8,128)(2,1)S(1)} collective-permute-done((bf16[16,512]{1,0:T(8,128)(2,1)S(1)}, bf16[16,512]{1,0:T(8,128)(2,1)S(1)}, u32[]{:S(2)}, u32[]{:S(2)}) %collective-permute-start.18) | collective-permute-done | bytes 16416 | tf_op jit(solution)/shard_map/ppermute | solution.py:251
  46.7 11.3 %all_to_all.10.own_ref = bf16[16,16,256]{2,1,0:T(8,128)(2,1)S(1)} all-to-all(bf16[16,16,256]{2,1,0:T(8,128)(2,1)S(1)} %shard_map.74), channel_id=1, replica_groups=mesh['chip'=4,'core'=2,'col'=4] {'chip','col'}, dimensions={0} | all-to-all | bytes 262144 | tf_op jit(solution)/shard_map/all_to_all | solution.py:31
  58.0 1.3 %collective-permute-done.19.other_ref = bf16[16,16,256]{2,1,0:T(8,128)(2,1)S(1)} collective-permute-done((bf16[16,16,256]{2,1,0:T(8,128)(2,1)S(1)}, bf16[16,16,256]{2,1,0:T(8,128)(2,1)S(1)}, u32[]{:S(2)}, u32[]{:S(2)}) %collective-permute-start.19) | collective-permute-done | bytes 131104 | tf_op jit(solution)/shard_map/ppermute | solution.py:248
  59.3 1.1 %shard_map.75 = (f32[64,512]{1,0:T(8,128)}, f32[2,64,256]{2,1,0:T(8,128)}) custom-call(bf16[64,512]{1,0:T(8,128)(2,1)S(1)} %copy-done.4, bf16[2,1024,512]{2,1,0:T(8,128)(2,1)S(1)} %copy-done.1, bf16[16,16,256]{2,1,0:T(8,128)(2,1)S(1)} %all_to_all.10.own_ref, bf16[16,16,256]{2,1,0:T(8,128)(2,1)S(1)} %collective-permute-done.19.other_ref), custom_call_target="tpu_custom_call" | custom-call | tf_op jit(solution)/shard_map/pallas_call | solution.py:312
  (34 shorter events, 0.8 us)
Async XLA Ops:
  0.6 19.2 %copy-start = (f32[2,256,64]{1,2,0:T(8,128)S(1)}, f32[2,256,64]{1,2,0:T(8,128)}, u32[]{:S(2)}) copy-start(f32[2,256,64]{1,2,0:T(8,128)} %param.9) | copy-start | bytes 393220
  0.6 18.1 %copy-start.2 = (bf16[2,128,256]{2,1,0:T(8,128)(2,1)S(1)}, bf16[2,128,256]{2,1,0:T(8,128)(2,1)}, u32[]{:S(2)}) copy-start(bf16[2,128,256]{2,1,0:T(8,128)(2,1)} %refs_4_.1) | copy-start | bytes 393220
  2.4 17.5 %copy-start.3 = (bf16[2,128,256]{2,1,0:T(8,128)(2,1)S(1)}, bf16[2,128,256]{2,1,0:T(8,128)(2,1)}, u32[]{:S(2)}) copy-start(bf16[2,128,256]{2,1,0:T(8,128)(2,1)} %shard_map.68.own_ref) | copy-start | bytes 393220
  2.4 10.6 %collective-permute-start = (bf16[2,128,256]{2,1,0:T(8,128)(2,1)}, bf16[2,128,256]{2,1,0:T(8,128)(2,1)S(1)}, u32[]{:S(2)}, u32[]{:S(2)}) collective-permute-start(bf16[2,128,256]{2,1,0:T(8,128)(2,1)} %shard_map.68.own_ref), channel_id=1, source_target_pairs={{0,2},{1,3},{2,0},{3,1},{4,6},{5,7},{6,4},{7,5},{8,10},{9,11},{10,... | collective-permute-start | bytes 393224 | tf_op jit(solution)/shard_map/ppermute | solution.py:251
  6.4 6.7 %collective-permute-start.3 = (bf16[2,128,256]{2,1,0:T(8,128)(2,1)}, bf16[2,128,256]{2,1,0:T(8,128)(2,1)S(1)}, u32[]{:S(2)}, u32[]{:S(2)}) collective-permute-start(bf16[2,128,256]{2,1,0:T(8,128)(2,1)} %refs_4_.1), channel_id=1, source_target_pairs={{0,24},{4,28},{8,16},{12,20},{16,8},{20,12},{24,0},{28,4},{1,25},{... | collective-permute-start | bytes 393224 | tf_op jit(solution)/shard_map/ppermute | solution.py:248
  8.8 6.4 %collective-permute-start.2 = (bf16[2,128,256]{2,1,0:T(8,128)(2,1)}, bf16[2,128,256]{2,1,0:T(8,128)(2,1)S(1)}, u32[]{:S(2)}, u32[]{:S(2)}) collective-permute-start(bf16[2,128,256]{2,1,0:T(8,128)(2,1)} %refs_4_.1), channel_id=1, source_target_pairs={{0,16},{4,20},{8,24},{12,28},{16,0},{20,4},{24,8},{28,12},{1,17},{... | collective-permute-start | bytes 393224 | tf_op jit(solution)/shard_map/ppermute | solution.py:248
  9.3 6.0 %collective-permute-start.1 = (bf16[2,128,256]{2,1,0:T(8,128)(2,1)}, bf16[2,128,256]{2,1,0:T(8,128)(2,1)S(1)}, u32[]{:S(2)}, u32[]{:S(2)}) collective-permute-start(bf16[2,128,256]{2,1,0:T(8,128)(2,1)} %refs_4_.1), channel_id=1, source_target_pairs={{0,8},{4,12},{8,0},{12,4},{16,24},{20,28},{24,16},{28,20},{1,9},{5... | collective-permute-start | bytes 393224 | tf_op jit(solution)/shard_map/ppermute | solution.py:248
  15.3 13.8 %all-to-all-start = ((bf16[32,16,256]{2,1,0:T(8,128)(2,1)}), bf16[32,16,256]{2,1,0:T(8,128)(2,1)S(1)}, u32[]{:S(2)}, u32[]{:S(2)}) async-start(bf16[32,16,256]{2,1,0:T(8,128)(2,1)} %bitcast.10), calls=%async_computation | async-start | bytes 524288 | tf_op jit(solution)/shard_map/all_to_all | solution.py:31
  18.7 3.9 %collective-permute-start.4 = (bf16[2,128,256]{2,1,0:T(8,128)(2,1)S(1)}, bf16[2,128,256]{2,1,0:T(8,128)(2,1)S(1)}, u32[]{:S(2)}, u32[]{:S(2)}) collective-permute-start(bf16[2,128,256]{2,1,0:T(8,128)(2,1)S(1)} %copy-done.2), channel_id=1, source_target_pairs={{0,4},{4,0},{8,12},{12,8},{16,20},{20,16},{24,28},{28,24},{1,5},{5... | collective-permute-start | bytes 393224 | tf_op jit(solution)/shard_map/ppermute | solution.py:248
  19.0 4.1 %collective-permute-start.7 = (bf16[2,128,256]{2,1,0:T(8,128)(2,1)S(1)}, bf16[2,128,256]{2,1,0:T(8,128)(2,1)S(1)}, u32[]{:S(2)}, u32[]{:S(2)}) collective-permute-start(bf16[2,128,256]{2,1,0:T(8,128)(2,1)S(1)} %collective-permute-done.3.refs_6_.refs_17_.refs_8_.refs_10_), channel_id=1, source_target_pairs={{0,4},{4,0},{8,12},{12,8},{16,20},{20,16},{24,28},{28,24},{1,5},{5... | collective-permute-start | bytes 393224 | tf_op jit(solution)/shard_map/ppermute | solution.py:248
  19.3 4.1 %collective-permute-start.6 = (bf16[2,128,256]{2,1,0:T(8,128)(2,1)S(1)}, bf16[2,128,256]{2,1,0:T(8,128)(2,1)S(1)}, u32[]{:S(2)}, u32[]{:S(2)}) collective-permute-start(bf16[2,128,256]{2,1,0:T(8,128)(2,1)S(1)} %collective-permute-done.2.refs_4_.refs_15_.refs_6_.refs_8_), channel_id=1, source_target_pairs={{0,4},{4,0},{8,12},{12,8},{16,20},{20,16},{24,28},{28,24},{1,5},{5... | collective-permute-start | bytes 393224 | tf_op jit(solution)/shard_map/ppermute | solution.py:248
  19.6 3.9 %collective-permute-start.5 = (bf16[2,128,256]{2,1,0:T(8,128)(2,1)S(1)}, bf16[2,128,256]{2,1,0:T(8,128)(2,1)S(1)}, u32[]{:S(2)}, u32[]{:S(2)}) collective-permute-start(bf16[2,128,256]{2,1,0:T(8,128)(2,1)S(1)} %collective-permute-done.1.refs_2_.refs_13_.refs_4_.refs_6_), channel_id=1, source_target_pairs={{0,4},{4,0},{8,12},{12,8},{16,20},{20,16},{24,28},{28,24},{1,5},{5... | collective-permute-start | bytes 393224 | tf_op jit(solution)/shard_map/ppermute | solution.py:248
  19.8 15.2 %collective-permute-start.15 = (bf16[3,128,256]{2,1,0:T(8,128)(2,1)S(1)}, bf16[3,128,256]{2,1,0:T(8,128)(2,1)S(1)}, u32[]{:S(2)}, u32[]{:S(2)}) collective-permute-start(bf16[3,128,256]{2,1,0:T(8,128)(2,1)S(1)} %shard_map.71.refs_3_.refs_10_), channel_id=1, source_target_pairs={{0,24},{4,28},{8,16},{12,20},{16,8},{20,12},{24,0},{28,4},{1,25},{... | collective-permute-start | bytes 589832 | tf_op jit(solution)/shard_map/ppermute | solution.py:248
  22.6 12.5 %collective-permute-start.13 = (bf16[3,128,256]{2,1,0:T(8,128)(2,1)S(1)}, bf16[3,128,256]{2,1,0:T(8,128)(2,1)S(1)}, u32[]{:S(2)}, u32[]{:S(2)}) collective-permute-start(bf16[3,128,256]{2,1,0:T(8,128)(2,1)S(1)} %shard_map.71.refs_3_.refs_10_), channel_id=1, source_target_pairs={{0,16},{4,20},{8,24},{12,28},{16,0},{20,4},{24,8},{28,12},{1,17},{... | collective-permute-start | bytes 589832 | tf_op jit(solution)/shard_map/ppermute | solution.py:248
  23.1 11.9 %collective-permute-start.11 = (bf16[3,128,256]{2,1,0:T(8,128)(2,1)S(1)}, bf16[3,128,256]{2,1,0:T(8,128)(2,1)S(1)}, u32[]{:S(2)}, u32[]{:S(2)}) collective-permute-start(bf16[3,128,256]{2,1,0:T(8,128)(2,1)S(1)} %shard_map.71.refs_3_.refs_10_), channel_id=1, source_target_pairs={{0,8},{4,12},{8,0},{12,4},{16,24},{20,28},{24,16},{28,20},{1,9},{5... | collective-permute-start | bytes 589832 | tf_op jit(solution)/shard_map/ppermute | solution.py:248
  29.3 4.7 %collective-permute-start.8 = (bf16[16,640]{1,0:T(8,128)(2,1)S(1)}, bf16[16,640]{1,0:T(8,128)(2,1)S(1)}, u32[]{:S(2)}, u32[]{:S(2)}) collective-permute-start(bf16[16,640]{1,0:T(8,128)(2,1)S(1)} %shard_map.70), channel_id=1, source_target_pairs={{0,2},{1,3},{2,0},{3,1},{4,6},{5,7},{6,4},{7,5},{8,10},{9,11},{10,... | collective-permute-start | bytes 61448 | tf_op jit(solution)/shard_map/ppermute | solution.py:251
  34.1 3.8 %collective-permute-start.9 = (bf16[16,512]{1,0:T(8,128)(2,1)S(1)}, bf16[16,512]{1,0:T(8,128)(2,1)S(1)}, u32[]{:S(2)}, u32[]{:S(2)}) collective-permute-start(bf16[16,512]{1,0:T(8,128)(2,1)S(1)} %add_convert_fusion.refs_0_), channel_id=1, source_target_pairs={{0,1},{1,0},{2,3},{3,2},{4,5},{5,4},{6,7},{7,6},{8,9},{9,8},{10,11... | collective-permute-start | bytes 49160 | tf_op jit(solution)/shard_map/ppermute | solution.py:251
  35.1 2.8 %collective-permute-start.10 = (bf16[3,128,256]{2,1,0:T(8,128)(2,1)S(1)}, bf16[3,128,256]{2,1,0:T(8,128)(2,1)S(1)}, u32[]{:S(2)}, u32[]{:S(2)}) collective-permute-start(bf16[3,128,256]{2,1,0:T(8,128)(2,1)S(1)} %shard_map.71.refs_3_.refs_10_), channel_id=1, source_target_pairs={{0,4},{4,0},{8,12},{12,8},{16,20},{20,16},{24,28},{28,24},{1,5},{5... | collective-permute-start | bytes 589832 | tf_op jit(solution)/shard_map/ppermute | solution.py:248
  35.1 2.7 %collective-permute-start.12 = (bf16[3,128,256]{2,1,0:T(8,128)(2,1)S(1)}, bf16[3,128,256]{2,1,0:T(8,128)(2,1)S(1)}, u32[]{:S(2)}, u32[]{:S(2)}) collective-permute-start(bf16[3,128,256]{2,1,0:T(8,128)(2,1)S(1)} %collective-permute-done.11.refs_5_.refs_12_), channel_id=1, source_target_pairs={{0,4},{4,0},{8,12},{12,8},{16,20},{20,16},{24,28},{28,24},{1,5},{5... | collective-permute-start | bytes 589832 | tf_op jit(solution)/shard_map/ppermute | solution.py:248
  35.6 2.2 %collective-permute-start.14 = (bf16[3,128,256]{2,1,0:T(8,128)(2,1)S(1)}, bf16[3,128,256]{2,1,0:T(8,128)(2,1)S(1)}, u32[]{:S(2)}, u32[]{:S(2)}) collective-permute-start(bf16[3,128,256]{2,1,0:T(8,128)(2,1)S(1)} %collective-permute-done.13.refs_7_.refs_14_), channel_id=1, source_target_pairs={{0,4},{4,0},{8,12},{12,8},{16,20},{20,16},{24,28},{28,24},{1,5},{5... | collective-permute-start | bytes 589832 | tf_op jit(solution)/shard_map/ppermute | solution.py:248
  35.7 2.2 %collective-permute-start.16 = (bf16[3,128,256]{2,1,0:T(8,128)(2,1)S(1)}, bf16[3,128,256]{2,1,0:T(8,128)(2,1)S(1)}, u32[]{:S(2)}, u32[]{:S(2)}) collective-permute-start(bf16[3,128,256]{2,1,0:T(8,128)(2,1)S(1)} %collective-permute-done.15.refs_9_.refs_16_), channel_id=1, source_target_pairs={{0,4},{4,0},{8,12},{12,8},{16,20},{20,16},{24,28},{28,24},{1,5},{5... | collective-permute-start | bytes 589832 | tf_op jit(solution)/shard_map/ppermute | solution.py:248
  38.5 20.9 %copy-start.1 = (bf16[2,1024,512]{2,1,0:T(8,128)(2,1)S(1)}, bf16[2,1024,512]{2,1,0:T(8,128)(2,1)}, u32[]{:S(2)}) copy-start(bf16[2,1024,512]{2,1,0:T(8,128)(2,1)} %factor_ref.3) | copy-start | bytes 6291460
  38.5 20.9 %copy-start.4 = (bf16[64,512]{1,0:T(8,128)(2,1)S(1)}, bf16[64,512]{1,0:T(8,128)(2,1)}, u32[]{:S(2)}) copy-start(bf16[64,512]{1,0:T(8,128)(2,1)} %solved_ref.2) | copy-start | bytes 196612
  38.5 3.8 %collective-permute-start.17 = (bf16[16,512]{1,0:T(8,128)(2,1)S(1)}, bf16[16,512]{1,0:T(8,128)(2,1)S(1)}, u32[]{:S(2)}, u32[]{:S(2)}) collective-permute-start(bf16[16,512]{1,0:T(8,128)(2,1)S(1)} %get-tuple-element.21.refs_0_), channel_id=1, source_target_pairs={{0,1},{1,0},{2,3},{3,2},{4,5},{5,4},{6,7},{7,6},{8,9},{9,8},{10,11... | collective-permute-start | bytes 49160 | tf_op jit(solution)/shard_map/ppermute | solution.py:251
  42.8 3.8 %collective-permute-start.18 = (bf16[16,512]{1,0:T(8,128)(2,1)S(1)}, bf16[16,512]{1,0:T(8,128)(2,1)S(1)}, u32[]{:S(2)}, u32[]{:S(2)}) collective-permute-start(bf16[16,512]{1,0:T(8,128)(2,1)S(1)} %get-tuple-element.23.refs_2_), channel_id=1, source_target_pairs={{0,1},{1,0},{2,3},{3,2},{4,5},{5,4},{6,7},{7,6},{8,9},{9,8},{10,11... | collective-permute-start | bytes 49160 | tf_op jit(solution)/shard_map/ppermute | solution.py:251
  58.0 1.3 %collective-permute-start.19 = (bf16[16,16,256]{2,1,0:T(8,128)(2,1)S(1)}, bf16[16,16,256]{2,1,0:T(8,128)(2,1)S(1)}, u32[]{:S(2)}, u32[]{:S(2)}) collective-permute-start(bf16[16,16,256]{2,1,0:T(8,128)(2,1)S(1)} %all_to_all.10.own_ref), channel_id=1, source_target_pairs={{0,4},{4,0},{8,12},{12,8},{16,20},{20,16},{24,28},{28,24},{1,5},{5... | collective-permute-start | bytes 393224 | tf_op jit(solution)/shard_map/ppermute | solution.py:248
